TPU v7x, 32 devices: a whole 2x2x4 slice. The times are simulated.
32 devices in a mesh: tensor: 4 (over z), context: 8 (over y, x, core).
Axes of the slice: x: 2, y: 2, z: 4, core: 2. Of those that a mesh axis runs over, the one named last changes fastest.
Arguments:
- query_in: bfloat16 [8192, 4096], P('context', 'tensor'), may hold values from -6 to 6
- key_in: bfloat16 [8192, 4096], P('context', 'tensor'), may hold values from -6 to 6
- value_in: bfloat16 [8192, 4096], P('context', 'tensor'), may hold values from -6 to 6
- filter_taps: bfloat16 [128, 4096], P(None, 'tensor'), may hold values from -0.5 to 0.5
- out_weight: bfloat16 [4096, 4096], P('tensor'), may hold values from -0.09375 to 0.09375
- out_grad: bfloat16 [8192, 4096], P('context', 'tensor'), may hold values from -6 to 6
Outputs:
- grad_query: float32 [8192, 4096], P('context', 'tensor')
- grad_key: float32 [8192, 4096], P('context', 'tensor')
- grad_value: float32 [8192, 4096], P('context', 'tensor')
- grad_filter: float32 [128, 4096], P(None, ('tensor', 'context'))
- grad_weight: float32 [4096, 4096], P('tensor', 'context')
All inputs are finite; a program needn't handle non-finite values.
Results may differ from a plain program's by a relative error of at most 0.0045.
Values may be sent and summed in bfloat16 or wider, within the bound.
No kernel may reach another device: no remote copies, remote signals or barrier semaphores. Data moves between devices by JAX's collectives and lax.ppermute only.
A program may use at most 256 MiB of HBM per device.

v0:
```python
import math

import jax
import jax.numpy as jnp
from jax import lax
from jax.sharding import PartitionSpec as P


def lag_table(taps, lag_of):
    span = taps.shape[0]
    row_idx = jnp.arange(span)[:, None]
    col_idx = jnp.arange(2 * span)[None, :]
    tap_lag = lag_of(row_idx, col_idx, span)
    onehot = (tap_lag[None, :, :] == jnp.arange(span)[:, None, None]).astype(jnp.bfloat16)
    table = jnp.einsum("jim,jc->imc", onehot, taps, preferred_element_type=jnp.float32)
    return table.astype(jnp.bfloat16)


def lag_before(row_idx, col_idx, span):
    return row_idx + span - col_idx


def lag_after(row_idx, col_idx, span):
    return col_idx - row_idx


def windows_of(signal, before):
    span = before.shape[0]
    count = signal.shape[0] // span
    chans = signal.shape[1]
    current = signal.reshape(count, span, chans)
    earlier = jnp.concatenate([before, signal[: signal.shape[0] - span]], axis=0).reshape(
        count, span, chans
    )
    return jnp.concatenate([earlier, current], axis=1)


def windows_after(signal, after):
    span = after.shape[0]
    count = signal.shape[0] // span
    chans = signal.shape[1]
    current = signal.reshape(count, span, chans)
    later = jnp.concatenate([signal[span:], after], axis=0).reshape(count, span, chans)
    return jnp.concatenate([current, later], axis=1)


def causal(signal, before, taps):
    window = windows_of(signal, before)
    result = jnp.einsum(
        "bmc,imc->bic", window, lag_table(taps, lag_before), preferred_element_type=jnp.float32
    )
    return result.reshape(signal.shape[0], signal.shape[1])


def reverse_causal(signal, after, taps):
    window = windows_after(signal, after)
    result = jnp.einsum(
        "bmc,imc->bic", window, lag_table(taps, lag_after), preferred_element_type=jnp.float32
    )
    return result.reshape(signal.shape[0], signal.shape[1])


def filter_corr(grad_sig, signal, before):
    span = before.shape[0]
    chans = signal.shape[1]
    group_width = min(chans, 128)
    window = windows_of(signal, before)
    grad_blocks = grad_sig.reshape(window.shape[0], span, chans)
    row_len = 2 * span

    def one_group(group):
        products = jnp.einsum(
            "bic,bmc->cim", grad_blocks, window, preferred_element_type=jnp.float32
        )
        flat = products.reshape(group_width, span * row_len)
        padded = jnp.concatenate([flat, jnp.zeros((group_width, span), jnp.float32)], axis=1)
        skewed = padded.reshape(group_width, span, row_len + 1)
        sums = jnp.sum(skewed[:, :, 1 : span + 1], axis=1)
        return sums[:, ::-1]

    groups = lax.map(one_group, jnp.arange(chans // group_width))
    return groups.reshape(chans, span).T


def body(query_in, key_in, value_in, filter_taps, out_weight, out_grad):
    tok_rows, chan_width = query_in.shape
    span = filter_taps.shape[0]
    ctx_size = lax.axis_size("context")
    loss_scale = 1.0 / math.sqrt(tok_rows * ctx_size)
    mixed_in = (key_in.astype(jnp.float32) * value_in.astype(jnp.float32)).astype(jnp.bfloat16)
    sub_width = chan_width // ctx_size
    own_taps = lax.dynamic_slice_in_dim(
        filter_taps, lax.axis_index("context") * sub_width, sub_width, 1
    )
    mixed_chan = lax.all_to_all(mixed_in, "context", split_axis=1, concat_axis=0, tiled=True)
    blank = jnp.zeros((span, sub_width), jnp.bfloat16)
    conv_chan = causal(mixed_chan, blank, own_taps)
    conv_out = lax.all_to_all(conv_chan, "context", split_axis=0, concat_axis=1, tiled=True)
    gated = (query_in.astype(jnp.float32) * conv_out).astype(jnp.bfloat16)
    segment = lax.all_gather(out_grad, "tensor", axis=1, tiled=True)
    grad_gated = lax.dot_general(
        segment, out_weight, (((1,), (1,)), ((), ())), preferred_element_type=jnp.float32
    )
    outer_block = lax.dot_general(
        gated, segment, (((0,), (0,)), ((), ())), preferred_element_type=jnp.float32
    )
    weight_part = outer_block
    grad_gated, weight_part = (grad_gated, weight_part)
    grad_query = grad_gated * conv_out
    grad_conv = (grad_gated * query_in.astype(jnp.float32)).astype(jnp.bfloat16)
    grad_chan = lax.all_to_all(grad_conv, "context", split_axis=1, concat_axis=0, tiled=True)
    mixed_grad_chan = reverse_causal(grad_chan, blank, own_taps)
    grad_filter = filter_corr(grad_chan, mixed_chan, blank) * loss_scale
    grad_mixed = lax.all_to_all(mixed_grad_chan, "context", split_axis=0, concat_axis=1, tiled=True)
    grad_weight = (
        lax.psum_scatter(weight_part, "context", scatter_dimension=1, tiled=True) * loss_scale
    )
    grad_key = grad_mixed * value_in.astype(jnp.float32)
    grad_value = grad_mixed * key_in.astype(jnp.float32)
    return (grad_query, grad_key, grad_value, grad_filter, grad_weight)


def solution(mesh):
    placed = (
        P("context", "tensor"),
        P("context", "tensor"),
        P("context", "tensor"),
        P(None, "tensor"),
        P("tensor", None),
        P("context", "tensor"),
    )
    return jax.shard_map(
        body,
        mesh=mesh,
        in_specs=placed,
        out_specs=(
            P("context", "tensor"),
            P("context", "tensor"),
            P("context", "tensor"),
            P(None, ("tensor", "context")),
            P("tensor", "context"),
        ),
        check_vma=False,
    )
```

profile of v0, /device:TPU:0, one launch (start us, length us, event | category | flops | bytes accessed | tf_op | source)
XLA Modules:
  0.0 357.9 jit_solution(10600739697720528662)
XLA Ops:
  7.2 0.0 copy-start
  7.2 0.0 all-gather.2.cloned.1.call-start
  7.2 0.7 all-gather.2.cloned.1.call-update
  7.9 3.2 fusion.6
  11.1 2.6 copy.40
  13.7 5.2 %all-to-all-start = ((bf16[1024,8,128]{0,2,1:T(8,128)(2,1)}), bf16[1024,8,128]{0,2,1:T(8,128)(2,1)S(1)}, u32[]{:S(2)}, u32[]{:S(2)}) async-start(bf16[1024,8,128]{0,2,1:T(8,128)(2,1)} %bitcast.50), calls=%async_computation | async-start | bytes 4194304 | tf_op jit(solution)/shard_map/all_to_all | solution.py:95
  18.8 0.1 iota_subtract_fusion.1
  18.9 0.0 copy-done
  18.9 8.5 %fusion.5 = bf16[128,256,128]{2,1,0:T(8,128)(2,1)} fusion(s32[128,256]{1,0:T(8,128)S(1)} %iota_subtract_fusion.1, bf16[128,1024]{1,0:T(8,128)(2,1)S(1)} %copy-done, s32[]{:T(128)S(6)} %select_n.3), kind=kOutput, calls=%fused_computation.8 | convolution fusion | flops 1082130432 | bytes 8552452 | tf_op jit(solution)/shard_map/jim,jc->imc/dot_general | solution.py:15
  27.5 12.8 %copy.44 = bf16[128,256,128]{1,0,2:T(8,128)(2,1)} copy(bf16[128,256,128]{2,1,0:T(8,128)(2,1)} %fusion.5) | data formatting | bytes 16777216 | tf_op jit(solution)/shard_map/convert_element_type | solution.py:16
  40.2 5.3 %all-to-all-done = bf16[1024,8,128]{0,2,1:T(8,128)(2,1)S(1)} async-done(((bf16[1024,8,128]{0,2,1:T(8,128)(2,1)}), bf16[1024,8,128]{0,2,1:T(8,128)(2,1)S(1)}, u32[]{:S(2)}, u32[]{:S(2)}) %all-to-all-start) | async-done | bytes 2097184 | tf_op jit(solution)/shard_map/all_to_all | solution.py:95
  45.5 2.5 copy.43
  48.0 4.2 %reshape.90 = bf16[64,128,128]{1,0,2:T(8,128)(2,1)} reshape(bf16[8,1024,128]{1,0,2:T(8,128)(2,1)} %copy.43) | data formatting | bytes 4194304 | tf_op jit(solution)/shard_map/reshape | solution.py:31
  52.1 2.4 copy.41
  54.5 1.7 slice.14
  56.2 0.0 copy-start.2
  56.2 1.5 concatenate.18
  57.7 4.1 %copy.56 = bf16[64,128,128]{1,0,2:T(8,128)(2,1)} copy(bf16[64,128,128]{2,1,0:T(8,128)(2,1)} %bitcast.52) | data formatting | bytes 4194304 | tf_op jit(solution)/shard_map/reshape | solution.py:32
  61.8 0.0 copy-done.2
  61.8 9.1 %fusion.15 = f32[64,128,128]{1,0,2:T(8,128)} fusion(bf16[128,256,128]{1,0,2:T(8,128)(2,1)} %copy.44, bf16[64,128,128]{1,0,2:T(8,128)(2,1)S(1)} %copy-done.2, bf16[64,128,128]{1,0,2:T(8,128)(2,1)} %copy.56), kind=kOutput, calls=%fused_computation.25 | convolution fusion | flops 545259520 | bytes 16777216 | tf_op jit(solution)/shard_map/bmc,imc->bic/dot_general | solution.py:49
  70.9 4.9 %all_to_all.60 = f32[8,1024,128]{1,0,2:T(8,128)} reshape(f32[64,128,128]{1,0,2:T(8,128)} %fusion.15) | data formatting | bytes 8388608 | tf_op jit(solution)/shard_map/all_to_all | solution.py:98
  75.8 6.7 %copy.45 = f32[8,1024,128]{1,2,0:T(8,128)} copy(f32[8,1024,128]{1,0,2:T(8,128)} %all_to_all.60) | data formatting | bytes 8388608 | tf_op jit(solution)/shard_map/all_to_all | solution.py:98
  82.5 4.6 %all-to-all-start.1 = ((f32[8,1024,128]{1,2,0:T(8,128)}), f32[8,1024,128]{1,2,0:T(8,128)}, u32[]{:S(2)}, u32[]{:S(2)}) async-start(f32[8,1024,128]{1,2,0:T(8,128)} %copy.45), calls=%async_computation.1 | async-start | bytes 8388608 | tf_op jit(solution)/shard_map/all_to_all | solution.py:98
  87.1 0.2 reduce-scatter.2.cloned.1.call-start
  87.3 4.0 %copy.46 = bf16[1024,1024]{0,1:T(8,128)(2,1)} copy(bf16[1024,1024]{1,0:T(8,128)(2,1)} %param.6) | data formatting | bytes 4194304 | tf_op args[0]
  91.3 44.9 %all-to-all-done.1 = f32[8,1024,128]{1,2,0:T(8,128)} async-done(((f32[8,1024,128]{1,2,0:T(8,128)}), f32[8,1024,128]{1,2,0:T(8,128)}, u32[]{:S(2)}, u32[]{:S(2)}) %all-to-all-start.1) | async-done | bytes 4194336 | tf_op jit(solution)/shard_map/all_to_all | solution.py:98
  136.2 25.8 %all-gather.2.cloned.1.call-done = bf16[1024,4096]{1,0:T(8,128)(2,1)} async-done(((bf16[1024,1024]{1,0:T(8,128)(2,1)}), bf16[1024,4096]{1,0:T(8,128)(2,1)}) %all-gather.2.cloned.1.call-update) | async-done | bytes 8388624 | tf_op jit(solution)/shard_map/all_gather | solution.py:100
  162.0 0.0 copy-start.4
  162.0 16.9 %fusion.8 = (bf16[1024,1024]{0,1:T(8,128)(2,1)S(1)}, f32[1024,1024]{0,1:T(8,128)}, bf16[1024,1024]{0,1:T(8,128)(2,1)}) fusion(bf16[1024,1024]{0,1:T(8,128)(2,1)} %copy.46, f32[8,1024,128]{1,2,0:T(8,128)} %all-to-all-done.1, bf16[1024,4096]{1,0:T(8,128)(2,1)} %all-gather.2.cloned.1.call-done, bf16[1024,4096]{1,0:T(8,128)(2,1)} %param.10), kind=kOutput, calls=%fused_computation.16 | convolution fusion | flops 8596226048 | bytes 31457280 | tf_op jit(solution)/shard_map/dot_general | solution.py:101
  178.9 0.0 copy-done.4
  178.9 12.0 %fusion.28 = f32[1024,4096]{1,0:T(8,128)} fusion(bf16[1024,1024]{0,1:T(8,128)(2,1)S(1)} %get-tuple-element.37, bf16[1024,4096]{1,0:T(8,128)(2,1)S(1)} %copy-done.4), kind=kOutput, calls=%fused_computation.41 | convolution fusion | flops 8589934592 | bytes 27262976 | tf_op jit(solution)/shard_map/dot_general | solution.py:104
  190.9 0.0 reduce-scatter.2.cloned.1.call-update
  190.9 3.9 %copy.47 = bf16[1024,8,128]{2,0,1:T(8,128)(2,1)} copy(bf16[1024,8,128]{0,2,1:T(8,128)(2,1)} %bitcast.54) | data formatting | bytes 4194304 | tf_op jit(solution)/shard_map/all_to_all | solution.py:111
  194.8 4.6 %all-to-all-start.2 = ((bf16[1024,8,128]{2,0,1:T(8,128)(2,1)}), bf16[1024,8,128]{2,0,1:T(8,128)(2,1)}, u32[]{:S(2)}, u32[]{:S(2)}) async-start(bf16[1024,8,128]{2,0,1:T(8,128)(2,1)} %copy.47), calls=%async_computation.2 | async-start | bytes 4194304 | tf_op jit(solution)/shard_map/all_to_all | solution.py:111
  199.5 8.5 %fusion.4 = bf16[128,256,128]{2,1,0:T(8,128)(2,1)} fusion(s32[128,256]{1,0:T(8,128)S(1)} %iota_subtract_fusion, bf16[128,1024]{1,0:T(8,128)(2,1)S(1)} %copy-done, s32[]{:T(128)S(6)} %select_n.3), kind=kOutput, calls=%fused_computation.7 | convolution fusion | flops 1082130432 | bytes 8552452 | tf_op jit(solution)/shard_map/jim,jc->imc/dot_general | solution.py:15
  208.0 13.4 %copy.50 = bf16[128,256,128]{1,0,2:T(8,128)(2,1)} copy(bf16[128,256,128]{2,1,0:T(8,128)(2,1)} %fusion.4) | data formatting | bytes 16777216 | tf_op jit(solution)/shard_map/convert_element_type | solution.py:16
  221.4 4.5 %all-to-all-done.2 = bf16[1024,8,128]{2,0,1:T(8,128)(2,1)} async-done(((bf16[1024,8,128]{2,0,1:T(8,128)(2,1)}), bf16[1024,8,128]{2,0,1:T(8,128)(2,1)}, u32[]{:S(2)}, u32[]{:S(2)}) %all-to-all-start.2) | async-done | bytes 2097184 | tf_op jit(solution)/shard_map/all_to_all | solution.py:111
  225.9 1.7 slice.15
  227.6 1.5 concatenate.20
  229.1 4.1 %copy.59 = bf16[64,128,128]{1,0,2:T(8,128)(2,1)} copy(bf16[64,128,128]{2,1,0:T(8,128)(2,1)} %bitcast.51) | data formatting | bytes 4194304 | tf_op jit(solution)/shard_map/reshape | solution.py:43
  233.2 4.1 %copy.58 = bf16[64,128,128]{1,0,2:T(8,128)(2,1)} copy(bf16[64,128,128]{2,1,0:T(8,128)(2,1)} %bitcast.11) | data formatting | bytes 4194304 | tf_op jit(solution)/shard_map/reshape | solution.py:42
  237.3 10.0 %fusion.16 = f32[64,128,128]{1,0,2:T(8,128)} fusion(bf16[128,256,128]{1,0,2:T(8,128)(2,1)} %copy.50, bf16[64,128,128]{1,0,2:T(8,128)(2,1)} %copy.59, bf16[64,128,128]{1,0,2:T(8,128)(2,1)} %copy.58), kind=kOutput, calls=%fused_computation.26 | convolution fusion | flops 545259520 | bytes 16777216 | tf_op jit(solution)/shard_map/bmc,imc->bic/dot_general | solution.py:57
  247.3 4.9 %all_to_all.68 = f32[8,1024,128]{1,0,2:T(8,128)} reshape(f32[64,128,128]{1,0,2:T(8,128)} %fusion.16) | data formatting | bytes 8388608 | tf_op jit(solution)/shard_map/all_to_all | solution.py:114
  252.2 6.6 %copy.51 = f32[8,1024,128]{1,2,0:T(8,128)} copy(f32[8,1024,128]{1,0,2:T(8,128)} %all_to_all.68) | data formatting | bytes 8388608 | tf_op jit(solution)/shard_map/all_to_all | solution.py:114
  258.8 4.8 %all-to-all-start.3 = ((f32[8,1024,128]{1,2,0:T(8,128)}), f32[8,1024,128]{1,2,0:T(8,128)}, u32[]{:S(2)}, u32[]{:S(2)}) async-start(f32[8,1024,128]{1,2,0:T(8,128)} %copy.51), calls=%async_computation.3 | async-start | bytes 8388608 | tf_op jit(solution)/shard_map/all_to_all | solution.py:114
  263.7 5.4 %copy.55 = f32[1024,1024]{1,0:T(8,128)} copy(f32[1024,1024]{0,1:T(8,128)} %get-tuple-element.38) | data formatting | bytes 8388608
  269.0 10.3 %fusion.13 = f32[128,128,256]{2,1,0:T(8,128)} fusion(bf16[64,128,128]{1,0,2:T(8,128)(2,1)} %copy.58, bf16[64,128,128]{1,0,2:T(8,128)(2,1)S(1)} %copy-done.2, bf16[64,128,128]{1,0,2:T(8,128)(2,1)} %copy.56), kind=kOutput, calls=%fused_computation.23 | convolution fusion | flops 545259520 | bytes 23068672 | tf_op jit(solution)/shard_map/while/body/eval_jaxpr/bic,bmc->cim/dot_general | solution.py:72
  279.4 17.9 %copy.60 = f32[128,128,256]{0,2,1:T(8,128)} copy(f32[128,128,256]{2,1,0:T(8,128)} %fusion.13) | data formatting | bytes 33554432 | tf_op jit(solution)/shard_map/while/body/eval_jaxpr/reshape | solution.py:75
  297.2 13.4 %concatenate.22 = f32[128,32896]{0,1:T(8,128)} pad(f32[128,32768]{0,1:T(8,128)} %bitcast.48, f32[]{:T(128)} %constant.12.clone.1), padding=0_0x0_128 | pad | bytes 33619972 | tf_op jit(solution)/shard_map/while/body/eval_jaxpr/concatenate | solution.py:76
  310.6 17.7 %reshape.94 = f32[128,128,257]{0,2,1:T(8,128)} reshape(f32[128,32896]{0,1:T(8,128)} %concatenate.22) | data formatting | bytes 33685504 | tf_op jit(solution)/shard_map/while/body/eval_jaxpr/reshape | solution.py:77
  328.3 4.5 %slice_reduce_fusion = f32[128,128]{0,1:T(8,128)S(1)} fusion(f32[128,128,257]{0,2,1:T(8,128)} %reshape.94), kind=kLoop, calls=%fused_computation.4 | loop fusion | flops 2080768 | bytes 8454144 | tf_op jit(solution)/shard_map/while/body/eval_jaxpr/reduce_sum | solution.py:78
  332.9 0.6 multiply_bitcast_fusion
  333.5 0.8 all-to-all-done.3
  334.3 0.0 copy-start.3
  334.3 5.5 %copy.52 = f32[1024,1024]{1,0:T(8,128)} copy(f32[1024,1024]{0,1:T(8,128)} %bitcast.16) | data formatting | bytes 8388608 | tf_op jit(solution)/shard_map/all_to_all | solution.py:114
  339.8 0.0 copy-done.3
  339.8 0.0 copy-start.1
  339.8 8.1 %convert_multiply_fusion.4 = (f32[1024,1024]{1,0:T(8,128)}, f32[1024,1024]{1,0:T(8,128)}) fusion(f32[1024,1024]{1,0:T(8,128)} %copy.52, bf16[1024,1024]{1,0:T(8,128)(2,1)} %param.7, bf16[1024,1024]{1,0:T(8,128)(2,1)S(1)} %copy-done.3), kind=kLoop, calls=%fused_computation.13 | loop fusion | flops 4194304 | bytes 16777216 | tf_op jit(solution)/shard_map/mul | solution.py:119
  347.9 0.0 reduce-scatter.2.cloned.1.call-done
  347.9 3.2 broadcast_multiply_fusion
  351.1 0.0 copy-done.1
  (3 shorter events, 0.0 us)
Async XLA Ops:
  7.2 11.8 %copy-start = (bf16[128,1024]{1,0:T(8,128)(2,1)S(1)}, bf16[128,1024]{1,0:T(8,128)(2,1)}, u32[]{:S(2)}) copy-start(bf16[128,1024]{1,0:T(8,128)(2,1)} %param.9) | copy-start | bytes 786436
  7.2 154.8 %all-gather.2.cloned.1.call-start = ((), (), s32[]{:S(2)}) async-start(), calls=%async_computation.5 | async-start | bytes 10485760 | tf_op jit(solution)/shard_map/all_gather | solution.py:100
  13.7 31.8 %all-to-all-start = ((bf16[1024,8,128]{0,2,1:T(8,128)(2,1)}), bf16[1024,8,128]{0,2,1:T(8,128)(2,1)S(1)}, u32[]{:S(2)}, u32[]{:S(2)}) async-start(bf16[1024,8,128]{0,2,1:T(8,128)(2,1)} %bitcast.50), calls=%async_computation | async-start | bytes 4194304 | tf_op jit(solution)/shard_map/all_to_all | solution.py:95
  56.2 5.6 %copy-start.2 = (bf16[64,128,128]{1,0,2:T(8,128)(2,1)S(1)}, bf16[64,128,128]{1,0,2:T(8,128)(2,1)}, u32[]{:S(2)}) copy-start(bf16[64,128,128]{1,0,2:T(8,128)(2,1)} %reshape.90) | copy-start | bytes 6291460
  82.5 53.7 %all-to-all-start.1 = ((f32[8,1024,128]{1,2,0:T(8,128)}), f32[8,1024,128]{1,2,0:T(8,128)}, u32[]{:S(2)}, u32[]{:S(2)}) async-start(f32[8,1024,128]{1,2,0:T(8,128)} %copy.45), calls=%async_computation.1 | async-start | bytes 8388608 | tf_op jit(solution)/shard_map/all_to_all | solution.py:98
  87.1 260.9 %reduce-scatter.2.cloned.1.call-start = ((), (), s32[]{:S(2)}) async-start(), calls=%async_computation.6 | async-start | bytes 18874368 | tf_op jit(solution)/shard_map/reduce_scatter | solution.py:116
  162.0 16.9 %copy-start.4 = (bf16[1024,4096]{1,0:T(8,128)(2,1)S(1)}, bf16[1024,4096]{1,0:T(8,128)(2,1)}, u32[]{:S(2)}) copy-start(bf16[1024,4096]{1,0:T(8,128)(2,1)} %all-gather.2.cloned.1.call-done) | copy-start | bytes 25165828
  194.8 31.0 %all-to-all-start.2 = ((bf16[1024,8,128]{2,0,1:T(8,128)(2,1)}), bf16[1024,8,128]{2,0,1:T(8,128)(2,1)}, u32[]{:S(2)}, u32[]{:S(2)}) async-start(bf16[1024,8,128]{2,0,1:T(8,128)(2,1)} %copy.47), calls=%async_computation.2 | async-start | bytes 4194304 | tf_op jit(solution)/shard_map/all_to_all | solution.py:111
  258.8 75.5 %all-to-all-start.3 = ((f32[8,1024,128]{1,2,0:T(8,128)}), f32[8,1024,128]{1,2,0:T(8,128)}, u32[]{:S(2)}, u32[]{:S(2)}) async-start(f32[8,1024,128]{1,2,0:T(8,128)} %copy.51), calls=%async_computation.3 | async-start | bytes 8388608 | tf_op jit(solution)/shard_map/all_to_all | solution.py:114
  334.3 5.5 %copy-start.3 = (bf16[1024,1024]{1,0:T(8,128)(2,1)S(1)}, bf16[1024,1024]{1,0:T(8,128)(2,1)}, u32[]{:S(2)}) copy-start(bf16[1024,1024]{1,0:T(8,128)(2,1)} %param.8) | copy-start | bytes 6291460
  339.8 11.2 %copy-start.1 = (bf16[128,1024]{1,0:T(8,128)(2,1)S(1)}, bf16[128,1024]{1,0:T(8,128)(2,1)}, u32[]{:S(2)}) copy-start(bf16[128,1024]{1,0:T(8,128)(2,1)} %param.9) | copy-start | bytes 786436
Sparse Core Ops, SparseCore 0:
  9.6 152.3 all-gather.1
  191.0 150.3 reduce-scatter.1
where the time goes:
time: 360 us; the launch traced here: 358 us
  local copies, waits for them, and re-layouts  147 us (41%)
  waiting for transfers between devices  81.9 us (23%)
  matrix products  75.4 us (21%)
  other arithmetic  19.7 us (5%)
  starting transfers between devices  19.4 us (5%)
  between operations  14.1 us (4%)
    all_to_all x1, waiting for transfers between devices, body(): lax.all_to_all(conv_chan, 'context', split_axis=0, concat_axis=1, tiled=T...  44.9 us
    convert_element_type x2, local copies, waits for them, and re-layouts, lag_table(): return table.astype(jnp.bfloat16)  26.1 us
    all_gather x1, waiting for transfers between devices, body(): segment = lax.all_gather(out_grad, 'tensor', axis=1, tiled=True)  25.8 us
    reshape x1, local copies, waits for them, and re-layouts, one_group(): flat = products.reshape(group_width, span * row_len)  17.9 us
    reshape x1, local copies, waits for them, and re-layouts, one_group(): skewed = padded.reshape(group_width, span, row_len + 1)  17.7 us
    all_to_all x3, local copies, waits for them, and re-layouts, body(): lax.all_to_all(mixed_grad_chan, 'context', split_axis=0, concat_axis=1, t...  17.1 us
    dot_general x2, matrix products, lag_table(): jnp.einsum('jim,jc->imc', onehot, taps, preferred_element_type=jnp.float32)  17.1 us
    dot_general x1, matrix products, body(): lax.dot_general(segment, out_weight, (((1,), (1,)), ((), ())), preferred_...  16.9 us
  transfers between devices with their start and end apart: 6, of which 5 were waited for; matrix products, arithmetic and copies ran while one was open for 56% of the time, Pallas kernels for 0%

commit v1 on v0

v1 whole, which is shorter than its diff:
```python
import functools
import math

import jax
import jax.numpy as jnp
import numpy as np
from jax import lax
from jax.experimental import pallas as pl
from jax.experimental.pallas import tpu as pltpu
from jax.sharding import PartitionSpec as P

BF16 = jnp.bfloat16
F32 = jnp.float32
VMEM_LIMIT = 48 * 1024 * 1024

ANYWHERE = pl.BlockSpec(memory_space=pl.ANY)
SCALAR = pl.BlockSpec(memory_space=pltpu.SMEM)


def weight_of(micros):
    return pl.CostEstimate(flops=1 << 20, bytes_accessed=int(micros * 3.7e6), transcendentals=0)


def split_const(matrix):
    high = matrix.astype(np.float32).astype(jnp.bfloat16)
    low = (matrix - high.astype(np.float64)).astype(np.float32).astype(jnp.bfloat16)
    return high, low


def odd_dft(span):
    freq = np.pi * (np.arange(span) + 0.5) / span
    pos = np.arange(span)
    ahead = np.outer(freq, pos)
    forward = np.concatenate([np.cos(ahead), -np.sin(ahead)], axis=0)

    def backward(at):
        angle = np.outer(at, freq)
        return np.concatenate([np.cos(angle), -np.sin(angle)], axis=1) / span

    f_high, f_low = split_const(forward)
    stacks = []
    for at in (span + pos, pos, span - pos):
        b_high, b_low = split_const(backward(at))
        stacks.append(np.concatenate([b_high, b_low], axis=0))
    return np.concatenate([f_high, f_low], axis=1), stacks


def dot(lhs, rhs):
    return jnp.dot(lhs, rhs, preferred_element_type=F32)


def to_freq(fwd, block):
    return dot(fwd, jnp.concatenate([block, block], axis=0))


def from_freq(stack, value, passes):
    span = stack.shape[0] // 2
    high = value.astype(BF16)
    if passes == 1:
        return dot(stack[:span], high)
    both = dot(stack, high)
    total = both[:span] + both[span:]
    if passes == 3:
        total = total + dot(stack[:span], (value - high.astype(F32)).astype(BF16))
    return total


def signs(span):
    row = lax.broadcasted_iota(jnp.int32, (span, 1), 0)
    return jnp.where(lax.rem(row, 2) == 0, 1.0, -1.0).astype(F32)


def window(first, second, sign):
    span = sign.shape[0]
    real = first[:span] + sign * second[span:]
    imag = first[span:] - sign * second[:span]
    return real, imag


def conv_kernel(start_ref, q_ref, k_ref, v_ref, halo_ref, taps_ref, fwd_ref, inv_ref, conv_ref, gated_ref):
    span = taps_ref.shape[0]
    sign = signs(span)
    taps = to_freq(fwd_ref[...], taps_ref[...])
    tr, ti = taps[:span], taps[span:]
    halo = jnp.where(start_ref[0] == 1, jnp.zeros_like(halo_ref), halo_ref[...])
    prev = to_freq(fwd_ref[...], halo)
    for b in range(q_ref.shape[0] // span):
        rows = pl.ds(b * span, span)
        mixed = (k_ref[rows, :].astype(F32) * v_ref[rows, :].astype(F32)).astype(BF16)
        cur = to_freq(fwd_ref[...], mixed)
        xr, xi = window(prev, cur, sign)
        spec = jnp.concatenate([xr * tr - xi * ti, xr * ti + xi * tr], axis=0)
        conv = from_freq(inv_ref[...], spec, 3)
        conv_ref[rows, :] = conv.astype(BF16)
        gated_ref[:, rows] = jnp.transpose(q_ref[rows, :].astype(F32) * conv).astype(BF16)
        prev = cur


def filtered(is_start, query, key, value, halo, taps, consts):
    rows, chans = query.shape
    span = taps.shape[0]
    tile = min(256, chans)
    fwd, stacks = consts
    col = pl.BlockSpec((rows, tile), lambda i: (0, i))
    short = pl.BlockSpec((span, tile), lambda i: (0, i))
    whole = pl.BlockSpec((2 * span, 2 * span), lambda i: (0, 0))
    return pl.pallas_call(
        conv_kernel,
        grid=(chans // tile,),
        in_specs=[SCALAR, col, col, col, short, short, whole, whole],
        out_specs=[
            col,
            pl.BlockSpec((tile, rows), lambda i: (i, 0)),
        ],
        out_shape=[
            jax.ShapeDtypeStruct((rows, chans), BF16),
            jax.ShapeDtypeStruct((chans, rows), BF16),
        ],
        compiler_params=pltpu.CompilerParams(vmem_limit_bytes=VMEM_LIMIT),
        cost_estimate=weight_of(100),
        name="filtered",
    )(is_start, query, key, value, halo, taps, fwd, stacks[0])


def pair_dot(lhs, rhs):
    return lax.dot_general(lhs, rhs, (((1,), (1,)), ((), ())), preferred_element_type=F32)


def read_pick(refs, second):
    value = refs[0][...]
    for ref in refs[1:]:
        value = jnp.where(second, ref[...], value)
    return value


class Operands:
    def __init__(self, slots, weight, tile, wide, weighted):
        rows = slots[0][1][0][0].shape[0]
        per_core = weight.shape[0] // (2 * wide)
        self.arrays, self.specs, self.groups, self.weights = [], [], [], []
        for held, parts, offset in slots:
            for side in range(2):
                group = []
                for array, at in parts:
                    column = at + side * (array.shape[1] // (2 * wide))
                    group.append(len(self.arrays))
                    self.arrays.append(array)
                    self.specs.append(pl.BlockSpec((rows, wide), functools.partial(self.fixed, column)))
                self.groups.append(group)
        for held, parts, offset in slots:
            for side in range(2):
                if held not in weighted:
                    self.weights.append(None)
                    continue
                at = side * per_core + offset // wide
                self.weights.append(len(self.arrays))
                self.arrays.append(weight)
                self.specs.append(
                    pl.BlockSpec((tile, wide), functools.partial(self.placed, held, 2 * per_core, at))
                )

    @staticmethod
    def fixed(column, i, place):
        return (0, column)

    @staticmethod
    def placed(held, blocks, at, i, place):
        return (i, place[held] * blocks + at)

    def values(self, refs, place_ref):
        second = place_ref[7] == 1
        sides = [read_pick([refs[n] for n in group], second) for group in self.groups]
        return [jnp.concatenate(sides[n : n + 2], axis=1) for n in range(0, len(sides), 2)]

    def weight_values(self, refs):
        sides = [None if n is None else refs[n][...] for n in self.weights]
        return [
            None if sides[n] is None else jnp.concatenate(sides[n : n + 2], axis=1)
            for n in range(0, len(sides), 2)
        ]


def project_kernel(place_ref, *refs, operands, products, earlier, carried):
    count = len(operands.arrays)
    blocks, rest = refs[:count], list(refs[count + earlier :])
    values = operands.values(blocks, place_ref)
    if "outer" in products:
        gated_ref = rest.pop(0)
        outs = [rest.pop() for _ in range(2 * len(values))][::-1]
        first_core = place_ref[4] == 0
        wide = outs[0].shape[1]
        outers = [dot(gated_ref[...], value).astype(BF16) for value in values]
        if len(outers) == 2:
            first_keeps = place_ref[5] == 0
            outers = [
                jnp.where(first_keeps, outers[0], outers[1]),
                jnp.where(first_keeps, outers[1], outers[0]),
            ]
        for n, outer in enumerate(outers):
            left, right = outer[:, :wide], outer[:, wide:]
            outs[2 * n][...] = jnp.where(first_core, left, right)
            outs[2 * n + 1][...] = jnp.where(first_core, right, left)
    if "inner" in products:
        total = rest.pop(0)[...] if carried else None
        for value, weight in zip(values, operands.weight_values(blocks)):
            if weight is not None:
                part = pair_dot(value, weight)
                total = part if total is None else total + part
        rest[0][...] = total


def project(place, slots, gated_t, weight, acc, wide, products, earlier, weighted, micros=100):
    chans, rows = gated_t.shape
    tile = min(256 if "inner" in products else 512, chans)
    operands = Operands(slots, weight, tile, wide, weighted)
    col = pl.BlockSpec((rows, tile), lambda i, p: (0, i))
    carried = "inner" in products and acc is not None
    outs, out_specs, specs, arrays = [], [], [], []
    if "outer" in products:
        specs.append(pl.BlockSpec((tile, rows), lambda i, p: (i, 0)))
        arrays.append(gated_t)
    if "inner" in products:
        outs.append(jax.ShapeDtypeStruct((rows, chans), F32))
        out_specs.append(col)
        if carried:
            specs.append(col)
            arrays.append(acc)
    if "outer" in products:
        outs += [jax.ShapeDtypeStruct((chans, wide), BF16)] * (2 * len(slots))
        out_specs += [pl.BlockSpec((tile, wide), lambda i, p: (i, 0))] * (2 * len(slots))
    return pl.pallas_call(
        functools.partial(
            project_kernel, operands=operands, products=products, earlier=len(earlier), carried=carried
        ),
        grid_spec=pltpu.PrefetchScalarGridSpec(
            num_scalar_prefetch=1,
            grid=(chans // tile,),
            in_specs=operands.specs + [ANYWHERE] * len(earlier) + specs,
            out_specs=out_specs,
        ),
        out_shape=outs,
        compiler_params=pltpu.CompilerParams(vmem_limit_bytes=VMEM_LIMIT),
        cost_estimate=weight_of(micros),
        name="project",
    )(place, *operands.arrays, *earlier, *arrays)


def grad_kernel(place_ref, *refs, operands, earlier, scale):
    count = len(operands.arrays) if operands else 0
    blocks = refs[:count]
    count += earlier
    acc_ref, conv_ref, q_ref, k_ref, v_ref, start_ref, before_ref, taps_ref, fwd_ref, inv_ref, lag_ref = refs[
        count : count + 11
    ]
    gq_ref, gk_ref, gv_ref, first_ref, last_ref, gf_ref = refs[count + 11 :]
    span, chans = taps_ref.shape
    sign = signs(span)
    taps = to_freq(fwd_ref[...], taps_ref[...])
    tr, ti = taps[:span], taps[span:]
    acc_r = jnp.zeros((span, chans), F32)
    acc_i = jnp.zeros((span, chans), F32)
    if operands:
        value = jnp.concatenate(operands.values(blocks, place_ref), axis=1)
        weight = jnp.concatenate(operands.weight_values(blocks), axis=1)
        added = pair_dot(value, weight)
    last = q_ref.shape[0] // span - 1
    halo = jnp.where(start_ref[0] == 1, jnp.zeros_like(before_ref), before_ref[...])
    prev_mixed = to_freq(fwd_ref[...], halo)
    prev = None
    for b in range(last + 1):
        rows = pl.ds(b * span, span)
        gg = acc_ref[rows, :]
        if operands:
            gg = gg + added[b * span : (b + 1) * span]
        gq_ref[rows, :] = gg * conv_ref[rows, :].astype(F32)
        grad_conv = (gg * q_ref[rows, :].astype(F32)).astype(BF16)
        if b == 0:
            first_ref[...] = grad_conv
        if b == last:
            last_ref[...] = grad_conv
        grad = to_freq(fwd_ref[...], grad_conv)
        mixed = (k_ref[rows, :].astype(F32) * v_ref[rows, :].astype(F32)).astype(BF16)
        cur = to_freq(fwd_ref[...], mixed)
        xr, xi = window(prev_mixed, cur, sign)
        prev_mixed = cur
        gr, gi = grad[:span], grad[span:]
        acc_r += gr * xr + gi * xi
        acc_i += gr * xi - gi * xr
        if b > 0:
            rows = pl.ds((b - 1) * span, span)
            back = filtered_back(prev, grad, tr, ti, sign, inv_ref[...])
            gk_ref[rows, :] = back * v_ref[rows, :].astype(F32)
            gv_ref[rows, :] = back * k_ref[rows, :].astype(F32)
        prev = grad
    part = from_freq(lag_ref[...], jnp.concatenate([acc_r, acc_i], axis=0), 3) * scale
    wide = gf_ref.shape[2]
    for n in range(gf_ref.shape[0]):
        gf_ref[n] = part[:, n * wide : (n + 1) * wide]


def filtered_back(cur, later, tr, ti, sign, stack):
    wr, wi = window(cur, later, sign)
    return from_freq(stack, jnp.concatenate([wr * tr + wi * ti, wi * tr - wr * ti], axis=0), 2)


def gradients(
    place, slots, weight, wide, acc, conv, query, key, value, is_start, before, taps, consts, contexts, scale, earlier
):
    rows, chans = query.shape
    span = taps.shape[0]
    tile = min(256, chans)
    own = chans // contexts
    fwd, stacks = consts
    operands = Operands(slots, weight, tile, wide, [held for held, _, _ in slots]) if slots else None
    col = pl.BlockSpec((rows, tile), lambda i, p: (0, i))
    short = pl.BlockSpec((span, tile), lambda i, p: (0, i))
    whole = pl.BlockSpec((2 * span, 2 * span), lambda i, p: (0, 0))
    return pl.pallas_call(
        functools.partial(grad_kernel, operands=operands, earlier=len(earlier), scale=scale),
        grid_spec=pltpu.PrefetchScalarGridSpec(
            num_scalar_prefetch=1,
            grid=(chans // tile,),
            in_specs=(operands.specs if slots else [])
            + [ANYWHERE] * len(earlier)
            + [col, col, col, col, col, SCALAR, short, short, whole, whole, whole],
            out_specs=[
                col,
                col,
                col,
                short,
                short,
                pl.BlockSpec((tile // own, span, own), lambda i, p: (i, 0, 0)),
            ],
        ),
        out_shape=[jax.ShapeDtypeStruct((rows, chans), F32)] * 3
        + [
            jax.ShapeDtypeStruct((span, chans), BF16),
            jax.ShapeDtypeStruct((span, chans), BF16),
            jax.ShapeDtypeStruct((contexts, span, own), F32),
        ],
        compiler_params=pltpu.CompilerParams(vmem_limit_bytes=VMEM_LIMIT),
        cost_estimate=weight_of(100),
        name="gradients",
    )(
        place, *(operands.arrays if slots else []), *earlier,
        acc, conv, query, key, value, is_start, before, taps, fwd, stacks[1], stacks[2],
    )


def last_kernel(end_ref, last_ref, after_ref, k_ref, v_ref, taps_ref, fwd_ref, inv_ref, gk_in, gv_in, gk_ref, gv_ref):
    span = taps_ref.shape[0]
    taps = to_freq(fwd_ref[...], taps_ref[...])
    cur = to_freq(fwd_ref[...], last_ref[...])
    later = to_freq(fwd_ref[...], jnp.where(end_ref[0] == 1, jnp.zeros_like(after_ref), after_ref[...]))
    back = filtered_back(cur, later, taps[:span], taps[span:], signs(span), inv_ref[...])
    gk_ref[...] = back * v_ref[...].astype(F32)
    gv_ref[...] = back * k_ref[...].astype(F32)


def last_rows(is_end, last, after_rows, key, value, taps, grad_key, grad_value, consts):
    rows, chans = key.shape
    span = taps.shape[0]
    tile = min(512, chans)
    fwd, stacks = consts
    bottom = rows // span - 1
    low = pl.BlockSpec((span, tile), lambda i: (bottom, i))
    short = pl.BlockSpec((span, tile), lambda i: (0, i))
    whole = pl.BlockSpec((2 * span, 2 * span), lambda i: (0, 0))
    return pl.pallas_call(
        last_kernel,
        grid=(chans // tile,),
        in_specs=[
            SCALAR, short, short, low, low, short, whole, whole, ANYWHERE, ANYWHERE,
        ],
        out_specs=[low, low],
        out_shape=[jax.ShapeDtypeStruct((rows, chans), F32)] * 2,
        input_output_aliases={8: 0, 9: 1},
        compiler_params=pltpu.CompilerParams(vmem_limit_bytes=VMEM_LIMIT),
        cost_estimate=weight_of(2),
        name="last_rows",
    )(is_end, last, after_rows, key, value, taps, fwd, stacks[1], grad_key, grad_value)


def finish_kernel(early_ref, *refs, own, groups, across, scale):
    out = refs[-1]
    for cols, late in group_sums(refs[own:], groups, across):
        early = sum(ref[:, cols].astype(F32) for ref in refs[:own])
        out[:, cols] = jnp.where(early_ref[0] == 1, early, late) * scale


def finish(is_early, own_terms, groups, across, out, at, scale):
    rows, wide = across[0].shape
    tile = rows // 2
    terms = [term for group in groups for term in group] + list(across)
    sizes = [(len(group), group[0].shape[1]) for group in groups]
    block = pl.BlockSpec((tile, wide), lambda i, p: (i, at))
    held = [] if out is None else [out]
    return pl.pallas_call(
        functools.partial(finish_kernel, own=len(own_terms), groups=sizes, across=len(across), scale=scale),
        grid_spec=pltpu.PrefetchScalarGridSpec(
            num_scalar_prefetch=1,
            grid=(rows // tile,),
            in_specs=[block] * len(own_terms)
            + [pl.BlockSpec((tile, term.shape[1]), lambda i, p: (i, 0)) for term in terms]
            + [ANYWHERE] * len(held),
            out_specs=block,
        ),
        out_shape=jax.ShapeDtypeStruct((rows, own_terms[0].shape[1]), F32),
        input_output_aliases={1 + len(own_terms) + len(terms): 0} if held else {},
        compiler_params=pltpu.CompilerParams(vmem_limit_bytes=VMEM_LIMIT),
        cost_estimate=weight_of(2),
        name="finish",
    )(is_early, *own_terms, *terms, *held)


def on_line(pairs, contexts):
    return [(a * contexts + c, b * contexts + c) for a, b in pairs for c in range(contexts)]


def send_line(value, pairs, contexts):
    return lax.ppermute(value, ("tensor", "context"), on_line(pairs, contexts))


def swap(value, bit, contexts):
    return lax.ppermute(value, "context", [(c, c ^ bit) for c in range(contexts)])


def pieces_kernel(*refs, pieces):
    outs = refs[-len(pieces) :]
    half = refs[0].shape[1] // 2
    for (offset, wide), out in zip(pieces, outs):
        for side in range(2):
            at = side * half + offset
            out[:, side * wide : (side + 1) * wide] = refs[0][:, at : at + wide]


def cut(block, pieces, earlier):
    rows, chans = block.shape
    return pl.pallas_call(
        functools.partial(pieces_kernel, pieces=pieces),
        grid=(4,),
        in_specs=[pl.BlockSpec((rows // 4, chans), lambda i: (i, 0))] + [ANYWHERE] * len(earlier),
        out_specs=[pl.BlockSpec((rows // 4, 2 * wide), lambda i: (i, 0)) for _, wide in pieces],
        out_shape=[jax.ShapeDtypeStruct((rows, 2 * wide), BF16) for _, wide in pieces],
        cost_estimate=weight_of(100),
        name="cut",
    )(block, *earlier)


def hold_kernel(*refs):
    pass


def hold(value, earlier):
    return pl.pallas_call(
        hold_kernel,
        in_specs=[ANYWHERE] * (1 + len(earlier)),
        out_specs=ANYWHERE,
        out_shape=jax.ShapeDtypeStruct(value.shape, value.dtype),
        input_output_aliases={0: 0},
        cost_estimate=weight_of(1),
        name="hold",
    )(value, *earlier)


def group_sums(refs, groups, across):
    at, column, wide_refs = 0, 0, refs[sum(count for count, _ in groups) :][:across]
    for count, wide in groups:
        cols = slice(column, column + wide)
        terms = [ref[...] for ref in refs[at : at + count]] + [ref[:, cols] for ref in wide_refs]
        yield cols, sum(term.astype(F32) for term in terms)
        at, column = at + count, column + wide


def add_kernel(*refs, groups, across):
    for cols, total in group_sums(refs, groups, across):
        refs[-1][:, cols] = total.astype(BF16)


def add_blocks(groups, earlier, micros=1, across=()):
    rows = groups[0][0].shape[0]
    tile = rows // 2
    terms = [term for group in groups for term in group] + list(across)
    sizes = [(len(group), group[0].shape[1]) for group in groups]
    wide = sum(size for _, size in sizes)
    return pl.pallas_call(
        functools.partial(add_kernel, groups=sizes, across=len(across)),
        grid=(rows // tile,),
        in_specs=[pl.BlockSpec((tile, term.shape[1]), lambda i: (i, 0)) for term in terms]
        + [ANYWHERE] * len(earlier),
        out_specs=pl.BlockSpec((tile, wide), lambda i: (i, 0)),
        out_shape=jax.ShapeDtypeStruct((rows, wide), BF16),
        compiler_params=pltpu.CompilerParams(vmem_limit_bytes=VMEM_LIMIT),
        cost_estimate=weight_of(micros),
        name="add_blocks",
    )(*terms, *earlier)


def body(query, key, value, taps, weight, out_grad, tensors, contexts):
    rows, chans = query.shape
    span = taps.shape[0]
    scale = 1.0 / math.sqrt(rows * contexts)
    consts = odd_dft(span)
    ctx = lax.axis_index("context")
    ten = lax.axis_index("tensor")

    tail = lambda x: x[rows - span :].astype(F32)
    last_mixed = (tail(key) * tail(value)).astype(BF16)
    before = lax.ppermute(last_mixed, "context", [(c, (c + 1) % contexts) for c in range(contexts)])
    is_start = (ctx == 0).astype(jnp.int32).reshape(1)
    is_end = (ctx == contexts - 1).astype(jnp.int32).reshape(1)

    if tensors == 4 and contexts == 8 and chans % 1024 == 0:
        half = chans // 2
        pieces = [(0, half // 2), (half // 2, half // 4), (3 * half // 4, half // 4)]
        chip, core = ctx // 2, lax.rem(ctx, 2)
        low = ten < 2
        edge = (ten == 0) | (ten == 3)
        held = [ten, ten ^ 1, jnp.where(low, 2, 1), jnp.where(low, 3, 0)]
        sides = [(h ^ chip) & 1 for h in held]
        early = jnp.stack(held + [core] + sides[:2] + [edge]).astype(jnp.int32)
        late = jnp.stack(held + [core] + sides[2:] + [edge]).astype(jnp.int32)
        is_early = ((chip // 2) == (ten // 2)).astype(jnp.int32).reshape(1)

        swap_ends = [(0, 1), (1, 0), (2, 3), (3, 2)]
        swap_mid = [(1, 2), (2, 1)]
        over = lambda value, bit: swap(value, bit, contexts)
        pair = send_line(out_grad, swap_ends, contexts)
        near_mid = send_line(out_grad, swap_mid, contexts)
        conv, gated_t = filtered(is_start, query, key, value, before, taps, consts)
        near_end = send_line(near_mid, swap_ends, contexts)

        slots = [(0, [(out_grad, 0)], 0), (1, [(pair, 0)], 0)]
        gg, keep, other_keep, cross, other_cross = project(
            early, slots, gated_t, weight, None, half, ("outer", "inner"), [near_mid], [0, 1]
        )
        far_mid = [send_line(block, swap_mid, contexts) for block in cut(pair, pieces, [gg])]
        far_end = [send_line(block, swap_ends, contexts) for block in far_mid]
        cross_in = add_blocks([[cross, over(other_cross, 1)]], [])
        own_terms = [keep, over(other_keep, 1), over(cross_in, 2)]

        slots = [(2, [(near_mid, 0), (near_end, 0)], 0)]
        (gg,) = project(late, slots, gated_t, weight, gg, half, ("inner",), [cross_in], [2])
        own_in = add_blocks([own_terms], [gg])
        own_terms.append(over(own_in, 4))

        keeps, crosses = [], []
        for n, (offset, wide) in enumerate(pieces):
            slots = [
                (2, [(near_mid, offset // wide), (near_end, offset // wide)], offset),
                (3, [(far_mid[n], 0), (far_end[n], 0)], offset),
            ]
            if n == 0:
                gg, *outer = project(
                    late, slots, gated_t, weight, gg, wide, ("outer", "inner"), [own_in], [3]
                )
            else:
                earlier = [] if n == 1 else [gg, own_terms[-1]]
                outer = project(late, slots, gated_t, weight, None, wide, ("outer",), earlier, [])
            keep, other_keep, cross, other_cross = outer
            keeps.append([keep, over(other_keep, 1)])
            crosses.append([cross, over(other_cross, 1)])
            if n == 1:
                first_cross = add_blocks([crosses[0]], [keep], 0.1)
                keeps[0].append(over(first_cross, 2))
                (gg,) = project(
                    late, slots[1:], gated_t, weight, gg, wide, ("inner",), [first_cross], [3], 0.1
                )
        first_in = add_blocks([keeps[0]], [])
        last_cross = add_blocks(crosses[1:], [first_in])
        last_over = over(last_cross, 2)
        grad_query, grad_key, grad_value, first, last, parts = gradients(
            late, slots[1:], weight, wide, gg, conv, query, key, value, is_start, before, taps, consts,
            contexts, scale, [last_cross],
        )
        first_over = over(first_in, 4)
        grad_weight = finish(is_early, own_terms, keeps[:1], [first_over], None, 0, scale)
        last_in = add_blocks(keeps[1:], [first], 1, [last_over])
        grad_weight = finish(
            is_early, own_terms, keeps[1:], [last_over, over(last_in, 4)], grad_weight, 1, scale
        )
    else:
        conv, gated_t = filtered(is_start, query, key, value, before, taps, consts)
        segment = lax.all_gather(out_grad, "tensor", axis=1, tiled=True)
        gg = lax.dot_general(segment, weight, (((1,), (1,)), ((), ())), preferred_element_type=F32)
        outer = dot(gated_t, segment)
        grad_weight = lax.psum_scatter(outer, "context", scatter_dimension=1, tiled=True) * scale
        grad_query, grad_key, grad_value, first, last, parts = gradients(
            jnp.zeros((1,), jnp.int32), None, weight, 0, gg, conv, query, key, value, is_start, before, taps, consts,
            contexts, scale, [],
        )

    after_rows = lax.ppermute(first, "context", [(c, (c - 1) % contexts) for c in range(contexts)])
    parts = hold(parts, [after_rows])
    parts = lax.all_to_all(parts, "context", split_axis=0, concat_axis=0, tiled=True)
    grad_filter = jnp.sum(parts, axis=0)
    grad_key, grad_value = last_rows(
        is_end, last, after_rows, key, value, taps, grad_key, grad_value, consts
    )
    return (grad_query, grad_key, grad_value, grad_filter, grad_weight)


def solution(mesh):
    placed = (
        P("context", "tensor"),
        P("context", "tensor"),
        P("context", "tensor"),
        P(None, "tensor"),
        P("tensor", None),
        P("context", "tensor"),
    )
    run = functools.partial(body, tensors=mesh.shape["tensor"], contexts=mesh.shape["context"])
    return jax.shard_map(
        run,
        mesh=mesh,
        in_specs=placed,
        out_specs=(
            P("context", "tensor"),
            P("context", "tensor"),
            P("context", "tensor"),
            P(None, ("tensor", "context")),
            P("tensor", "context"),
        ),
        check_vma=False,
    )
```

time: 360 us -> 212 us (0.59)
  local copies, waits for them, and re-layouts: 147 us -> 13.8 us
  Pallas kernels: 0 us -> 83.9 us
  matrix products: 75.4 us -> 0 us
  starting transfers between devices: 19.4 us -> 77.7 us
  waiting for transfers between devices: 81.9 us -> 31.3 us
  other arithmetic: 19.7 us -> 2.8 us
  between operations: 14.1 us -> 1.09 us
    pallas_call x0 -> x19, Pallas kernels: none -> 83.9 us  [the longest x6 43.5 us: project(): pl.pallas_call(functools.partial(project_kernel, operands=operands, produ...]
    dot_general x7 -> x0, matrix products: 75.4 us -> none  [the longest x2 17.1 us: lag_table(): jnp.einsum('jim,jc->imc', onehot, taps, preferred_element_type=jnp.float32)]
    ppermute x0 -> x25, starting transfers between devices: none -> 73.5 us  [the longest x9 62.3 us: send_line(): return lax.ppermute(value, ('tensor', 'context'), on_line(pairs, contexts))]
    reshape x6 -> x0, local copies, waits for them, and re-layouts: 52.2 us -> none  [the longest x1 17.9 us: one_group(): flat = products.reshape(group_width, span * row_len)]
    all_to_all x4 -> x1, waiting for transfers between devices: 55.5 us -> 8.28 us  [body(): lax.all_to_all(parts, 'context', split_axis=0, concat_axis=0, tiled=True)]
    all_to_all x8 -> x0, local copies, waits for them, and re-layouts: 37.4 us -> none  [the longest x3 17.1 us: body(): lax.all_to_all(mixed_grad_chan, 'context', split_axis=0, concat_axis=1, t...]
    convert_element_type x3 -> x0, local copies, waits for them, and re-layouts: 28.7 us -> none  [the longest x2 26.1 us: lag_table(): return table.astype(jnp.bfloat16)]
    all_gather x1 -> x0, waiting for transfers between devices: 25.8 us -> none  [body(): segment = lax.all_gather(out_grad, 'tensor', axis=1, tiled=True)]
  transfers between devices with their start and end apart: 6 -> 26, of which waited for: 5 -> 5; matrix products, arithmetic and copies ran while one was open for 56% -> 1% of each run, Pallas kernels for 0% -> 39%
where the time goes in v1:
time: 212 us; the launch traced here: 211 us
  Pallas kernels  83.9 us (40%)
  starting transfers between devices  77.7 us (37%)
  waiting for transfers between devices  31.3 us (15%)
  local copies, waits for them, and re-layouts  13.8 us (7%)
  other arithmetic  2.8 us (1%)
    ppermute x9, starting transfers between devices, send_line(): return lax.ppermute(value, ('tensor', 'context'), on_line(pairs, contexts))  62.3 us
    pallas_call x6, Pallas kernels, project(): pl.pallas_call(functools.partial(project_kernel, operands=operands, produ...  43.5 us
    pallas_call x1, Pallas kernels, gradients(): pl.pallas_call(functools.partial(grad_kernel, operands=operands, earlier=...  13.9 us
    unnamed x76, local copies, waits for them, and re-layouts  13.6 us
    ppermute x14, starting transfers between devices, swap(): lax.ppermute(value, 'context', [(c, c ^ bit) for c in range(contexts)])  10.1 us
    ppermute x14, waiting for transfers between devices, swap(): lax.ppermute(value, 'context', [(c, c ^ bit) for c in range(contexts)])  9.43 us
    pallas_call x1, Pallas kernels, filtered(): pl.pallas_call(conv_kernel, grid=(chans // tile,), in_specs=[SCALAR, col,...  8.9 us
    all_to_all x1, waiting for transfers between devices, body(): lax.all_to_all(parts, 'context', split_axis=0, concat_axis=0, tiled=True)  8.28 us
  transfers between devices with their start and end apart: 26, of which 5 were waited for; matrix products, arithmetic and copies ran while one was open for 1% of the time, Pallas kernels for 39%

profile of v1, /device:TPU:0, one launch (start us, length us, event | category | flops | bytes accessed | tf_op | source)
XLA Modules:
  0.0 210.6 jit_solution(3515418691849592234)
XLA Ops:
  0.6 2.0 collective-permute-start.1
  2.7 4.6 %collective-permute-start = (bf16[1024,1024]{1,0:T(8,128)(2,1)}, bf16[1024,1024]{1,0:T(8,128)(2,1)}, u32[]{:S(2)}, u32[]{:S(2)}) collective-permute-start(bf16[1024,1024]{1,0:T(8,128)(2,1)} %refs_1_.1), channel_id=1, source_target_pairs={{0,8},{1,9},{2,10},{3,11},{4,12},{5,13},{6,14},{7,15},{8,0},{9,1},... | collective-permute-start | bytes 6291464 | tf_op jit(solution)/shard_map/ppermute | solution.py:421
  7.2 1.1 multiply_convert_fusion
  8.4 0.1 stack.57.place_ref
  8.5 6.6 %collective-permute-done.2.halo_ref.refs_13_ = bf16[128,1024]{1,0:T(8,128)(2,1)S(1)} collective-permute-done((bf16[128,1024]{1,0:T(8,128)(2,1)S(1)}, bf16[128,1024]{1,0:T(8,128)(2,1)S(1)}, u32[]{:S(2)}, u32[]{:S(2)}) %collective-permute-start.2) | collective-permute-done | bytes 262176 | tf_op jit(solution)/shard_map/ppermute | solution.py:509
  15.1 0.9 copy-done.6
  16.0 0.9 copy-done.19
  16.9 0.9 copy-done.36
  17.8 8.9 %filtered.1 = (bf16[1024,1024]{1,0:T(8,128)(2,1)S(1)}, bf16[1024,1024]{1,0:T(8,128)(2,1)S(1)}) custom-call(s32[1]{0:T(128)} %bitcast.10.start_ref.refs_12_, bf16[1024,1024]{1,0:T(8,128)(2,1)} %refs_9_.3, bf16[1024,1024]{1,0:T(8,128)(2,1)} %k_ref.3, bf16[1024,1024]{1,0:T(8,128)(2,1)} %v_ref.3, bf16[128,1024]{1,0:T(8,128)(2,1)S(1)} %collective-permute-done.2.halo_ref.refs_13_, ...), custom_call_target="tpu_custom_call" | custom-call | flops 1048576 | bytes 370000000 | tf_op jit(solution)/shard_map/filtered/pallas_call | solution.py:107
  26.7 1.3 copy-done.2
  28.1 1.4 copy-done.8
  29.4 23.8 %collective-permute-start.5 = (bf16[1024,1024]{1,0:T(8,128)(2,1)}, bf16[1024,1024]{1,0:T(8,128)(2,1)S(1)}, u32[]{:S(2)}, u32[]{:S(2)}) collective-permute-start(bf16[1024,1024]{1,0:T(8,128)(2,1)} %collective-permute-done.1.refs_8_.refs_0_.refs_2_), channel_id=1, source_target_pairs={{0,8},{1,9},{2,10},{3,11},{4,12},{5,13},{6,14},{7,15},{8,0},{9,1},... | collective-permute-start | bytes 6291464 | tf_op jit(solution)/shard_map/ppermute | solution.py:421
  53.2 14.0 %project.6 = (f32[1024,1024]{1,0:T(8,128)}, bf16[1024,512]{1,0:T(8,128)(2,1)S(1)}, bf16[1024,512]{1,0:T(8,128)(2,1)S(1)}, bf16[1024,512]{1,0:T(8,128)(2,1)S(1)}, bf16[1024,512]{1,0:T(8,128)(2,1)}) custom-call(s32[8]{0:T(128)S(1)} %stack.57.place_ref, bf16[1024,1024]{1,0:T(8,128)(2,1)} %refs_1_.1, bf16[1024,1024]{1,0:T(8,128)(2,1)} %refs_1_.1, ...), custom_call_target="tpu_custom_call" | custom-call | flops 1048576 | bytes 370000000 | tf_op jit(solution)/shard_map/project/pallas_call | solution.py:231
  67.3 1.0 copy-done.21
  68.2 1.0 copy-done.37
  69.2 3.8 %cut.1 = (bf16[1024,512]{1,0:T(8,128)(2,1)}, bf16[1024,256]{1,0:T(8,128)(2,1)}, bf16[1024,256]{1,0:T(8,128)(2,1)}) custom-call(bf16[1024,1024]{1,0:T(8,128)(2,1)} %collective-permute-done.refs_2_.refs_3_.refs_0_, f32[1024,1024]{1,0:T(8,128)} %get-tuple-element.37.refs_1_.refs_7_), custom_call_target="tpu_custom_call" | custom-call | flops 1048576 | bytes 370000000 | tf_op jit(solution)/shard_map/cut/pallas_call | solution.py:439
  73.1 1.6 collective-permute-start.9
  74.7 0.5 collective-permute-start.11
  75.2 1.2 copy-done.22
  76.4 2.2 %add_blocks.6.refs_6_ = bf16[1024,512]{1,0:T(8,128)(2,1)} custom-call(bf16[1024,512]{1,0:T(8,128)(2,1)S(1)} %copy-done.22, bf16[1024,512]{1,0:T(8,128)(2,1)} %collective-permute-done.12.refs_1_), custom_call_target="tpu_custom_call" | custom-call | flops 1048576 | bytes 3700000 | tf_op jit(solution)/shard_map/add_blocks/pallas_call | solution.py:486
  78.6 1.5 collective-permute-start.13
  80.1 22.1 %collective-permute-start.10 = (bf16[1024,512]{1,0:T(8,128)(2,1)}, bf16[1024,512]{1,0:T(8,128)(2,1)}, u32[]{:S(2)}, u32[]{:S(2)}) collective-permute-start(bf16[1024,512]{1,0:T(8,128)(2,1)} %collective-permute-done.9.refs_4_.refs_6_), channel_id=1, source_target_pairs={{0,8},{1,9},{2,10},{3,11},{4,12},{5,13},{6,14},{7,15},{8,0},{9,1},... | collective-permute-start | bytes 3145736 | tf_op jit(solution)/shard_map/ppermute | solution.py:421
  102.2 1.4 collective-permute-start.6
  103.6 0.1 stack.54.place_ref
  103.7 0.9 collective-permute-start.3
  104.6 7.9 %project.8.refs_3_.refs_12_ = f32[1024,1024]{1,0:T(8,128)} custom-call(s32[8]{0:T(128)S(1)} %stack.54.place_ref, bf16[1024,1024]{1,0:T(8,128)(2,1)} %collective-permute-done.1.refs_8_.refs_0_.refs_2_, bf16[1024,1024]{1,0:T(8,128)(2,1)S(1)} %collective-permute-done.5.refs_1_.refs_3_, bf16[1024,1024]{1,0:T(8,128)(2,1)} %collective-permute-done.1.refs_8_.refs_0_.refs_2_, ...), custom_call_target="tpu_custom_call" | custom-call | flops 1048576 | bytes 370000000 | tf_op jit(solution)/shard_map/project/pallas_call | solution.py:231
  112.5 1.7 add_blocks.7.refs_10_
  114.2 1.6 collective-permute-start.15
  115.8 3.7 %collective-permute-start.7 = (bf16[1024,256]{1,0:T(8,128)(2,1)}, bf16[1024,256]{1,0:T(8,128)(2,1)S(1)}, u32[]{:S(2)}, u32[]{:S(2)}) collective-permute-start(bf16[1024,256]{1,0:T(8,128)(2,1)} %collective-permute-done.6.refs_4_.refs_6_.refs_0_.refs_2_), channel_id=1, source_target_pairs={{0,8},{1,9},{2,10},{3,11},{4,12},{5,13},{6,14},{7,15},{8,0},{9,1},... | collective-permute-start | bytes 1572872 | tf_op jit(solution)/shard_map/ppermute | solution.py:421
  119.6 7.0 %collective-permute-done.10.refs_5_.refs_7_ = bf16[1024,512]{1,0:T(8,128)(2,1)} collective-permute-done((bf16[1024,512]{1,0:T(8,128)(2,1)}, bf16[1024,512]{1,0:T(8,128)(2,1)}, u32[]{:S(2)}, u32[]{:S(2)}) %collective-permute-start.10) | collective-permute-done | bytes 1048608 | tf_op jit(solution)/shard_map/ppermute | solution.py:421
  126.5 9.5 %project.9 = (f32[1024,1024]{1,0:T(8,128)}, bf16[1024,256]{1,0:T(8,128)(2,1)S(1)}, bf16[1024,256]{1,0:T(8,128)(2,1)S(1)}, bf16[1024,256]{1,0:T(8,128)(2,1)S(1)}, bf16[1024,256]{1,0:T(8,128)(2,1)S(1)}) custom-call(s32[8]{0:T(128)S(1)} %stack.54.place_ref, bf16[1024,1024]{1,0:T(8,128)(2,1)} %collective-permute-done.1.refs_8_.refs_0_.refs_2_, ...), custom_call_target="tpu_custom_call" | custom-call | flops 1048576 | bytes 370000000 | tf_op jit(solution)/shard_map/project/pallas_call | solution.py:231
  136.1 2.1 %collective-permute-start.4 = (bf16[1024,256]{1,0:T(8,128)(2,1)S(1)}, bf16[1024,256]{1,0:T(8,128)(2,1)S(1)}, u32[]{:S(2)}, u32[]{:S(2)}) collective-permute-start(bf16[1024,256]{1,0:T(8,128)(2,1)S(1)} %collective-permute-done.3.refs_4_.refs_6_.refs_0_.refs_2_), channel_id=1, source_target_pairs={{0,8},{1,9},{2,10},{3,11},{4,12},{5,13},{6,14},{7,15},{8,0},{9,1},... | collective-permute-start | bytes 1572872 | tf_op jit(solution)/shard_map/ppermute | solution.py:421
  138.2 0.2 collective-permute-start.17
  138.4 3.8 %project.7 = (bf16[1024,128]{1,0:T(8,128)(2,1)S(1)}, bf16[1024,128]{1,0:T(8,128)(2,1)S(1)}, bf16[1024,128]{1,0:T(8,128)(2,1)S(1)}, bf16[1024,128]{1,0:T(8,128)(2,1)S(1)}) custom-call(s32[8]{0:T(128)S(1)} %stack.54.place_ref, bf16[1024,1024]{1,0:T(8,128)(2,1)} %collective-permute-done.1.refs_8_.refs_0_.refs_2_, bf16[1024,1024]{1,0:T(8,128)(2,1)} %copy-done, ...), custom_call_target="tpu_custom_call" | custom-call | flops 1048576 | bytes 370000000 | tf_op jit(solution)/shard_map/project/pallas_call | solution.py:231
  142.2 0.2 add_blocks.8.refs_6_
  142.4 1.6 collective-permute-start.18
  143.9 0.1 collective-permute-start.8
  144.0 4.7 %project.10.refs_8_.refs_7_ = f32[1024,1024]{1,0:T(8,128)S(1)} custom-call(s32[8]{0:T(128)S(1)} %stack.54.place_ref, bf16[1024,256]{1,0:T(8,128)(2,1)} %collective-permute-done.6.refs_4_.refs_6_.refs_0_.refs_2_, bf16[1024,256]{1,0:T(8,128)(2,1)S(1)} %collective-permute-done.7.refs_5_.refs_7_.refs_1_.refs_3_, ...), custom_call_target="tpu_custom_call" | custom-call | flops 1048576 | bytes 370000 | tf_op jit(solution)/shard_map/project/pallas_call | solution.py:231
  148.8 2.0 copy-done.1
  150.8 3.6 %project.11 = (bf16[1024,128]{1,0:T(8,128)(2,1)S(1)}, bf16[1024,128]{1,0:T(8,128)(2,1)S(1)}, bf16[1024,128]{1,0:T(8,128)(2,1)S(1)}, bf16[1024,128]{1,0:T(8,128)(2,1)S(1)}) custom-call(s32[8]{0:T(128)S(1)} %stack.54.place_ref, bf16[1024,1024]{1,0:T(8,128)(2,1)} %collective-permute-done.1.refs_8_.refs_0_.refs_2_, bf16[1024,1024]{1,0:T(8,128)(2,1)} %copy-done, ...), custom_call_target="tpu_custom_call" | custom-call | flops 1048576 | bytes 370000000 | tf_op jit(solution)/shard_map/project/pallas_call | solution.py:231
  154.4 0.5 collective-permute-start.16
  154.9 1.7 collective-permute-done.18.refs_2_.refs_6_
  156.6 0.9 add_blocks.9.refs_4_
  157.6 0.2 add_blocks.10.refs_6_
  157.8 1.6 collective-permute-start.22
  159.4 0.5 collective-permute-start.21
  159.9 13.9 %gradients.1 = (f32[1024,1024]{1,0:T(8,128)}, f32[1024,1024]{1,0:T(8,128)}, f32[1024,1024]{1,0:T(8,128)}, bf16[128,1024]{1,0:T(8,128)(2,1)S(1)}, bf16[128,1024]{...) custom-call(s32[8]{0:T(128)S(1)} %stack.54.place_ref, ...), custom_call_target="tpu_custom_call" | custom-call | flops 1048576 | bytes 370000000 | tf_op jit(solution)/shard_map/gradients/pallas_call | solution.py:318
  173.8 0.8 copy-done.16
  174.7 1.1 collective-permute-start.19
  175.8 0.5 collective-permute-start.24
  176.4 1.0 add_blocks.11
  177.3 0.8 copy-done.17
  178.2 1.5 collective-permute-start.23
  179.7 0.7 copy-done.23
  180.4 4.2 %all-to-all-start = ((f32[8,128,128]{2,1,0:T(8,128)}), f32[8,128,128]{2,1,0:T(8,128)}, u32[]{:S(2)}, u32[]{:S(2)}) async-start(f32[8,128,128]{2,1,0:T(8,128)} %hold.1), calls=%async_computation | async-start | bytes 1048576 | tf_op jit(solution)/shard_map/all_to_all | solution.py:595
  184.6 7.7 %collective-permute-done.24.refs_7_ = bf16[1024,256]{1,0:T(8,128)(2,1)} collective-permute-done((bf16[1024,256]{1,0:T(8,128)(2,1)}, bf16[1024,256]{1,0:T(8,128)(2,1)}, u32[]{:S(2)}, u32[]{:S(2)}) %collective-permute-start.24) | collective-permute-done | bytes 524320 | tf_op jit(solution)/shard_map/ppermute | solution.py:425
  192.4 2.8 %finish.2.refs_10_ = f32[1024,512]{1,0:T(8,128)} custom-call(s32[1]{0:T(128)} %bitcast.12.early_ref, bf16[1024,512]{1,0:T(8,128)(2,1)S(1)} %get-tuple-element.43.refs_0_, bf16[1024,512]{1,0:T(8,128)(2,1)} %collective-permute-done.11.refs_1_, bf16[1024,512]{1,0:T(8,128)(2,1)} %collective-permute-done.13.refs_2_, bf16[1024,512]{1,0:T(8,128)(2,1)} %copy-done.5, ...), custom_call_target="tpu_custom_call" | custom-call | flops 1048576 | bytes 7400000 | tf_op jit(solution)/shard_map/finish/pallas_call | solution.py:398
  195.2 0.3 copy-done.4
  195.5 0.1 copy-done.24
  195.6 0.1 copy-done.34
  195.7 2.2 %last_rows.1 = (f32[1024,1024]{1,0:T(8,128)}, f32[1024,1024]{1,0:T(8,128)}) custom-call(s32[1]{0:T(128)} %bitcast.11.end_ref, bf16[128,1024]{1,0:T(8,128)(2,1)S(1)} %copy-done.34, bf16[128,1024]{1,0:T(8,128)(2,1)S(1)} %copy-done.24, bf16[1024,1024]{1,0:T(8,128)(2,1)S(1)} %copy-done.3, ...), custom_call_target="tpu_custom_call", output_to_operand_aliasing={{0}: (8, {}), {1}: (9, {})} | custom-call | flops 1048576 | bytes 7400000 | tf_op jit(solution)/shard_map/last_rows/pallas_call | solution.py:369
  197.9 8.3 %all-to-all-done = f32[8,128,128]{2,1,0:T(8,128)} async-done(((f32[8,128,128]{2,1,0:T(8,128)}), f32[8,128,128]{2,1,0:T(8,128)}, u32[]{:S(2)}, u32[]{:S(2)}) %all-to-all-start) | async-done | bytes 524320 | tf_op jit(solution)/shard_map/all_to_all | solution.py:595
  206.2 1.7 reduce_sum.9
  207.9 2.6 %finish.3 = f32[1024,512]{1,0:T(8,128)} custom-call(s32[1]{0:T(128)} %bitcast.12.early_ref, bf16[1024,512]{1,0:T(8,128)(2,1)S(1)} %get-tuple-element.43.refs_0_, bf16[1024,512]{1,0:T(8,128)(2,1)} %collective-permute-done.11.refs_1_, bf16[1024,512]{1,0:T(8,128)(2,1)} %collective-permute-done.13.refs_2_, ...), custom_call_target="tpu_custom_call", output_to_operand_aliasing={{}: (11, {})} | custom-call | flops 1048576 | bytes 7400000 | tf_op jit(solution)/shard_map/finish/pallas_call | solution.py:398
  (87 shorter events, 0.4 us)
Async XLA Ops:
  0.6 28.8 %collective-permute-start.1 = (bf16[1024,1024]{1,0:T(8,128)(2,1)}, bf16[1024,1024]{1,0:T(8,128)(2,1)}, u32[]{:S(2)}, u32[]{:S(2)}) collective-permute-start(bf16[1024,1024]{1,0:T(8,128)(2,1)} %refs_1_.1), channel_id=1, source_target_pairs={{8,16},{9,17},{10,18},{11,19},{12,20},{13,21},{14,22},{15,23},{16,... | collective-permute-start | bytes 6291464 | tf_op jit(solution)/shard_map/ppermute | solution.py:421
  2.7 50.6 %collective-permute-start = (bf16[1024,1024]{1,0:T(8,128)(2,1)}, bf16[1024,1024]{1,0:T(8,128)(2,1)}, u32[]{:S(2)}, u32[]{:S(2)}) collective-permute-start(bf16[1024,1024]{1,0:T(8,128)(2,1)} %refs_1_.1), channel_id=1, source_target_pairs={{0,8},{1,9},{2,10},{3,11},{4,12},{5,13},{6,14},{7,15},{8,0},{9,1},... | collective-permute-start | bytes 6291464 | tf_op jit(solution)/shard_map/ppermute | solution.py:421
  8.3 6.7 %collective-permute-start.2 = (bf16[128,1024]{1,0:T(8,128)(2,1)S(1)}, bf16[128,1024]{1,0:T(8,128)(2,1)S(1)}, u32[]{:S(2)}, u32[]{:S(2)}) collective-permute-start(bf16[128,1024]{1,0:T(8,128)(2,1)S(1)} %multiply_convert_fusion), channel_id=1, source_target_pairs={{0,1},{1,2},{2,3},{3,4},{4,5},{5,6},{6,7},{7,0},{8,9},{9,10},{10,1... | collective-permute-start | bytes 786440 | tf_op jit(solution)/shard_map/ppermute | solution.py:509
  15.1 1.0 copy-start.6
  16.0 0.9 copy-start.19
  16.9 0.9 copy-start.36
  26.7 1.3 copy-start.2
  28.1 1.4 copy-start.8
  29.4 74.3 %collective-permute-start.5 = (bf16[1024,1024]{1,0:T(8,128)(2,1)}, bf16[1024,1024]{1,0:T(8,128)(2,1)S(1)}, u32[]{:S(2)}, u32[]{:S(2)}) collective-permute-start(bf16[1024,1024]{1,0:T(8,128)(2,1)} %collective-permute-done.1.refs_8_.refs_0_.refs_2_), channel_id=1, source_target_pairs={{0,8},{1,9},{2,10},{3,11},{4,12},{5,13},{6,14},{7,15},{8,0},{9,1},... | collective-permute-start | bytes 6291464 | tf_op jit(solution)/shard_map/ppermute | solution.py:421
  67.3 1.0 copy-start.21
  68.2 1.0 copy-start.37
  69.2 6.0 %collective-permute-start.12 = (bf16[1024,512]{1,0:T(8,128)(2,1)}, bf16[1024,512]{1,0:T(8,128)(2,1)}, u32[]{:S(2)}, u32[]{:S(2)}) collective-permute-start(bf16[1024,512]{1,0:T(8,128)(2,1)} %get-tuple-element.46), channel_id=1, source_target_pairs={{0,1},{1,0},{2,3},{3,2},{4,5},{5,4},{6,7},{7,6},{8,9},{9,8},{10,11... | collective-permute-start | bytes 3145736 | tf_op jit(solution)/shard_map/ppermute | solution.py:425
  73.1 7.0 %collective-permute-start.9 = (bf16[1024,512]{1,0:T(8,128)(2,1)}, bf16[1024,512]{1,0:T(8,128)(2,1)}, u32[]{:S(2)}, u32[]{:S(2)}) collective-permute-start(bf16[1024,512]{1,0:T(8,128)(2,1)} %get-tuple-element.42), channel_id=1, source_target_pairs={{8,16},{9,17},{10,18},{11,19},{12,20},{13,21},{14,22},{15,23},{16,... | collective-permute-start | bytes 3145736 | tf_op jit(solution)/shard_map/ppermute | solution.py:421
  74.7 37.8 %collective-permute-start.11 = (bf16[1024,512]{1,0:T(8,128)(2,1)}, bf16[1024,512]{1,0:T(8,128)(2,1)}, u32[]{:S(2)}, u32[]{:S(2)}) collective-permute-start(bf16[1024,512]{1,0:T(8,128)(2,1)} %copy-done.37), channel_id=1, source_target_pairs={{0,1},{1,0},{2,3},{3,2},{4,5},{5,4},{6,7},{7,6},{8,9},{9,8},{10,11... | collective-permute-start | bytes 3145736 | tf_op jit(solution)/shard_map/ppermute | solution.py:425
  75.2 1.2 copy-start.22
  78.6 33.9 %collective-permute-start.13 = (bf16[1024,512]{1,0:T(8,128)(2,1)}, bf16[1024,512]{1,0:T(8,128)(2,1)}, u32[]{:S(2)}, u32[]{:S(2)}) collective-permute-start(bf16[1024,512]{1,0:T(8,128)(2,1)} %add_blocks.6.refs_6_), channel_id=1, source_target_pairs={{0,2},{1,3},{2,0},{3,1},{4,6},{5,7},{6,4},{7,5},{8,10},{9,11},{10,... | collective-permute-start | bytes 3145736 | tf_op jit(solution)/shard_map/ppermute | solution.py:425
  80.1 46.4 %collective-permute-start.10 = (bf16[1024,512]{1,0:T(8,128)(2,1)}, bf16[1024,512]{1,0:T(8,128)(2,1)}, u32[]{:S(2)}, u32[]{:S(2)}) collective-permute-start(bf16[1024,512]{1,0:T(8,128)(2,1)} %collective-permute-done.9.refs_4_.refs_6_), channel_id=1, source_target_pairs={{0,8},{1,9},{2,10},{3,11},{4,12},{5,13},{6,14},{7,15},{8,0},{9,1},... | collective-permute-start | bytes 3145736 | tf_op jit(solution)/shard_map/ppermute | solution.py:421
  102.2 13.6 %collective-permute-start.6 = (bf16[1024,256]{1,0:T(8,128)(2,1)}, bf16[1024,256]{1,0:T(8,128)(2,1)}, u32[]{:S(2)}, u32[]{:S(2)}) collective-permute-start(bf16[1024,256]{1,0:T(8,128)(2,1)} %get-tuple-element.39), channel_id=1, source_target_pairs={{8,16},{9,17},{10,18},{11,19},{12,20},{13,21},{14,22},{15,23},{16,... | collective-permute-start | bytes 1572872 | tf_op jit(solution)/shard_map/ppermute | solution.py:421
  103.7 8.8 %copy-start = (bf16[1024,1024]{1,0:T(8,128)(2,1)}, bf16[1024,1024]{1,0:T(8,128)(2,1)S(1)}, u32[]{:S(2)}) copy-start(bf16[1024,1024]{1,0:T(8,128)(2,1)S(1)} %collective-permute-done.5.refs_1_.refs_3_) | copy-start | bytes 6291460
  103.7 32.3 %collective-permute-start.3 = (bf16[1024,256]{1,0:T(8,128)(2,1)}, bf16[1024,256]{1,0:T(8,128)(2,1)S(1)}, u32[]{:S(2)}, u32[]{:S(2)}) collective-permute-start(bf16[1024,256]{1,0:T(8,128)(2,1)} %get-tuple-element.38), channel_id=1, source_target_pairs={{8,16},{9,17},{10,18},{11,19},{12,20},{13,21},{14,22},{15,23},{16,... | collective-permute-start | bytes 1572872 | tf_op jit(solution)/shard_map/ppermute | solution.py:421
  114.2 36.5 %collective-permute-start.15 = (bf16[1024,512]{1,0:T(8,128)(2,1)S(1)}, bf16[1024,512]{1,0:T(8,128)(2,1)S(1)}, u32[]{:S(2)}, u32[]{:S(2)}) collective-permute-start(bf16[1024,512]{1,0:T(8,128)(2,1)S(1)} %add_blocks.7.refs_10_), channel_id=1, source_target_pairs={{0,4},{1,5},{2,6},{3,7},{4,0},{5,1},{6,2},{7,3},{8,12},{9,13},{10,... | collective-permute-start | bytes 3145736 | tf_op jit(solution)/shard_map/ppermute | solution.py:425
  115.8 22.5 %collective-permute-start.7 = (bf16[1024,256]{1,0:T(8,128)(2,1)}, bf16[1024,256]{1,0:T(8,128)(2,1)S(1)}, u32[]{:S(2)}, u32[]{:S(2)}) collective-permute-start(bf16[1024,256]{1,0:T(8,128)(2,1)} %collective-permute-done.6.refs_4_.refs_6_.refs_0_.refs_2_), channel_id=1, source_target_pairs={{0,8},{1,9},{2,10},{3,11},{4,12},{5,13},{6,14},{7,15},{8,0},{9,1},... | collective-permute-start | bytes 1572872 | tf_op jit(solution)/shard_map/ppermute | solution.py:421
  136.0 20.6 %copy-start.10 = (bf16[1024,256]{1,0:T(8,128)(2,1)}, bf16[1024,256]{1,0:T(8,128)(2,1)S(1)}, u32[]{:S(2)}) copy-start(bf16[1024,256]{1,0:T(8,128)(2,1)S(1)} %get-tuple-element.53.refs_0_.refs_4_) | copy-start | bytes 1572868
  136.0 6.2 %collective-permute-start.14 = (bf16[1024,256]{1,0:T(8,128)(2,1)S(1)}, bf16[1024,256]{1,0:T(8,128)(2,1)S(1)}, u32[]{:S(2)}, u32[]{:S(2)}) collective-permute-start(bf16[1024,256]{1,0:T(8,128)(2,1)S(1)} %get-tuple-element.48), channel_id=1, source_target_pairs={{0,1},{1,0},{2,3},{3,2},{4,5},{5,4},{6,7},{7,6},{8,9},{9,8},{10,11... | collective-permute-start | bytes 1572872 | tf_op jit(solution)/shard_map/ppermute | solution.py:425
  136.1 14.7 %collective-permute-start.4 = (bf16[1024,256]{1,0:T(8,128)(2,1)S(1)}, bf16[1024,256]{1,0:T(8,128)(2,1)S(1)}, u32[]{:S(2)}, u32[]{:S(2)}) collective-permute-start(bf16[1024,256]{1,0:T(8,128)(2,1)S(1)} %collective-permute-done.3.refs_4_.refs_6_.refs_0_.refs_2_), channel_id=1, source_target_pairs={{0,8},{1,9},{2,10},{3,11},{4,12},{5,13},{6,14},{7,15},{8,0},{9,1},... | collective-permute-start | bytes 1572872 | tf_op jit(solution)/shard_map/ppermute | solution.py:421
  138.2 16.7 %collective-permute-start.17 = (bf16[1024,256]{1,0:T(8,128)(2,1)S(1)}, bf16[1024,256]{1,0:T(8,128)(2,1)S(1)}, u32[]{:S(2)}, u32[]{:S(2)}) collective-permute-start(bf16[1024,256]{1,0:T(8,128)(2,1)S(1)} %get-tuple-element.54), channel_id=1, source_target_pairs={{0,1},{1,0},{2,3},{3,2},{4,5},{5,4},{6,7},{7,6},{8,9},{9,8},{10,11... | collective-permute-start | bytes 1572872 | tf_op jit(solution)/shard_map/ppermute | solution.py:425
  142.4 14.2 %collective-permute-start.18 = (bf16[1024,256]{1,0:T(8,128)(2,1)S(1)}, bf16[1024,256]{1,0:T(8,128)(2,1)S(1)}, u32[]{:S(2)}, u32[]{:S(2)}) collective-permute-start(bf16[1024,256]{1,0:T(8,128)(2,1)S(1)} %add_blocks.8.refs_6_), channel_id=1, source_target_pairs={{0,2},{1,3},{2,0},{3,1},{4,6},{5,7},{6,4},{7,5},{8,10},{9,11},{10,... | collective-permute-start | bytes 1572872 | tf_op jit(solution)/shard_map/ppermute | solution.py:425
  143.9 13.7 %collective-permute-start.8 = (bf16[1024,128]{1,0:T(8,128)(2,1)S(1)}, bf16[1024,128]{1,0:T(8,128)(2,1)S(1)}, u32[]{:S(2)}, u32[]{:S(2)}) collective-permute-start(bf16[1024,128]{1,0:T(8,128)(2,1)S(1)} %get-tuple-element.41), channel_id=1, source_target_pairs={{0,1},{1,0},{2,3},{3,2},{4,5},{5,4},{6,7},{7,6},{8,9},{9,8},{10,11... | collective-permute-start | bytes 786440 | tf_op jit(solution)/shard_map/ppermute | solution.py:425
  148.7 2.0 copy-start.1
  150.7 3.6 %copy-start.5 = (bf16[1024,512]{1,0:T(8,128)(2,1)}, bf16[1024,512]{1,0:T(8,128)(2,1)S(1)}, u32[]{:S(2)}) copy-start(bf16[1024,512]{1,0:T(8,128)(2,1)S(1)} %collective-permute-done.15.refs_9_.refs_3_) | copy-start | bytes 3145732
  154.4 21.9 %copy-start.25 = (bf16[1024,128]{1,0:T(8,128)(2,1)}, bf16[1024,128]{1,0:T(8,128)(2,1)S(1)}, u32[]{:S(2)}) copy-start(bf16[1024,128]{1,0:T(8,128)(2,1)S(1)} %get-tuple-element.65.refs_2_.refs_6_) | copy-start | bytes 786436
  154.4 3.2 %collective-permute-start.16 = (bf16[1024,128]{1,0:T(8,128)(2,1)S(1)}, bf16[1024,128]{1,0:T(8,128)(2,1)S(1)}, u32[]{:S(2)}, u32[]{:S(2)}) collective-permute-start(bf16[1024,128]{1,0:T(8,128)(2,1)S(1)} %get-tuple-element.52), channel_id=1, source_target_pairs={{0,1},{1,0},{2,3},{3,2},{4,5},{5,4},{6,7},{7,6},{8,9},{9,8},{10,11... | collective-permute-start | bytes 786440 | tf_op jit(solution)/shard_map/ppermute | solution.py:425
  154.9 2.9 %copy-start.12 = (bf16[1024,256]{1,0:T(8,128)(2,1)}, bf16[1024,256]{1,0:T(8,128)(2,1)S(1)}, u32[]{:S(2)}) copy-start(bf16[1024,256]{1,0:T(8,128)(2,1)S(1)} %collective-permute-done.17.refs_1_.refs_5_) | copy-start | bytes 1572868
  156.6 1.2 copy-start.14
  156.6 3.3 %copy-start.7 = (bf16[128,1024]{1,0:T(8,128)(2,1)S(1)}, bf16[128,1024]{1,0:T(8,128)(2,1)}, u32[]{:S(2)}) copy-start(bf16[128,1024]{1,0:T(8,128)(2,1)} %taps_ref.3) | copy-start | bytes 786436
  156.6 3.3 %copy-start.9 = (bf16[1024,1024]{1,0:T(8,128)(2,1)S(1)}, bf16[1024,1024]{1,0:T(8,128)(2,1)}, u32[]{:S(2)}) copy-start(bf16[1024,1024]{1,0:T(8,128)(2,1)} %copy-done.8) | copy-start | bytes 6291460
  156.6 3.3 %copy-start.20 = (bf16[256,256]{1,0:T(8,128)(2,1)S(1)}, bf16[256,256]{1,0:T(8,128)(2,1)}, u32[]{:S(2)}) copy-start(bf16[256,256]{1,0:T(8,128)(2,1)} %constant.53.clone.fwd_ref.refs_15_) | copy-start | bytes 393220
  156.6 3.3 %copy-start.31 = (bf16[256,256]{1,0:T(8,128)(2,1)S(1)}, bf16[256,256]{1,0:T(8,128)(2,1)}, u32[]{:S(2)}) copy-start(bf16[256,256]{1,0:T(8,128)(2,1)} %constant.55.clone.refs_16_.inv_ref) | copy-start | bytes 393220
  156.6 3.3 %copy-start.35 = (bf16[256,256]{1,0:T(8,128)(2,1)S(1)}, bf16[256,256]{1,0:T(8,128)(2,1)}, u32[]{:S(2)}) copy-start(bf16[256,256]{1,0:T(8,128)(2,1)} %constant.56.clone.refs_17_) | copy-start | bytes 393220
  157.8 18.5 %collective-permute-start.22 = (bf16[1024,256]{1,0:T(8,128)(2,1)S(1)}, bf16[1024,256]{1,0:T(8,128)(2,1)S(1)}, u32[]{:S(2)}, u32[]{:S(2)}) collective-permute-start(bf16[1024,256]{1,0:T(8,128)(2,1)S(1)} %add_blocks.10.refs_6_), channel_id=1, source_target_pairs={{0,2},{1,3},{2,0},{3,1},{4,6},{5,7},{6,4},{7,5},{8,10},{9,11},{10,... | collective-permute-start | bytes 1572872 | tf_op jit(solution)/shard_map/ppermute | solution.py:425
  159.4 16.9 %collective-permute-start.20 = (bf16[1024,128]{1,0:T(8,128)(2,1)S(1)}, bf16[1024,128]{1,0:T(8,128)(2,1)S(1)}, u32[]{:S(2)}, u32[]{:S(2)}) collective-permute-start(bf16[1024,128]{1,0:T(8,128)(2,1)S(1)} %get-tuple-element.64), channel_id=1, source_target_pairs={{0,1},{1,0},{2,3},{3,2},{4,5},{5,4},{6,7},{7,6},{8,9},{9,8},{10,11... | collective-permute-start | bytes 786440 | tf_op jit(solution)/shard_map/ppermute | solution.py:425
  159.4 16.9 %collective-permute-start.21 = (bf16[1024,128]{1,0:T(8,128)(2,1)S(1)}, bf16[1024,128]{1,0:T(8,128)(2,1)S(1)}, u32[]{:S(2)}, u32[]{:S(2)}) collective-permute-start(bf16[1024,128]{1,0:T(8,128)(2,1)S(1)} %get-tuple-element.66), channel_id=1, source_target_pairs={{0,1},{1,0},{2,3},{3,2},{4,5},{5,4},{6,7},{7,6},{8,9},{9,8},{10,11... | collective-permute-start | bytes 786440 | tf_op jit(solution)/shard_map/ppermute | solution.py:425
  173.8 0.8 copy-start.16
  174.7 5.0 %copy-start.33 = (bf16[128,1024]{1,0:T(8,128)(2,1)}, bf16[128,1024]{1,0:T(8,128)(2,1)S(1)}, u32[]{:S(2)}) copy-start(bf16[128,1024]{1,0:T(8,128)(2,1)S(1)} %get-tuple-element.57.last_ref) | copy-start | bytes 786436
  174.7 5.0 %collective-permute-start.19 = (bf16[128,1024]{1,0:T(8,128)(2,1)S(1)}, bf16[128,1024]{1,0:T(8,128)(2,1)S(1)}, u32[]{:S(2)}, u32[]{:S(2)}) collective-permute-start(bf16[128,1024]{1,0:T(8,128)(2,1)S(1)} %get-tuple-element.58.refs_5_), channel_id=1, source_target_pairs={{0,7},{1,0},{2,1},{3,2},{4,3},{5,4},{6,5},{7,6},{8,15},{9,8},{10,9... | collective-permute-start | bytes 786440 | tf_op jit(solution)/shard_map/ppermute | solution.py:593
  175.8 16.6 %collective-permute-start.24 = (bf16[1024,256]{1,0:T(8,128)(2,1)}, bf16[1024,256]{1,0:T(8,128)(2,1)}, u32[]{:S(2)}, u32[]{:S(2)}) collective-permute-start(bf16[1024,256]{1,0:T(8,128)(2,1)} %add_blocks.9.refs_4_), channel_id=1, source_target_pairs={{0,4},{1,5},{2,6},{3,7},{4,0},{5,1},{6,2},{7,3},{8,12},{9,13},{10,... | collective-permute-start | bytes 1572872 | tf_op jit(solution)/shard_map/ppermute | solution.py:425
  176.3 3.4 %copy-start.27 = (bf16[1024,128]{1,0:T(8,128)(2,1)}, bf16[1024,128]{1,0:T(8,128)(2,1)S(1)}, u32[]{:S(2)}) copy-start(bf16[1024,128]{1,0:T(8,128)(2,1)S(1)} %collective-permute-done.20.refs_1_.refs_5_) | copy-start | bytes 786436
  176.3 3.4 %copy-start.29 = (bf16[1024,128]{1,0:T(8,128)(2,1)}, bf16[1024,128]{1,0:T(8,128)(2,1)S(1)}, u32[]{:S(2)}) copy-start(bf16[1024,128]{1,0:T(8,128)(2,1)S(1)} %collective-permute-done.21.refs_3_.refs_7_) | copy-start | bytes 786436
  176.3 16.0 %copy-start.11 = (bf16[1024,256]{1,0:T(8,128)(2,1)S(1)}, bf16[1024,256]{1,0:T(8,128)(2,1)}, u32[]{:S(2)}) copy-start(bf16[1024,256]{1,0:T(8,128)(2,1)} %copy-done.10) | copy-start | bytes 1572868
  176.3 16.0 %copy-start.13 = (bf16[1024,256]{1,0:T(8,128)(2,1)S(1)}, bf16[1024,256]{1,0:T(8,128)(2,1)}, u32[]{:S(2)}) copy-start(bf16[1024,256]{1,0:T(8,128)(2,1)} %copy-done.12) | copy-start | bytes 1572868
  176.3 16.0 %copy-start.15 = (bf16[1024,256]{1,0:T(8,128)(2,1)S(1)}, bf16[1024,256]{1,0:T(8,128)(2,1)}, u32[]{:S(2)}) copy-start(bf16[1024,256]{1,0:T(8,128)(2,1)} %copy-done.14) | copy-start | bytes 1572868
  177.3 0.8 copy-start.17
  178.2 29.7 %collective-permute-start.23 = (bf16[1024,256]{1,0:T(8,128)(2,1)}, bf16[1024,256]{1,0:T(8,128)(2,1)}, u32[]{:S(2)}, u32[]{:S(2)}) collective-permute-start(bf16[1024,256]{1,0:T(8,128)(2,1)} %add_blocks.11), channel_id=1, source_target_pairs={{0,4},{1,5},{2,6},{3,7},{4,0},{5,1},{6,2},{7,3},{8,12},{9,13},{10,... | collective-permute-start | bytes 1572872 | tf_op jit(solution)/shard_map/ppermute | solution.py:425
  179.7 0.7 copy-start.23
  180.4 25.8 %all-to-all-start = ((f32[8,128,128]{2,1,0:T(8,128)}), f32[8,128,128]{2,1,0:T(8,128)}, u32[]{:S(2)}, u32[]{:S(2)}) async-start(f32[8,128,128]{2,1,0:T(8,128)} %hold.1), calls=%async_computation | async-start | bytes 1048576 | tf_op jit(solution)/shard_map/all_to_all | solution.py:595
  192.4 2.8 %copy-start.3 = (bf16[1024,1024]{1,0:T(8,128)(2,1)S(1)}, bf16[1024,1024]{1,0:T(8,128)(2,1)}, u32[]{:S(2)}) copy-start(bf16[1024,1024]{1,0:T(8,128)(2,1)} %k_ref.3) | copy-start | bytes 6291460
  192.4 3.1 %copy-start.4 = (bf16[1024,1024]{1,0:T(8,128)(2,1)S(1)}, bf16[1024,1024]{1,0:T(8,128)(2,1)}, u32[]{:S(2)}) copy-start(bf16[1024,1024]{1,0:T(8,128)(2,1)} %v_ref.3) | copy-start | bytes 6291460
  192.4 3.2 %copy-start.24 = (bf16[128,1024]{1,0:T(8,128)(2,1)S(1)}, bf16[128,1024]{1,0:T(8,128)(2,1)}, u32[]{:S(2)}) copy-start(bf16[128,1024]{1,0:T(8,128)(2,1)} %copy-done.23) | copy-start | bytes 786436
  192.4 3.2 %copy-start.32 = (bf16[256,256]{1,0:T(8,128)(2,1)S(1)}, bf16[256,256]{1,0:T(8,128)(2,1)}, u32[]{:S(2)}) copy-start(bf16[256,256]{1,0:T(8,128)(2,1)} %constant.55.clone.refs_16_.inv_ref) | copy-start | bytes 393220
  192.4 3.3 %copy-start.34 = (bf16[128,1024]{1,0:T(8,128)(2,1)S(1)}, bf16[128,1024]{1,0:T(8,128)(2,1)}, u32[]{:S(2)}) copy-start(bf16[128,1024]{1,0:T(8,128)(2,1)} %copy-done.33) | copy-start | bytes 786436
  195.7 12.2 %copy-start.18 = (bf16[1024,256]{1,0:T(8,128)(2,1)S(1)}, bf16[1024,256]{1,0:T(8,128)(2,1)}, u32[]{:S(2)}) copy-start(bf16[1024,256]{1,0:T(8,128)(2,1)} %copy-done.17) | copy-start | bytes 1572868
  195.7 12.2 %copy-start.26 = (bf16[1024,128]{1,0:T(8,128)(2,1)S(1)}, bf16[1024,128]{1,0:T(8,128)(2,1)}, u32[]{:S(2)}) copy-start(bf16[1024,128]{1,0:T(8,128)(2,1)} %copy-done.25) | copy-start | bytes 786436
  195.7 12.2 %copy-start.28 = (bf16[1024,128]{1,0:T(8,128)(2,1)S(1)}, bf16[1024,128]{1,0:T(8,128)(2,1)}, u32[]{:S(2)}) copy-start(bf16[1024,128]{1,0:T(8,128)(2,1)} %copy-done.27) | copy-start | bytes 786436
  195.7 12.2 %copy-start.30 = (bf16[1024,128]{1,0:T(8,128)(2,1)S(1)}, bf16[1024,128]{1,0:T(8,128)(2,1)}, u32[]{:S(2)}) copy-start(bf16[1024,128]{1,0:T(8,128)(2,1)} %copy-done.29) | copy-start | bytes 786436

commit v2 on v1

--- a/solution.py
+++ b/solution.py
@@ -28,7 +28,7 @@
 
 
 def odd_dft(span):
-    freq = np.pi * (np.arange(span) + 0.5) / span
+    freq = np.pi * (np.arange(span) + 0.5) / span * (1 - 2 * (np.arange(span) % 2))
     pos = np.arange(span)
     ahead = np.outer(freq, pos)
     forward = np.concatenate([np.cos(ahead), -np.sin(ahead)], axis=0)
@@ -65,21 +65,15 @@
     return total
 
 
-def signs(span):
-    row = lax.broadcasted_iota(jnp.int32, (span, 1), 0)
-    return jnp.where(lax.rem(row, 2) == 0, 1.0, -1.0).astype(F32)
-
-
-def window(first, second, sign):
-    span = sign.shape[0]
-    real = first[:span] + sign * second[span:]
-    imag = first[span:] - sign * second[:span]
+def window(first, second):
+    span = first.shape[0] // 2
+    real = first[:span] + second[span:]
+    imag = first[span:] - second[:span]
     return real, imag
 
 
 def conv_kernel(start_ref, q_ref, k_ref, v_ref, halo_ref, taps_ref, fwd_ref, inv_ref, conv_ref, gated_ref):
     span = taps_ref.shape[0]
-    sign = signs(span)
     taps = to_freq(fwd_ref[...], taps_ref[...])
     tr, ti = taps[:span], taps[span:]
     halo = jnp.where(start_ref[0] == 1, jnp.zeros_like(halo_ref), halo_ref[...])
@@ -88,7 +82,7 @@
         rows = pl.ds(b * span, span)
         mixed = (k_ref[rows, :].astype(F32) * v_ref[rows, :].astype(F32)).astype(BF16)
         cur = to_freq(fwd_ref[...], mixed)
-        xr, xi = window(prev, cur, sign)
+        xr, xi = window(prev, cur)
         spec = jnp.concatenate([xr * tr - xi * ti, xr * ti + xi * tr], axis=0)
         conv = from_freq(inv_ref[...], spec, 3)
         conv_ref[rows, :] = conv.astype(BF16)
@@ -180,26 +174,30 @@
         ]
 
 
-def project_kernel(place_ref, *refs, operands, products, earlier, carried):
+def project_kernel(place_ref, *refs, operands, products, earlier, carried, joined):
     count = len(operands.arrays)
     blocks, rest = refs[:count], list(refs[count + earlier :])
     values = operands.values(blocks, place_ref)
     if "outer" in products:
         gated_ref = rest.pop(0)
-        outs = [rest.pop() for _ in range(2 * len(values))][::-1]
-        first_core = place_ref[4] == 0
+        other_ref = rest.pop() if joined else None
+        outs = [rest.pop() for _ in range(2 if joined else 4)][::-1]
+        first_core, first_keeps = place_ref[4] == 0, place_ref[5] == 0
         wide = outs[0].shape[1]
         outers = [dot(gated_ref[...], value).astype(BF16) for value in values]
-        if len(outers) == 2:
-            first_keeps = place_ref[5] == 0
-            outers = [
-                jnp.where(first_keeps, outers[0], outers[1]),
-                jnp.where(first_keeps, outers[1], outers[0]),
-            ]
+        outers = [
+            jnp.where(first_keeps, outers[0], outers[1]),
+            jnp.where(first_keeps, outers[1], outers[0]),
+        ]
         for n, outer in enumerate(outers):
             left, right = outer[:, :wide], outer[:, wide:]
-            outs[2 * n][...] = jnp.where(first_core, left, right)
-            outs[2 * n + 1][...] = jnp.where(first_core, right, left)
+            other = jnp.where(first_core, right, left)
+            if joined:
+                outs[n][...] = jnp.where(first_core, left, right)
+                other_ref[:, n * wide : (n + 1) * wide] = other
+            else:
+                outs[2 * n][...] = jnp.where(first_core, left, right)
+                outs[2 * n + 1][...] = other
     if "inner" in products:
         total = rest.pop(0)[...] if carried else None
         for value, weight in zip(values, operands.weight_values(blocks)):
@@ -209,7 +207,7 @@
         rest[0][...] = total
 
 
-def project(place, slots, gated_t, weight, acc, wide, products, earlier, weighted, micros=100):
+def project(place, slots, gated_t, weight, acc, wide, products, earlier, weighted, micros=100, joined=False):
     chans, rows = gated_t.shape
     tile = min(256 if "inner" in products else 512, chans)
     operands = Operands(slots, weight, tile, wide, weighted)
@@ -226,11 +224,13 @@
             specs.append(col)
             arrays.append(acc)
     if "outer" in products:
-        outs += [jax.ShapeDtypeStruct((chans, wide), BF16)] * (2 * len(slots))
-        out_specs += [pl.BlockSpec((tile, wide), lambda i, p: (i, 0))] * (2 * len(slots))
+        sizes = [wide, wide, 2 * wide] if joined else [wide] * 4
+        outs += [jax.ShapeDtypeStruct((chans, size), BF16) for size in sizes]
+        out_specs += [pl.BlockSpec((tile, size), lambda i, p: (i, 0)) for size in sizes]
     return pl.pallas_call(
         functools.partial(
-            project_kernel, operands=operands, products=products, earlier=len(earlier), carried=carried
+            project_kernel, operands=operands, products=products, earlier=len(earlier), carried=carried,
+            joined=joined,
         ),
         grid_spec=pltpu.PrefetchScalarGridSpec(
             num_scalar_prefetch=1,
@@ -252,9 +252,8 @@
     acc_ref, conv_ref, q_ref, k_ref, v_ref, start_ref, before_ref, taps_ref, fwd_ref, inv_ref, lag_ref = refs[
         count : count + 11
     ]
-    gq_ref, gk_ref, gv_ref, first_ref, last_ref, gf_ref = refs[count + 11 :]
+    gq_ref, gk_ref, gv_ref, first_ref, last_ref, *gf_refs = refs[count + 11 :]
     span, chans = taps_ref.shape
-    sign = signs(span)
     taps = to_freq(fwd_ref[...], taps_ref[...])
     tr, ti = taps[:span], taps[span:]
     acc_r = jnp.zeros((span, chans), F32)
@@ -281,35 +280,40 @@
         grad = to_freq(fwd_ref[...], grad_conv)
         mixed = (k_ref[rows, :].astype(F32) * v_ref[rows, :].astype(F32)).astype(BF16)
         cur = to_freq(fwd_ref[...], mixed)
-        xr, xi = window(prev_mixed, cur, sign)
+        xr, xi = window(prev_mixed, cur)
         prev_mixed = cur
         gr, gi = grad[:span], grad[span:]
         acc_r += gr * xr + gi * xi
         acc_i += gr * xi - gi * xr
         if b > 0:
             rows = pl.ds((b - 1) * span, span)
-            back = filtered_back(prev, grad, tr, ti, sign, inv_ref[...])
+            back = filtered_back(prev, grad, tr, ti, inv_ref[...])
             gk_ref[rows, :] = back * v_ref[rows, :].astype(F32)
             gv_ref[rows, :] = back * k_ref[rows, :].astype(F32)
         prev = grad
     part = from_freq(lag_ref[...], jnp.concatenate([acc_r, acc_i], axis=0), 3) * scale
-    wide = gf_ref.shape[2]
-    for n in range(gf_ref.shape[0]):
-        gf_ref[n] = part[:, n * wide : (n + 1) * wide]
-
-
-def filtered_back(cur, later, tr, ti, sign, stack):
-    wr, wi = window(cur, later, sign)
-    return from_freq(stack, jnp.concatenate([wr * tr + wi * ti, wi * tr - wr * ti], axis=0), 2)
+    if operands:
+        even_ref, odd_ref = gf_refs
+        wide = chans // 2
+        first_core = place_ref[4] == 0
+        away = pl.program_id(0) ^ place_ref[8]
+        even_ref[away] = jnp.where(first_core, part[:, :wide], part[:, wide:])
+        odd_ref[away] = jnp.where(first_core, part[:, wide:], part[:, :wide])
+    else:
+        gf_refs[0][...] = part
+
+
+def filtered_back(cur, later, tr, ti, stack):
+    wr, wi = window(cur, later)
+    return from_freq(stack, jnp.concatenate([wr * tr + wi * ti, wi * tr - wr * ti], axis=0), 1)
 
 
 def gradients(
-    place, slots, weight, wide, acc, conv, query, key, value, is_start, before, taps, consts, contexts, scale, earlier
+    place, slots, weight, wide, acc, conv, query, key, value, is_start, before, taps, consts, scale, earlier
 ):
     rows, chans = query.shape
     span = taps.shape[0]
     tile = min(256, chans)
-    own = chans // contexts
     fwd, stacks = consts
     operands = Operands(slots, weight, tile, wide, [held for held, _, _ in slots]) if slots else None
     col = pl.BlockSpec((rows, tile), lambda i, p: (0, i))
@@ -329,15 +333,19 @@
                 col,
                 short,
                 short,
-                pl.BlockSpec((tile // own, span, own), lambda i, p: (i, 0, 0)),
-            ],
+            ]
+            + ([pl.BlockSpec((4, span, tile // 2), lambda i, p: (0, 0, 0))] * 2 if slots else [short]),
         ),
         out_shape=[jax.ShapeDtypeStruct((rows, chans), F32)] * 3
         + [
             jax.ShapeDtypeStruct((span, chans), BF16),
             jax.ShapeDtypeStruct((span, chans), BF16),
-            jax.ShapeDtypeStruct((contexts, span, own), F32),
-        ],
+        ]
+        + (
+            [jax.ShapeDtypeStruct((4, span, tile // 2), F32)] * 2
+            if slots
+            else [jax.ShapeDtypeStruct((span, chans), F32)]
+        ),
         compiler_params=pltpu.CompilerParams(vmem_limit_bytes=VMEM_LIMIT),
         cost_estimate=weight_of(100),
         name="gradients",
@@ -352,7 +360,7 @@
     taps = to_freq(fwd_ref[...], taps_ref[...])
     cur = to_freq(fwd_ref[...], last_ref[...])
     later = to_freq(fwd_ref[...], jnp.where(end_ref[0] == 1, jnp.zeros_like(after_ref), after_ref[...]))
-    back = filtered_back(cur, later, taps[:span], taps[span:], signs(span), inv_ref[...])
+    back = filtered_back(cur, later, taps[:span], taps[span:], inv_ref[...])
     gk_ref[...] = back * v_ref[...].astype(F32)
     gv_ref[...] = back * k_ref[...].astype(F32)
 
@@ -401,7 +409,7 @@
             num_scalar_prefetch=1,
             grid=(rows // tile,),
             in_specs=[block] * len(own_terms)
-            + [pl.BlockSpec((tile, term.shape[1]), lambda i, p: (i, 0)) for term in terms]
+            + [half_spec(term, tile) for term in terms]
             + [ANYWHERE] * len(held),
             out_specs=block,
         ),
@@ -410,7 +418,7 @@
         compiler_params=pltpu.CompilerParams(vmem_limit_bytes=VMEM_LIMIT),
         cost_estimate=weight_of(2),
         name="finish",
-    )(is_early, *own_terms, *terms, *held)
+    )(is_early, *own_terms, *bare(terms), *held)
 
 
 def on_line(pairs, contexts):
@@ -472,6 +480,16 @@
         at, column = at + count, column + wide
 
 
+def half_spec(term, tile):
+    array, at = term if isinstance(term, tuple) else (term, None)
+    wide = array.shape[1] if at is None else array.shape[1] // 2
+    return pl.BlockSpec((tile, wide), lambda i, *_: (i, at or 0))
+
+
+def bare(terms):
+    return [term[0] if isinstance(term, tuple) else term for term in terms]
+
+
 def add_kernel(*refs, groups, across):
     for cols, total in group_sums(refs, groups, across):
         refs[-1][:, cols] = total.astype(BF16)
@@ -486,14 +504,13 @@
     return pl.pallas_call(
         functools.partial(add_kernel, groups=sizes, across=len(across)),
         grid=(rows // tile,),
-        in_specs=[pl.BlockSpec((tile, term.shape[1]), lambda i: (i, 0)) for term in terms]
-        + [ANYWHERE] * len(earlier),
+        in_specs=[half_spec(term, tile) for term in terms] + [ANYWHERE] * len(earlier),
         out_specs=pl.BlockSpec((tile, wide), lambda i: (i, 0)),
         out_shape=jax.ShapeDtypeStruct((rows, wide), BF16),
         compiler_params=pltpu.CompilerParams(vmem_limit_bytes=VMEM_LIMIT),
         cost_estimate=weight_of(micros),
         name="add_blocks",
-    )(*terms, *earlier)
+    )(*bare(terms), *earlier)
 
 
 def body(query, key, value, taps, weight, out_grad, tensors, contexts):
@@ -510,7 +527,11 @@
     is_start = (ctx == 0).astype(jnp.int32).reshape(1)
     is_end = (ctx == contexts - 1).astype(jnp.int32).reshape(1)
 
-    if tensors == 4 and contexts == 8 and chans % 1024 == 0:
+    def complete(first, last, grad_key, grad_value):
+        after_rows = lax.ppermute(first, "context", [(c, (c - 1) % contexts) for c in range(contexts)])
+        return last_rows(is_end, last, after_rows, key, value, taps, grad_key, grad_value, consts)
+
+    if tensors == 4 and contexts == 8 and chans == 1024:
         half = chans // 2
         pieces = [(0, half // 2), (half // 2, half // 4), (3 * half // 4, half // 4)]
         chip, core = ctx // 2, lax.rem(ctx, 2)
@@ -519,7 +540,7 @@
         held = [ten, ten ^ 1, jnp.where(low, 2, 1), jnp.where(low, 3, 0)]
         sides = [(h ^ chip) & 1 for h in held]
         early = jnp.stack(held + [core] + sides[:2] + [edge]).astype(jnp.int32)
-        late = jnp.stack(held + [core] + sides[2:] + [edge]).astype(jnp.int32)
+        late = jnp.stack(held + [core] + sides[2:] + [edge, chip]).astype(jnp.int32)
         is_early = ((chip // 2) == (ten // 2)).astype(jnp.int32).reshape(1)
 
         swap_ends = [(0, 1), (1, 0), (2, 3), (3, 2)]
@@ -556,10 +577,16 @@
                 )
             else:
                 earlier = [] if n == 1 else [gg, own_terms[-1]]
-                outer = project(late, slots, gated_t, weight, None, wide, ("outer",), earlier, [])
-            keep, other_keep, cross, other_cross = outer
-            keeps.append([keep, over(other_keep, 1)])
-            crosses.append([cross, over(other_cross, 1)])
+                outer = project(late, slots, gated_t, weight, None, wide, ("outer",), earlier, [], joined=True)
+            if n == 0:
+                keep, other_keep, cross, other_cross = outer
+                keeps.append([keep, over(other_keep, 1)])
+                crosses.append([cross, over(other_cross, 1)])
+            else:
+                keep, cross, other = outer
+                got = over(other, 1)
+                keeps.append([keep, (got, 0)])
+                crosses.append([cross, (got, 1)])
             if n == 1:
                 first_cross = add_blocks([crosses[0]], [keep], 0.1)
                 keeps[0].append(over(first_cross, 2))
@@ -569,15 +596,20 @@
         first_in = add_blocks([keeps[0]], [])
         last_cross = add_blocks(crosses[1:], [first_in])
         last_over = over(last_cross, 2)
-        grad_query, grad_key, grad_value, first, last, parts = gradients(
+        grad_query, grad_key, grad_value, first, last, even, odd = gradients(
             late, slots[1:], weight, wide, gg, conv, query, key, value, is_start, before, taps, consts,
-            contexts, scale, [last_cross],
+            scale, [last_cross],
         )
         first_over = over(first_in, 4)
         grad_weight = finish(is_early, own_terms, keeps[:1], [first_over], None, 0, scale)
-        last_in = add_blocks(keeps[1:], [first], 1, [last_over])
+        last_in = add_blocks(keeps[1:], [first, first_over], 1, [last_over])
+        last_over_y = over(last_in, 4)
+        got = over(hold(odd, [last_in]), 1)
+        grad_key, grad_value = complete(first, last, grad_key, grad_value)
+        got = hold(got, [last_over_y, grad_weight, grad_key])
+        grad_filter = even[0] + got[0] + sum(over(even[n] + got[n], 2 * n) for n in (1, 2, 3))
         grad_weight = finish(
-            is_early, own_terms, keeps[1:], [last_over, over(last_in, 4)], grad_weight, 1, scale
+            is_early, own_terms, keeps[1:], [last_over, last_over_y], grad_weight, 1, scale
         )
     else:
         conv, gated_t = filtered(is_start, query, key, value, before, taps, consts)
@@ -585,18 +617,14 @@
         gg = lax.dot_general(segment, weight, (((1,), (1,)), ((), ())), preferred_element_type=F32)
         outer = dot(gated_t, segment)
         grad_weight = lax.psum_scatter(outer, "context", scatter_dimension=1, tiled=True) * scale
-        grad_query, grad_key, grad_value, first, last, parts = gradients(
+        grad_query, grad_key, grad_value, first, last, part = gradients(
             jnp.zeros((1,), jnp.int32), None, weight, 0, gg, conv, query, key, value, is_start, before, taps, consts,
-            contexts, scale, [],
+            scale, [],
         )
-
-    after_rows = lax.ppermute(first, "context", [(c, (c - 1) % contexts) for c in range(contexts)])
-    parts = hold(parts, [after_rows])
-    parts = lax.all_to_all(parts, "context", split_axis=0, concat_axis=0, tiled=True)
-    grad_filter = jnp.sum(parts, axis=0)
-    grad_key, grad_value = last_rows(
-        is_end, last, after_rows, key, value, taps, grad_key, grad_value, consts
-    )
+        grad_filter = lax.psum_scatter(part, "context", scatter_dimension=1, tiled=True)
+        grad_key, grad_value = complete(first, last, grad_key, grad_value)
+
+
     return (grad_query, grad_key, grad_value, grad_filter, grad_weight)
 
 

time: 212 us -> 202 us (0.953)
  waiting for transfers between devices: 31.3 us -> 18.3 us
  local copies, waits for them, and re-layouts: 13.8 us -> 17.3 us
    all_to_all x1 -> x0, waiting for transfers between devices: 8.28 us -> none  [body(): lax.all_to_all(parts, 'context', split_axis=0, concat_axis=0, tiled=True)]
    ppermute x14 -> x16, starting transfers between devices: 10.1 us -> 14.9 us  [swap(): lax.ppermute(value, 'context', [(c, c ^ bit) for c in range(contexts)])]
    ppermute x14 -> x16, waiting for transfers between devices: 9.43 us -> 4.74 us  [swap(): lax.ppermute(value, 'context', [(c, c ^ bit) for c in range(contexts)])]
    all_to_all x1 -> x0, starting transfers between devices: 4.15 us -> none  [body(): lax.all_to_all(parts, 'context', split_axis=0, concat_axis=0, tiled=True)]
    unnamed x76 -> x80, local copies, waits for them, and re-layouts: 13.6 us -> 17.1 us
    add x0 -> x2, other arithmetic: none -> 2.63 us  [the longest x1 1.53 us: body(): even[0] + got[0] + sum((over(even[n] + got[n], 2 * n) for n in (1, 2, 3)))]
  transfers between devices with their start and end apart: 26 -> 27, of which waited for: 5 -> 4; matrix products, arithmetic and copies ran while one was open for 1% -> 1% of each run, Pallas kernels for 39% -> 41%
where the time goes in v2:
time: 202 us; the launch traced here: 201 us
  Pallas kernels  83.6 us (41%)
  starting transfers between devices  77.3 us (38%)
  waiting for transfers between devices  18.3 us (9%)
  local copies, waits for them, and re-layouts  17.3 us (9%)
  other arithmetic  3.73 us (2%)
    ppermute x9, starting transfers between devices, send_line(): return lax.ppermute(value, ('tensor', 'context'), on_line(pairs, contexts))  62.3 us
    pallas_call x6, Pallas kernels, project(): pl.pallas_call(functools.partial(project_kernel, operands=operands, produ...  43.5 us
    unnamed x80, local copies, waits for them, and re-layouts  17.1 us
    ppermute x16, starting transfers between devices, swap(): lax.ppermute(value, 'context', [(c, c ^ bit) for c in range(contexts)])  14.9 us
    pallas_call x1, Pallas kernels, gradients(): pl.pallas_call(functools.partial(grad_kernel, operands=operands, earlier=...  13.9 us
    pallas_call x1, Pallas kernels, filtered(): pl.pallas_call(conv_kernel, grid=(chans // tile,), in_specs=[SCALAR, col,...  8.76 us
    ppermute x9, waiting for transfers between devices, send_line(): return lax.ppermute(value, ('tensor', 'context'), on_line(pairs, contexts))  6.99 us
    ppermute x1, waiting for transfers between devices, body(): lax.ppermute(last_mixed, 'context', [(c, (c + 1) % contexts) for c in ran...  6.56 us
  transfers between devices with their start and end apart: 27, of which 4 were waited for; matrix products, arithmetic and copies ran while one was open for 1% of the time, Pallas kernels for 41%

profile of v2, /device:TPU:0, one launch (start us, length us, event | category | flops | bytes accessed | tf_op | source)
XLA Modules:
  0.0 201.3 jit_solution(8166828341591079803)
XLA Ops:
  0.6 2.0 %collective-permute-start.1 = (bf16[1024,1024]{1,0:T(8,128)(2,1)}, bf16[1024,1024]{1,0:T(8,128)(2,1)}, u32[]{:S(2)}, u32[]{:S(2)}) collective-permute-start(bf16[1024,1024]{1,0:T(8,128)(2,1)} %refs_1_.1), channel_id=1, source_target_pairs={{8,16},{9,17},{10,18},{11,19},{12,20},{13,21},{14,22},{15,23},{16,... | collective-permute-start | bytes 6291464 | tf_op jit(solution)/shard_map/ppermute | solution.py:429
  2.6 4.6 %collective-permute-start = (bf16[1024,1024]{1,0:T(8,128)(2,1)}, bf16[1024,1024]{1,0:T(8,128)(2,1)}, u32[]{:S(2)}, u32[]{:S(2)}) collective-permute-start(bf16[1024,1024]{1,0:T(8,128)(2,1)} %refs_1_.1), channel_id=1, source_target_pairs={{0,8},{1,9},{2,10},{3,11},{4,12},{5,13},{6,14},{7,15},{8,0},{9,1},... | collective-permute-start | bytes 6291464 | tf_op jit(solution)/shard_map/ppermute | solution.py:429
  7.2 1.1 multiply_convert_fusion
  8.4 0.1 stack.61.place_ref
  8.5 6.6 %collective-permute-done.2.halo_ref.refs_13_ = bf16[128,1024]{1,0:T(8,128)(2,1)S(1)} collective-permute-done((bf16[128,1024]{1,0:T(8,128)(2,1)S(1)}, bf16[128,1024]{1,0:T(8,128)(2,1)S(1)}, u32[]{:S(2)}, u32[]{:S(2)}) %collective-permute-start.2) | collective-permute-done | bytes 262176 | tf_op jit(solution)/shard_map/ppermute | solution.py:526
  15.1 1.0 copy-done.8
  16.1 0.9 copy-done.24
  17.0 0.9 copy-done.38
  17.9 8.8 %filtered.1 = (bf16[1024,1024]{1,0:T(8,128)(2,1)S(1)}, bf16[1024,1024]{1,0:T(8,128)(2,1)S(1)}) custom-call(s32[1]{0:T(128)} %bitcast.11.start_ref.refs_12_, bf16[1024,1024]{1,0:T(8,128)(2,1)} %refs_9_.3, bf16[1024,1024]{1,0:T(8,128)(2,1)} %k_ref.3, bf16[1024,1024]{1,0:T(8,128)(2,1)} %v_ref.3, bf16[128,1024]{1,0:T(8,128)(2,1)S(1)} %collective-permute-done.2.halo_ref.refs_13_, ...), custom_call_target="tpu_custom_call" | custom-call | flops 1048576 | bytes 370000000 | tf_op jit(solution)/shard_map/filtered/pallas_call | solution.py:101
  26.7 1.3 copy-done.2
  28.0 1.4 copy-done.12
  29.4 23.8 %collective-permute-start.5 = (bf16[1024,1024]{1,0:T(8,128)(2,1)}, bf16[1024,1024]{1,0:T(8,128)(2,1)S(1)}, u32[]{:S(2)}, u32[]{:S(2)}) collective-permute-start(bf16[1024,1024]{1,0:T(8,128)(2,1)} %collective-permute-done.1.refs_8_.refs_0_.refs_2_), channel_id=1, source_target_pairs={{0,8},{1,9},{2,10},{3,11},{4,12},{5,13},{6,14},{7,15},{8,0},{9,1},... | collective-permute-start | bytes 6291464 | tf_op jit(solution)/shard_map/ppermute | solution.py:429
  53.2 14.0 %project.6 = (f32[1024,1024]{1,0:T(8,128)}, bf16[1024,512]{1,0:T(8,128)(2,1)S(1)}, bf16[1024,512]{1,0:T(8,128)(2,1)S(1)}, bf16[1024,512]{1,0:T(8,128)(2,1)S(1)}, bf16[1024,512]{1,0:T(8,128)(2,1)}) custom-call(s32[8]{0:T(128)S(1)} %stack.61.place_ref, bf16[1024,1024]{1,0:T(8,128)(2,1)} %refs_1_.1, bf16[1024,1024]{1,0:T(8,128)(2,1)} %refs_1_.1, ...), custom_call_target="tpu_custom_call" | custom-call | flops 1048576 | bytes 370000000 | tf_op jit(solution)/shard_map/project/pallas_call | solution.py:230
  67.3 1.0 copy-done.28
  68.3 1.0 copy-done.39
  69.3 3.8 %cut.1 = (bf16[1024,512]{1,0:T(8,128)(2,1)}, bf16[1024,256]{1,0:T(8,128)(2,1)}, bf16[1024,256]{1,0:T(8,128)(2,1)}) custom-call(bf16[1024,1024]{1,0:T(8,128)(2,1)} %collective-permute-done.refs_2_.refs_3_.refs_0_, f32[1024,1024]{1,0:T(8,128)} %get-tuple-element.36.refs_1_.refs_7_), custom_call_target="tpu_custom_call" | custom-call | flops 1048576 | bytes 370000000 | tf_op jit(solution)/shard_map/cut/pallas_call | solution.py:447
  73.1 1.6 collective-permute-start.9
  74.7 0.5 collective-permute-start.11
  75.2 1.2 copy-done.29
  76.4 2.2 %add_blocks.6.refs_6_ = bf16[1024,512]{1,0:T(8,128)(2,1)} custom-call(bf16[1024,512]{1,0:T(8,128)(2,1)S(1)} %copy-done.29, bf16[1024,512]{1,0:T(8,128)(2,1)} %collective-permute-done.12.refs_1_), custom_call_target="tpu_custom_call" | custom-call | flops 1048576 | bytes 3700000 | tf_op jit(solution)/shard_map/add_blocks/pallas_call | solution.py:504
  78.6 1.5 collective-permute-start.13
  80.1 22.1 %collective-permute-start.10 = (bf16[1024,512]{1,0:T(8,128)(2,1)}, bf16[1024,512]{1,0:T(8,128)(2,1)}, u32[]{:S(2)}, u32[]{:S(2)}) collective-permute-start(bf16[1024,512]{1,0:T(8,128)(2,1)} %collective-permute-done.9.refs_4_.refs_6_), channel_id=1, source_target_pairs={{0,8},{1,9},{2,10},{3,11},{4,12},{5,13},{6,14},{7,15},{8,0},{9,1},... | collective-permute-start | bytes 3145736 | tf_op jit(solution)/shard_map/ppermute | solution.py:429
  102.2 1.5 collective-permute-start.6
  103.7 0.1 stack.58.place_ref
  103.8 0.9 collective-permute-start.3
  104.6 7.9 %project.8.refs_3_.refs_12_ = f32[1024,1024]{1,0:T(8,128)} custom-call(s32[9]{0:T(128)S(1)} %stack.58.place_ref, bf16[1024,1024]{1,0:T(8,128)(2,1)} %collective-permute-done.1.refs_8_.refs_0_.refs_2_, bf16[1024,1024]{1,0:T(8,128)(2,1)S(1)} %collective-permute-done.5.refs_1_.refs_3_, bf16[1024,1024]{1,0:T(8,128)(2,1)} %collective-permute-done.1.refs_8_.refs_0_.refs_2_, ...), custom_call_target="tpu_custom_call" | custom-call | flops 1048576 | bytes 370000000 | tf_op jit(solution)/shard_map/project/pallas_call | solution.py:230
  112.5 1.7 add_blocks.7.refs_10_
  114.3 1.6 collective-permute-start.15
  115.9 3.7 %collective-permute-start.7 = (bf16[1024,256]{1,0:T(8,128)(2,1)}, bf16[1024,256]{1,0:T(8,128)(2,1)S(1)}, u32[]{:S(2)}, u32[]{:S(2)}) collective-permute-start(bf16[1024,256]{1,0:T(8,128)(2,1)} %collective-permute-done.6.refs_4_.refs_6_.refs_0_.refs_2_), channel_id=1, source_target_pairs={{0,8},{1,9},{2,10},{3,11},{4,12},{5,13},{6,14},{7,15},{8,0},{9,1},... | collective-permute-start | bytes 1572872 | tf_op jit(solution)/shard_map/ppermute | solution.py:429
  119.6 7.0 %collective-permute-done.10.refs_5_.refs_7_ = bf16[1024,512]{1,0:T(8,128)(2,1)} collective-permute-done((bf16[1024,512]{1,0:T(8,128)(2,1)}, bf16[1024,512]{1,0:T(8,128)(2,1)}, u32[]{:S(2)}, u32[]{:S(2)}) %collective-permute-start.10) | collective-permute-done | bytes 1048608 | tf_op jit(solution)/shard_map/ppermute | solution.py:429
  126.5 9.5 %project.9 = (f32[1024,1024]{1,0:T(8,128)}, bf16[1024,256]{1,0:T(8,128)(2,1)S(1)}, bf16[1024,256]{1,0:T(8,128)(2,1)S(1)}, bf16[1024,256]{1,0:T(8,128)(2,1)S(1)}, bf16[1024,256]{1,0:T(8,128)(2,1)S(1)}) custom-call(s32[9]{0:T(128)S(1)} %stack.58.place_ref, bf16[1024,1024]{1,0:T(8,128)(2,1)} %collective-permute-done.1.refs_8_.refs_0_.refs_2_, ...), custom_call_target="tpu_custom_call" | custom-call | flops 1048576 | bytes 370000000 | tf_op jit(solution)/shard_map/project/pallas_call | solution.py:230
  136.1 2.1 %collective-permute-start.4 = (bf16[1024,256]{1,0:T(8,128)(2,1)S(1)}, bf16[1024,256]{1,0:T(8,128)(2,1)S(1)}, u32[]{:S(2)}, u32[]{:S(2)}) collective-permute-start(bf16[1024,256]{1,0:T(8,128)(2,1)S(1)} %collective-permute-done.3.refs_4_.refs_6_.refs_0_.refs_2_), channel_id=1, source_target_pairs={{0,8},{1,9},{2,10},{3,11},{4,12},{5,13},{6,14},{7,15},{8,0},{9,1},... | collective-permute-start | bytes 1572872 | tf_op jit(solution)/shard_map/ppermute | solution.py:429
  138.2 3.8 %project.7 = (bf16[1024,128]{1,0:T(8,128)(2,1)S(1)}, bf16[1024,128]{1,0:T(8,128)(2,1)S(1)}, bf16[1024,256]{1,0:T(8,128)(2,1)S(1)}) custom-call(s32[9]{0:T(128)S(1)} %stack.58.place_ref, bf16[1024,1024]{1,0:T(8,128)(2,1)} %collective-permute-done.1.refs_8_.refs_0_.refs_2_, bf16[1024,1024]{1,0:T(8,128)(2,1)} %copy-done, ...), custom_call_target="tpu_custom_call" | custom-call | flops 1048576 | bytes 370000000 | tf_op jit(solution)/shard_map/project/pallas_call | solution.py:230
  142.0 0.2 collective-permute-start.8
  142.2 0.4 collective-permute-start.17
  142.6 0.1 add_blocks.8.refs_6_
  142.7 1.5 collective-permute-start.18
  144.3 4.7 %project.10.refs_8_.refs_7_ = f32[1024,1024]{1,0:T(8,128)S(1)} custom-call(s32[9]{0:T(128)S(1)} %stack.58.place_ref, bf16[1024,256]{1,0:T(8,128)(2,1)} %collective-permute-done.6.refs_4_.refs_6_.refs_0_.refs_2_, bf16[1024,256]{1,0:T(8,128)(2,1)S(1)} %collective-permute-done.7.refs_5_.refs_7_.refs_1_.refs_3_, ...), custom_call_target="tpu_custom_call" | custom-call | flops 1048576 | bytes 370000 | tf_op jit(solution)/shard_map/project/pallas_call | solution.py:230
  149.0 2.0 copy-done.1
  151.0 3.6 %project.11 = (bf16[1024,128]{1,0:T(8,128)(2,1)S(1)}, bf16[1024,128]{1,0:T(8,128)(2,1)S(1)}, bf16[1024,256]{1,0:T(8,128)(2,1)S(1)}) custom-call(s32[9]{0:T(128)S(1)} %stack.58.place_ref, bf16[1024,1024]{1,0:T(8,128)(2,1)} %collective-permute-done.1.refs_8_.refs_0_.refs_2_, bf16[1024,1024]{1,0:T(8,128)(2,1)} %copy-done, ...), custom_call_target="tpu_custom_call" | custom-call | flops 1048576 | bytes 370000000 | tf_op jit(solution)/shard_map/project/pallas_call | solution.py:230
  154.8 2.0 collective-permute-done.18.refs_2_.refs_6_
  156.9 0.2 add_blocks.9.refs_4_
  157.1 1.6 collective-permute-start.21
  158.7 0.3 add_blocks.10.refs_6_
  159.0 1.6 collective-permute-start.20
  160.6 13.9 %gradients.1 = (f32[1024,1024]{1,0:T(8,128)}, f32[1024,1024]{1,0:T(8,128)}, f32[1024,1024]{1,0:T(8,128)}, bf16[128,1024]{1,0:T(8,128)(2,1)}, bf16[128,1024]{1,0:...) custom-call(s32[9]{0:T(128)S(1)} %stack.58.place_ref, ...), custom_call_target="tpu_custom_call" | custom-call | flops 1048576 | bytes 370000000 | tf_op jit(solution)/shard_map/gradients/pallas_call | solution.py:322
  174.6 1.1 add_blocks.11.refs_1_
  175.7 0.5 collective-permute-start.23
  176.2 0.6 collective-permute-start.22
  176.8 1.0 copy-done.17
  177.8 1.0 copy-done.19
  178.9 1.0 copy-done.23
  179.9 2.7 %finish.2.refs_2_.refs_10_ = f32[1024,512]{1,0:T(8,128)} custom-call(s32[1]{0:T(128)} %bitcast.13.early_ref, bf16[1024,512]{1,0:T(8,128)(2,1)S(1)} %get-tuple-element.42.refs_0_, bf16[1024,512]{1,0:T(8,128)(2,1)} %collective-permute-done.11.refs_1_, bf16[1024,512]{1,0:T(8,128)(2,1)} %collective-permute-done.13.refs_2_, bf16[1024,512]{1,0:T(8,128)(2,1)} %copy-done.5, ...), custom_call_target="tpu_custom_call" | custom-call | flops 1048576 | bytes 7400000 | tf_op jit(solution)/shard_map/finish/pallas_call | solution.py:406
  182.6 0.3 copy-done.4
  183.0 2.9 %last_rows.1 = (f32[1024,1024]{1,0:T(8,128)}, f32[1024,1024]{1,0:T(8,128)}) custom-call(s32[1]{0:T(128)} %bitcast.12.end_ref, bf16[128,1024]{1,0:T(8,128)(2,1)S(1)} %copy-done.34, bf16[128,1024]{1,0:T(8,128)(2,1)} %collective-permute-done.19.after_ref, bf16[1024,1024]{1,0:T(8,128)(2,1)S(1)} %copy-done.3, ...), custom_call_target="tpu_custom_call", output_to_operand_aliasing={{0}: (8, {}), {1}: (9, {})} | custom-call | flops 1048576 | bytes 7400000 | tf_op jit(solution)/shard_map/last_rows/pallas_call | solution.py:377
  185.8 2.7 %collective-permute-done.23.refs_1_.refs_9_ = bf16[1024,256]{1,0:T(8,128)(2,1)S(1)} collective-permute-done((bf16[1024,256]{1,0:T(8,128)(2,1)}, bf16[1024,256]{1,0:T(8,128)(2,1)S(1)}, u32[]{:S(2)}, u32[]{:S(2)}) %collective-permute-start.23) | collective-permute-done | bytes 524320 | tf_op jit(solution)/shard_map/ppermute | solution.py:433
  188.5 0.8 copy-done.10
  189.3 1.1 fusion.1
  190.4 4.2 %collective-permute-start.26 = (f32[128,128]{1,0:T(8,128)S(1)}, f32[128,128]{1,0:T(8,128)S(1)}, u32[]{:S(2)}, u32[]{:S(2)}) collective-permute-start(f32[128,128]{1,0:T(8,128)S(1)} %get-tuple-element.66), channel_id=1, source_target_pairs={{0,6},{1,7},{2,4},{3,5},{4,2},{5,3},{6,0},{7,1},{8,14},{9,15},{10,... | collective-permute-start | bytes 196616 | tf_op jit(solution)/shard_map/ppermute | solution.py:433
  194.6 0.7 collective-permute-start.25
  195.3 1.0 copy-done.11
  196.3 0.9 copy-done.31
  197.3 2.5 %finish.3 = f32[1024,512]{1,0:T(8,128)} custom-call(s32[1]{0:T(128)} %bitcast.13.early_ref, bf16[1024,512]{1,0:T(8,128)(2,1)S(1)} %get-tuple-element.42.refs_0_, bf16[1024,512]{1,0:T(8,128)(2,1)} %collective-permute-done.11.refs_1_, bf16[1024,512]{1,0:T(8,128)(2,1)} %collective-permute-done.13.refs_2_, ...), custom_call_target="tpu_custom_call", output_to_operand_aliasing={{}: (11, {})} | custom-call | flops 1048576 | bytes 7400000 | tf_op jit(solution)/shard_map/finish/pallas_call | solution.py:406
  199.8 1.5 fusion.4
  (95 shorter events, 0.5 us)
Async XLA Ops:
  0.6 28.8 %collective-permute-start.1 = (bf16[1024,1024]{1,0:T(8,128)(2,1)}, bf16[1024,1024]{1,0:T(8,128)(2,1)}, u32[]{:S(2)}, u32[]{:S(2)}) collective-permute-start(bf16[1024,1024]{1,0:T(8,128)(2,1)} %refs_1_.1), channel_id=1, source_target_pairs={{8,16},{9,17},{10,18},{11,19},{12,20},{13,21},{14,22},{15,23},{16,... | collective-permute-start | bytes 6291464 | tf_op jit(solution)/shard_map/ppermute | solution.py:429
  2.6 50.6 %collective-permute-start = (bf16[1024,1024]{1,0:T(8,128)(2,1)}, bf16[1024,1024]{1,0:T(8,128)(2,1)}, u32[]{:S(2)}, u32[]{:S(2)}) collective-permute-start(bf16[1024,1024]{1,0:T(8,128)(2,1)} %refs_1_.1), channel_id=1, source_target_pairs={{0,8},{1,9},{2,10},{3,11},{4,12},{5,13},{6,14},{7,15},{8,0},{9,1},... | collective-permute-start | bytes 6291464 | tf_op jit(solution)/shard_map/ppermute | solution.py:429
  8.3 6.7 %collective-permute-start.2 = (bf16[128,1024]{1,0:T(8,128)(2,1)S(1)}, bf16[128,1024]{1,0:T(8,128)(2,1)S(1)}, u32[]{:S(2)}, u32[]{:S(2)}) collective-permute-start(bf16[128,1024]{1,0:T(8,128)(2,1)S(1)} %multiply_convert_fusion), channel_id=1, source_target_pairs={{0,1},{1,2},{2,3},{3,4},{4,5},{5,6},{6,7},{7,0},{8,9},{9,10},{10,1... | collective-permute-start | bytes 786440 | tf_op jit(solution)/shard_map/ppermute | solution.py:526
  15.1 11.6 %copy-start.26 = (bf16[128,1024]{1,0:T(8,128)(2,1)}, bf16[128,1024]{1,0:T(8,128)(2,1)S(1)}, u32[]{:S(2)}) copy-start(bf16[128,1024]{1,0:T(8,128)(2,1)S(1)} %collective-permute-done.2.halo_ref.refs_13_) | copy-start | bytes 786436
  15.1 1.0 copy-start.8
  26.7 1.3 copy-start.2
  28.0 1.4 copy-start.12
  29.4 74.3 %collective-permute-start.5 = (bf16[1024,1024]{1,0:T(8,128)(2,1)}, bf16[1024,1024]{1,0:T(8,128)(2,1)S(1)}, u32[]{:S(2)}, u32[]{:S(2)}) collective-permute-start(bf16[1024,1024]{1,0:T(8,128)(2,1)} %collective-permute-done.1.refs_8_.refs_0_.refs_2_), channel_id=1, source_target_pairs={{0,8},{1,9},{2,10},{3,11},{4,12},{5,13},{6,14},{7,15},{8,0},{9,1},... | collective-permute-start | bytes 6291464 | tf_op jit(solution)/shard_map/ppermute | solution.py:429
  67.3 1.0 copy-start.28
  68.3 1.0 copy-start.39
  69.3 5.9 %collective-permute-start.12 = (bf16[1024,512]{1,0:T(8,128)(2,1)}, bf16[1024,512]{1,0:T(8,128)(2,1)}, u32[]{:S(2)}, u32[]{:S(2)}) collective-permute-start(bf16[1024,512]{1,0:T(8,128)(2,1)} %get-tuple-element.45), channel_id=1, source_target_pairs={{0,1},{1,0},{2,3},{3,2},{4,5},{5,4},{6,7},{7,6},{8,9},{9,8},{10,11... | collective-permute-start | bytes 3145736 | tf_op jit(solution)/shard_map/ppermute | solution.py:433
  73.1 7.0 %collective-permute-start.9 = (bf16[1024,512]{1,0:T(8,128)(2,1)}, bf16[1024,512]{1,0:T(8,128)(2,1)}, u32[]{:S(2)}, u32[]{:S(2)}) collective-permute-start(bf16[1024,512]{1,0:T(8,128)(2,1)} %get-tuple-element.41), channel_id=1, source_target_pairs={{8,16},{9,17},{10,18},{11,19},{12,20},{13,21},{14,22},{15,23},{16,... | collective-permute-start | bytes 3145736 | tf_op jit(solution)/shard_map/ppermute | solution.py:429
  74.7 37.8 %collective-permute-start.11 = (bf16[1024,512]{1,0:T(8,128)(2,1)}, bf16[1024,512]{1,0:T(8,128)(2,1)}, u32[]{:S(2)}, u32[]{:S(2)}) collective-permute-start(bf16[1024,512]{1,0:T(8,128)(2,1)} %copy-done.39), channel_id=1, source_target_pairs={{0,1},{1,0},{2,3},{3,2},{4,5},{5,4},{6,7},{7,6},{8,9},{9,8},{10,11... | collective-permute-start | bytes 3145736 | tf_op jit(solution)/shard_map/ppermute | solution.py:433
  75.2 1.2 copy-start.29
  78.6 33.9 %collective-permute-start.13 = (bf16[1024,512]{1,0:T(8,128)(2,1)}, bf16[1024,512]{1,0:T(8,128)(2,1)}, u32[]{:S(2)}, u32[]{:S(2)}) collective-permute-start(bf16[1024,512]{1,0:T(8,128)(2,1)} %add_blocks.6.refs_6_), channel_id=1, source_target_pairs={{0,2},{1,3},{2,0},{3,1},{4,6},{5,7},{6,4},{7,5},{8,10},{9,11},{10,... | collective-permute-start | bytes 3145736 | tf_op jit(solution)/shard_map/ppermute | solution.py:433
  80.1 46.5 %collective-permute-start.10 = (bf16[1024,512]{1,0:T(8,128)(2,1)}, bf16[1024,512]{1,0:T(8,128)(2,1)}, u32[]{:S(2)}, u32[]{:S(2)}) collective-permute-start(bf16[1024,512]{1,0:T(8,128)(2,1)} %collective-permute-done.9.refs_4_.refs_6_), channel_id=1, source_target_pairs={{0,8},{1,9},{2,10},{3,11},{4,12},{5,13},{6,14},{7,15},{8,0},{9,1},... | collective-permute-start | bytes 3145736 | tf_op jit(solution)/shard_map/ppermute | solution.py:429
  102.2 13.6 %collective-permute-start.6 = (bf16[1024,256]{1,0:T(8,128)(2,1)}, bf16[1024,256]{1,0:T(8,128)(2,1)}, u32[]{:S(2)}, u32[]{:S(2)}) collective-permute-start(bf16[1024,256]{1,0:T(8,128)(2,1)} %get-tuple-element.38), channel_id=1, source_target_pairs={{8,16},{9,17},{10,18},{11,19},{12,20},{13,21},{14,22},{15,23},{16,... | collective-permute-start | bytes 1572872 | tf_op jit(solution)/shard_map/ppermute | solution.py:429
  103.8 8.8 %copy-start = (bf16[1024,1024]{1,0:T(8,128)(2,1)}, bf16[1024,1024]{1,0:T(8,128)(2,1)S(1)}, u32[]{:S(2)}) copy-start(bf16[1024,1024]{1,0:T(8,128)(2,1)S(1)} %collective-permute-done.5.refs_1_.refs_3_) | copy-start | bytes 6291460
  103.8 32.3 %collective-permute-start.3 = (bf16[1024,256]{1,0:T(8,128)(2,1)}, bf16[1024,256]{1,0:T(8,128)(2,1)S(1)}, u32[]{:S(2)}, u32[]{:S(2)}) collective-permute-start(bf16[1024,256]{1,0:T(8,128)(2,1)} %get-tuple-element.37), channel_id=1, source_target_pairs={{8,16},{9,17},{10,18},{11,19},{12,20},{13,21},{14,22},{15,23},{16,... | collective-permute-start | bytes 1572872 | tf_op jit(solution)/shard_map/ppermute | solution.py:429
  114.3 36.8 %collective-permute-start.15 = (bf16[1024,512]{1,0:T(8,128)(2,1)S(1)}, bf16[1024,512]{1,0:T(8,128)(2,1)S(1)}, u32[]{:S(2)}, u32[]{:S(2)}) collective-permute-start(bf16[1024,512]{1,0:T(8,128)(2,1)S(1)} %add_blocks.7.refs_10_), channel_id=1, source_target_pairs={{0,4},{1,5},{2,6},{3,7},{4,0},{5,1},{6,2},{7,3},{8,12},{9,13},{10,... | collective-permute-start | bytes 3145736 | tf_op jit(solution)/shard_map/ppermute | solution.py:433
  115.9 22.3 %collective-permute-start.7 = (bf16[1024,256]{1,0:T(8,128)(2,1)}, bf16[1024,256]{1,0:T(8,128)(2,1)S(1)}, u32[]{:S(2)}, u32[]{:S(2)}) collective-permute-start(bf16[1024,256]{1,0:T(8,128)(2,1)} %collective-permute-done.6.refs_4_.refs_6_.refs_0_.refs_2_), channel_id=1, source_target_pairs={{0,8},{1,9},{2,10},{3,11},{4,12},{5,13},{6,14},{7,15},{8,0},{9,1},... | collective-permute-start | bytes 1572872 | tf_op jit(solution)/shard_map/ppermute | solution.py:429
  136.0 20.8 %copy-start.14 = (bf16[1024,256]{1,0:T(8,128)(2,1)}, bf16[1024,256]{1,0:T(8,128)(2,1)S(1)}, u32[]{:S(2)}) copy-start(bf16[1024,256]{1,0:T(8,128)(2,1)S(1)} %get-tuple-element.52.refs_0_.refs_4_) | copy-start | bytes 1572868
  136.0 6.6 %collective-permute-start.14 = (bf16[1024,256]{1,0:T(8,128)(2,1)S(1)}, bf16[1024,256]{1,0:T(8,128)(2,1)S(1)}, u32[]{:S(2)}, u32[]{:S(2)}) collective-permute-start(bf16[1024,256]{1,0:T(8,128)(2,1)S(1)} %get-tuple-element.47), channel_id=1, source_target_pairs={{0,1},{1,0},{2,3},{3,2},{4,5},{5,4},{6,7},{7,6},{8,9},{9,8},{10,11... | collective-permute-start | bytes 1572872 | tf_op jit(solution)/shard_map/ppermute | solution.py:433
  136.1 14.9 %collective-permute-start.4 = (bf16[1024,256]{1,0:T(8,128)(2,1)S(1)}, bf16[1024,256]{1,0:T(8,128)(2,1)S(1)}, u32[]{:S(2)}, u32[]{:S(2)}) collective-permute-start(bf16[1024,256]{1,0:T(8,128)(2,1)S(1)} %collective-permute-done.3.refs_4_.refs_6_.refs_0_.refs_2_), channel_id=1, source_target_pairs={{0,8},{1,9},{2,10},{3,11},{4,12},{5,13},{6,14},{7,15},{8,0},{9,1},... | collective-permute-start | bytes 1572872 | tf_op jit(solution)/shard_map/ppermute | solution.py:429
  142.0 16.7 %collective-permute-start.8 = (bf16[1024,256]{1,0:T(8,128)(2,1)S(1)}, bf16[1024,256]{1,0:T(8,128)(2,1)S(1)}, u32[]{:S(2)}, u32[]{:S(2)}) collective-permute-start(bf16[1024,256]{1,0:T(8,128)(2,1)S(1)} %get-tuple-element.40), channel_id=1, source_target_pairs={{0,1},{1,0},{2,3},{3,2},{4,5},{5,4},{6,7},{7,6},{8,9},{9,8},{10,11... | collective-permute-start | bytes 1572872 | tf_op jit(solution)/shard_map/ppermute | solution.py:433
  142.2 12.5 %collective-permute-start.17 = (bf16[1024,256]{1,0:T(8,128)(2,1)S(1)}, bf16[1024,256]{1,0:T(8,128)(2,1)S(1)}, u32[]{:S(2)}, u32[]{:S(2)}) collective-permute-start(bf16[1024,256]{1,0:T(8,128)(2,1)S(1)} %get-tuple-element.53), channel_id=1, source_target_pairs={{0,1},{1,0},{2,3},{3,2},{4,5},{5,4},{6,7},{7,6},{8,9},{9,8},{10,11... | collective-permute-start | bytes 1572872 | tf_op jit(solution)/shard_map/ppermute | solution.py:433
  142.7 14.0 %collective-permute-start.18 = (bf16[1024,256]{1,0:T(8,128)(2,1)S(1)}, bf16[1024,256]{1,0:T(8,128)(2,1)S(1)}, u32[]{:S(2)}, u32[]{:S(2)}) collective-permute-start(bf16[1024,256]{1,0:T(8,128)(2,1)S(1)} %add_blocks.8.refs_6_), channel_id=1, source_target_pairs={{0,2},{1,3},{2,0},{3,1},{4,6},{5,7},{6,4},{7,5},{8,10},{9,11},{10,... | collective-permute-start | bytes 1572872 | tf_op jit(solution)/shard_map/ppermute | solution.py:433
  149.0 2.0 copy-start.1
  151.0 3.6 %copy-start.5 = (bf16[1024,512]{1,0:T(8,128)(2,1)}, bf16[1024,512]{1,0:T(8,128)(2,1)S(1)}, u32[]{:S(2)}) copy-start(bf16[1024,512]{1,0:T(8,128)(2,1)S(1)} %collective-permute-done.15.refs_9_.refs_3_) | copy-start | bytes 3145732
  154.7 19.9 %copy-start.30 = (bf16[1024,128]{1,0:T(8,128)(2,1)}, bf16[1024,128]{1,0:T(8,128)(2,1)S(1)}, u32[]{:S(2)}) copy-start(bf16[1024,128]{1,0:T(8,128)(2,1)S(1)} %get-tuple-element.64.refs_2_.refs_6_) | copy-start | bytes 786436
  154.7 4.0 %collective-permute-start.16 = (bf16[1024,256]{1,0:T(8,128)(2,1)S(1)}, bf16[1024,256]{1,0:T(8,128)(2,1)S(1)}, u32[]{:S(2)}, u32[]{:S(2)}) collective-permute-start(bf16[1024,256]{1,0:T(8,128)(2,1)S(1)} %get-tuple-element.51), channel_id=1, source_target_pairs={{0,1},{1,0},{2,3},{3,2},{4,5},{5,4},{6,7},{7,6},{8,9},{9,8},{10,11... | collective-permute-start | bytes 1572872 | tf_op jit(solution)/shard_map/ppermute | solution.py:433
  154.8 4.2 %copy-start.16 = (bf16[1024,256]{1,0:T(8,128)(2,1)}, bf16[1024,256]{1,0:T(8,128)(2,1)S(1)}, u32[]{:S(2)}) copy-start(bf16[1024,256]{1,0:T(8,128)(2,1)S(1)} %collective-permute-done.17.refs_1_.refs_5_) | copy-start | bytes 1572868
  156.8 2.2 %copy-start.18 = (bf16[1024,256]{1,0:T(8,128)(2,1)}, bf16[1024,256]{1,0:T(8,128)(2,1)S(1)}, u32[]{:S(2)}) copy-start(bf16[1024,256]{1,0:T(8,128)(2,1)S(1)} %collective-permute-done.18.refs_2_.refs_6_) | copy-start | bytes 1572868
  156.8 3.8 %copy-start.9 = (bf16[128,1024]{1,0:T(8,128)(2,1)S(1)}, bf16[128,1024]{1,0:T(8,128)(2,1)}, u32[]{:S(2)}) copy-start(bf16[128,1024]{1,0:T(8,128)(2,1)} %taps_ref.3) | copy-start | bytes 786436
  156.8 3.8 %copy-start.13 = (bf16[1024,1024]{1,0:T(8,128)(2,1)S(1)}, bf16[1024,1024]{1,0:T(8,128)(2,1)}, u32[]{:S(2)}) copy-start(bf16[1024,1024]{1,0:T(8,128)(2,1)} %copy-done.12) | copy-start | bytes 6291460
  156.8 3.8 %copy-start.25 = (bf16[256,256]{1,0:T(8,128)(2,1)S(1)}, bf16[256,256]{1,0:T(8,128)(2,1)}, u32[]{:S(2)}) copy-start(bf16[256,256]{1,0:T(8,128)(2,1)} %constant.51.clone.fwd_ref.refs_15_) | copy-start | bytes 393220
  156.8 3.8 %copy-start.27 = (bf16[128,1024]{1,0:T(8,128)(2,1)S(1)}, bf16[128,1024]{1,0:T(8,128)(2,1)}, u32[]{:S(2)}) copy-start(bf16[128,1024]{1,0:T(8,128)(2,1)} %copy-done.26) | copy-start | bytes 786436
  156.8 3.8 %copy-start.32 = (bf16[256,256]{1,0:T(8,128)(2,1)S(1)}, bf16[256,256]{1,0:T(8,128)(2,1)}, u32[]{:S(2)}) copy-start(bf16[256,256]{1,0:T(8,128)(2,1)} %constant.53.clone.refs_16_.inv_ref) | copy-start | bytes 393220
  156.8 3.8 %copy-start.37 = (bf16[256,256]{1,0:T(8,128)(2,1)S(1)}, bf16[256,256]{1,0:T(8,128)(2,1)}, u32[]{:S(2)}) copy-start(bf16[256,256]{1,0:T(8,128)(2,1)} %constant.54.clone.refs_17_) | copy-start | bytes 393220
  157.1 17.5 %collective-permute-start.21 = (bf16[1024,256]{1,0:T(8,128)(2,1)S(1)}, bf16[1024,256]{1,0:T(8,128)(2,1)S(1)}, u32[]{:S(2)}, u32[]{:S(2)}) collective-permute-start(bf16[1024,256]{1,0:T(8,128)(2,1)S(1)} %add_blocks.9.refs_4_), channel_id=1, source_target_pairs={{0,4},{1,5},{2,6},{3,7},{4,0},{5,1},{6,2},{7,3},{8,12},{9,13},{10,... | collective-permute-start | bytes 1572872 | tf_op jit(solution)/shard_map/ppermute | solution.py:433
  158.7 15.9 %copy-start.6 = (bf16[1024,256]{1,0:T(8,128)(2,1)}, bf16[1024,256]{1,0:T(8,128)(2,1)S(1)}, u32[]{:S(2)}) copy-start(bf16[1024,256]{1,0:T(8,128)(2,1)S(1)} %collective-permute-done.8.refs_1_.refs_5_) | copy-start | bytes 1572868
  159.0 15.5 %collective-permute-start.20 = (bf16[1024,256]{1,0:T(8,128)(2,1)S(1)}, bf16[1024,256]{1,0:T(8,128)(2,1)S(1)}, u32[]{:S(2)}, u32[]{:S(2)}) collective-permute-start(bf16[1024,256]{1,0:T(8,128)(2,1)S(1)} %add_blocks.10.refs_6_), channel_id=1, source_target_pairs={{0,2},{1,3},{2,0},{3,1},{4,6},{5,7},{6,4},{7,5},{8,10},{9,11},{10,... | collective-permute-start | bytes 1572872 | tf_op jit(solution)/shard_map/ppermute | solution.py:433
  174.5 1.7 copy-start.33
  174.5 1.7 copy-start.35
  174.5 1.7 copy-start.36
  174.6 1.6 copy-start.22
  174.6 1.1 copy-start.20
  174.6 2.2 %copy-start.15 = (bf16[1024,256]{1,0:T(8,128)(2,1)S(1)}, bf16[1024,256]{1,0:T(8,128)(2,1)}, u32[]{:S(2)}) copy-start(bf16[1024,256]{1,0:T(8,128)(2,1)} %copy-done.14) | copy-start | bytes 1572868
  175.7 12.8 %collective-permute-start.23 = (bf16[1024,256]{1,0:T(8,128)(2,1)}, bf16[1024,256]{1,0:T(8,128)(2,1)S(1)}, u32[]{:S(2)}, u32[]{:S(2)}) collective-permute-start(bf16[1024,256]{1,0:T(8,128)(2,1)} %add_blocks.11.refs_1_), channel_id=1, source_target_pairs={{0,4},{1,5},{2,6},{3,7},{4,0},{5,1},{6,2},{7,3},{8,12},{9,13},{10,... | collective-permute-start | bytes 1572872 | tf_op jit(solution)/shard_map/ppermute | solution.py:433
  176.2 6.4 %collective-permute-start.19 = (bf16[128,1024]{1,0:T(8,128)(2,1)}, bf16[128,1024]{1,0:T(8,128)(2,1)}, u32[]{:S(2)}, u32[]{:S(2)}) collective-permute-start(bf16[128,1024]{1,0:T(8,128)(2,1)} %get-tuple-element.57.refs_5_), channel_id=1, source_target_pairs={{0,7},{1,0},{2,1},{3,2},{4,3},{5,4},{6,5},{7,6},{8,15},{9,8},{10,9... | collective-permute-start | bytes 786440 | tf_op jit(solution)/shard_map/ppermute | solution.py:531
  176.2 9.6 %collective-permute-start.22 = (f32[4,128,128]{2,1,0:T(8,128)}, f32[4,128,128]{2,1,0:T(8,128)}, u32[]{:S(2)}, u32[]{:S(2)}) collective-permute-start(f32[4,128,128]{2,1,0:T(8,128)} %hold.2), channel_id=1, source_target_pairs={{0,1},{1,0},{2,3},{3,2},{4,5},{5,4},{6,7},{7,6},{8,9},{9,8},{10,11... | collective-permute-start | bytes 786440 | tf_op jit(solution)/shard_map/ppermute | solution.py:433
  176.8 1.0 copy-start.17
  177.8 1.0 copy-start.19
  178.9 1.0 copy-start.23
  179.9 2.7 %copy-start.3 = (bf16[1024,1024]{1,0:T(8,128)(2,1)S(1)}, bf16[1024,1024]{1,0:T(8,128)(2,1)}, u32[]{:S(2)}) copy-start(bf16[1024,1024]{1,0:T(8,128)(2,1)} %k_ref.3) | copy-start | bytes 6291460
  179.9 3.0 %copy-start.4 = (bf16[1024,1024]{1,0:T(8,128)(2,1)S(1)}, bf16[1024,1024]{1,0:T(8,128)(2,1)}, u32[]{:S(2)}) copy-start(bf16[1024,1024]{1,0:T(8,128)(2,1)} %v_ref.3) | copy-start | bytes 6291460
  179.9 3.1 %copy-start.34 = (bf16[128,1024]{1,0:T(8,128)(2,1)S(1)}, bf16[128,1024]{1,0:T(8,128)(2,1)}, u32[]{:S(2)}) copy-start(bf16[128,1024]{1,0:T(8,128)(2,1)} %copy-done.33) | copy-start | bytes 786436
  189.3 6.0 %copy-start.7 = (bf16[1024,256]{1,0:T(8,128)(2,1)S(1)}, bf16[1024,256]{1,0:T(8,128)(2,1)}, u32[]{:S(2)}) copy-start(bf16[1024,256]{1,0:T(8,128)(2,1)} %copy-done.6) | copy-start | bytes 1572868
  189.3 6.0 %copy-start.21 = (bf16[1024,256]{1,0:T(8,128)(2,1)S(1)}, bf16[1024,256]{1,0:T(8,128)(2,1)}, u32[]{:S(2)}) copy-start(bf16[1024,256]{1,0:T(8,128)(2,1)} %copy-done.20) | copy-start | bytes 1572868
  190.4 9.4 %collective-permute-start.26 = (f32[128,128]{1,0:T(8,128)S(1)}, f32[128,128]{1,0:T(8,128)S(1)}, u32[]{:S(2)}, u32[]{:S(2)}) collective-permute-start(f32[128,128]{1,0:T(8,128)S(1)} %get-tuple-element.66), channel_id=1, source_target_pairs={{0,6},{1,7},{2,4},{3,5},{4,2},{5,3},{6,0},{7,1},{8,14},{9,15},{10,... | collective-permute-start | bytes 196616 | tf_op jit(solution)/shard_map/ppermute | solution.py:433
  194.6 5.2 %collective-permute-start.24 = (f32[128,128]{1,0:T(8,128)S(1)}, f32[128,128]{1,0:T(8,128)S(1)}, u32[]{:S(2)}, u32[]{:S(2)}) collective-permute-start(f32[128,128]{1,0:T(8,128)S(1)} %get-tuple-element.67), channel_id=1, source_target_pairs={{0,2},{1,3},{2,0},{3,1},{4,6},{5,7},{6,4},{7,5},{8,10},{9,11},{10,... | collective-permute-start | bytes 196616 | tf_op jit(solution)/shard_map/ppermute | solution.py:433
  194.6 5.2 %collective-permute-start.25 = (f32[128,128]{1,0:T(8,128)S(1)}, f32[128,128]{1,0:T(8,128)S(1)}, u32[]{:S(2)}, u32[]{:S(2)}) collective-permute-start(f32[128,128]{1,0:T(8,128)S(1)} %get-tuple-element.65), channel_id=1, source_target_pairs={{0,4},{1,5},{2,6},{3,7},{4,0},{5,1},{6,2},{7,3},{8,12},{9,13},{10,... | collective-permute-start | bytes 196616 | tf_op jit(solution)/shard_map/ppermute | solution.py:433
  195.3 1.0 copy-start.11
  196.3 0.9 copy-start.31
  (3 other events, 2.6 us)

commit v3 on v2

--- a/solution.py
+++ b/solution.py
@@ -606,11 +606,13 @@
         last_over_y = over(last_in, 4)
         got = over(hold(odd, [last_in]), 1)
         grad_key, grad_value = complete(first, last, grad_key, grad_value)
-        got = hold(got, [last_over_y, grad_weight, grad_key])
-        grad_filter = even[0] + got[0] + sum(over(even[n] + got[n], 2 * n) for n in (1, 2, 3))
+        got = hold(got, [grad_weight, grad_key])
+        others = [over(even[n] + got[n], 2 * n) for n in (1, 2, 3)]
         grad_weight = finish(
             is_early, own_terms, keeps[1:], [last_over, last_over_y], grad_weight, 1, scale
         )
+        others[0] = hold(others[0], [grad_weight])
+        grad_filter = even[0] + got[0] + sum(others)
     else:
         conv, gated_t = filtered(is_start, query, key, value, before, taps, consts)
         segment = lax.all_gather(out_grad, "tensor", axis=1, tiled=True)

time: 202 us -> 197 us (0.975)
  waiting for transfers between devices: 18.3 us -> 16.2 us
    ppermute x16, waiting for transfers between devices: 4.74 us -> 2.67 us  [swap(): lax.ppermute(value, 'context', [(c, c ^ bit) for c in range(contexts)])]
  transfers between devices with their start and end apart: 27 -> 27, of which waited for: 4 -> 4; matrix products, arithmetic and copies ran while one was open for 1% -> 1% of each run, Pallas kernels for 41% -> 42%
where the time goes in v3:
time: 197 us; the launch traced here: 196 us
  Pallas kernels  82.3 us (42%)
  starting transfers between devices  75.8 us (38%)
  local copies, waits for them, and re-layouts  16.5 us (8%)
  waiting for transfers between devices  16.2 us (8%)
  other arithmetic  4.23 us (2%)
    ppermute x9, starting transfers between devices, send_line(): return lax.ppermute(value, ('tensor', 'context'), on_line(pairs, contexts))  62.4 us
    pallas_call x6, Pallas kernels, project(): pl.pallas_call(functools.partial(project_kernel, operands=operands, produ...  43.5 us
    unnamed x80, local copies, waits for them, and re-layouts  16.3 us
    pallas_call x1, Pallas kernels, gradients(): pl.pallas_call(functools.partial(grad_kernel, operands=operands, earlier=...  13.9 us
    ppermute x16, starting transfers between devices, swap(): lax.ppermute(value, 'context', [(c, c ^ bit) for c in range(contexts)])  13.3 us
    pallas_call x1, Pallas kernels, filtered(): pl.pallas_call(conv_kernel, grid=(chans // tile,), in_specs=[SCALAR, col,...  8.76 us
    ppermute x9, waiting for transfers between devices, send_line(): return lax.ppermute(value, ('tensor', 'context'), on_line(pairs, contexts))  6.99 us
    ppermute x1, waiting for transfers between devices, body(): lax.ppermute(last_mixed, 'context', [(c, (c + 1) % contexts) for c in ran...  6.56 us
  transfers between devices with their start and end apart: 27, of which 4 were waited for; matrix products, arithmetic and copies ran while one was open for 1% of the time, Pallas kernels for 42%

profile of v3, /device:TPU:0, one launch (start us, length us, event | category | flops | bytes accessed | tf_op | source)
XLA Modules:
  0.0 196.2 jit_solution(362109068886360405)
XLA Ops:
  0.6 2.0 %collective-permute-start.1 = (bf16[1024,1024]{1,0:T(8,128)(2,1)}, bf16[1024,1024]{1,0:T(8,128)(2,1)}, u32[]{:S(2)}, u32[]{:S(2)}) collective-permute-start(bf16[1024,1024]{1,0:T(8,128)(2,1)} %refs_1_.1), channel_id=1, source_target_pairs={{8,16},{9,17},{10,18},{11,19},{12,20},{13,21},{14,22},{15,23},{16,... | collective-permute-start | bytes 6291464 | tf_op jit(solution)/shard_map/ppermute | solution.py:429
  2.6 4.6 %collective-permute-start = (bf16[1024,1024]{1,0:T(8,128)(2,1)}, bf16[1024,1024]{1,0:T(8,128)(2,1)}, u32[]{:S(2)}, u32[]{:S(2)}) collective-permute-start(bf16[1024,1024]{1,0:T(8,128)(2,1)} %refs_1_.1), channel_id=1, source_target_pairs={{0,8},{1,9},{2,10},{3,11},{4,12},{5,13},{6,14},{7,15},{8,0},{9,1},... | collective-permute-start | bytes 6291464 | tf_op jit(solution)/shard_map/ppermute | solution.py:429
  7.2 1.1 multiply_convert_fusion
  8.5 6.6 %collective-permute-done.2.halo_ref.refs_13_ = bf16[128,1024]{1,0:T(8,128)(2,1)S(1)} collective-permute-done((bf16[128,1024]{1,0:T(8,128)(2,1)S(1)}, bf16[128,1024]{1,0:T(8,128)(2,1)S(1)}, u32[]{:S(2)}, u32[]{:S(2)}) %collective-permute-start.2) | collective-permute-done | bytes 262176 | tf_op jit(solution)/shard_map/ppermute | solution.py:526
  15.1 0.9 copy-done.8
  16.0 0.9 copy-done.23
  16.9 0.9 copy-done.37
  17.8 8.8 %filtered.1 = (bf16[1024,1024]{1,0:T(8,128)(2,1)S(1)}, bf16[1024,1024]{1,0:T(8,128)(2,1)S(1)}) custom-call(s32[1]{0:T(128)} %bitcast.11.start_ref.refs_12_, bf16[1024,1024]{1,0:T(8,128)(2,1)} %refs_9_.3, bf16[1024,1024]{1,0:T(8,128)(2,1)} %k_ref.3, bf16[1024,1024]{1,0:T(8,128)(2,1)} %v_ref.3, bf16[128,1024]{1,0:T(8,128)(2,1)S(1)} %collective-permute-done.2.halo_ref.refs_13_, ...), custom_call_target="tpu_custom_call" | custom-call | flops 1048576 | bytes 370000000 | tf_op jit(solution)/shard_map/filtered/pallas_call | solution.py:101
  26.6 1.3 copy-done.2
  27.9 1.4 copy-done.10
  29.3 23.9 %collective-permute-start.5 = (bf16[1024,1024]{1,0:T(8,128)(2,1)}, bf16[1024,1024]{1,0:T(8,128)(2,1)S(1)}, u32[]{:S(2)}, u32[]{:S(2)}) collective-permute-start(bf16[1024,1024]{1,0:T(8,128)(2,1)} %collective-permute-done.1.refs_8_.refs_0_.refs_2_), channel_id=1, source_target_pairs={{0,8},{1,9},{2,10},{3,11},{4,12},{5,13},{6,14},{7,15},{8,0},{9,1},... | collective-permute-start | bytes 6291464 | tf_op jit(solution)/shard_map/ppermute | solution.py:429
  53.2 14.0 %project.6 = (f32[1024,1024]{1,0:T(8,128)}, bf16[1024,512]{1,0:T(8,128)(2,1)S(1)}, bf16[1024,512]{1,0:T(8,128)(2,1)S(1)}, bf16[1024,512]{1,0:T(8,128)(2,1)S(1)}, bf16[1024,512]{1,0:T(8,128)(2,1)}) custom-call(s32[8]{0:T(128)S(1)} %stack.61.place_ref, bf16[1024,1024]{1,0:T(8,128)(2,1)} %refs_1_.1, bf16[1024,1024]{1,0:T(8,128)(2,1)} %refs_1_.1, ...), custom_call_target="tpu_custom_call" | custom-call | flops 1048576 | bytes 370000000 | tf_op jit(solution)/shard_map/project/pallas_call | solution.py:230
  67.3 1.0 copy-done.25
  68.3 1.0 copy-done.38
  69.3 3.8 %cut.1 = (bf16[1024,512]{1,0:T(8,128)(2,1)}, bf16[1024,256]{1,0:T(8,128)(2,1)}, bf16[1024,256]{1,0:T(8,128)(2,1)}) custom-call(bf16[1024,1024]{1,0:T(8,128)(2,1)} %collective-permute-done.refs_2_.refs_3_.refs_0_, f32[1024,1024]{1,0:T(8,128)} %get-tuple-element.36.refs_1_.refs_7_), custom_call_target="tpu_custom_call" | custom-call | flops 1048576 | bytes 370000000 | tf_op jit(solution)/shard_map/cut/pallas_call | solution.py:447
  73.1 1.6 collective-permute-start.9
  74.7 0.5 collective-permute-start.11
  75.2 1.2 copy-done.26
  76.4 2.2 %add_blocks.6.refs_6_ = bf16[1024,512]{1,0:T(8,128)(2,1)} custom-call(bf16[1024,512]{1,0:T(8,128)(2,1)S(1)} %copy-done.26, bf16[1024,512]{1,0:T(8,128)(2,1)} %collective-permute-done.12.refs_1_), custom_call_target="tpu_custom_call" | custom-call | flops 1048576 | bytes 3700000 | tf_op jit(solution)/shard_map/add_blocks/pallas_call | solution.py:504
  78.6 1.5 collective-permute-start.13
  80.1 22.1 %collective-permute-start.10 = (bf16[1024,512]{1,0:T(8,128)(2,1)}, bf16[1024,512]{1,0:T(8,128)(2,1)}, u32[]{:S(2)}, u32[]{:S(2)}) collective-permute-start(bf16[1024,512]{1,0:T(8,128)(2,1)} %collective-permute-done.9.refs_4_.refs_6_), channel_id=1, source_target_pairs={{0,8},{1,9},{2,10},{3,11},{4,12},{5,13},{6,14},{7,15},{8,0},{9,1},... | collective-permute-start | bytes 3145736 | tf_op jit(solution)/shard_map/ppermute | solution.py:429
  102.2 1.5 collective-permute-start.6
  103.8 0.9 collective-permute-start.3
  104.6 7.9 %project.8.refs_3_.refs_12_ = f32[1024,1024]{1,0:T(8,128)} custom-call(s32[9]{0:T(128)S(1)} %stack.58.place_ref, bf16[1024,1024]{1,0:T(8,128)(2,1)} %collective-permute-done.1.refs_8_.refs_0_.refs_2_, bf16[1024,1024]{1,0:T(8,128)(2,1)S(1)} %collective-permute-done.5.refs_1_.refs_3_, bf16[1024,1024]{1,0:T(8,128)(2,1)} %collective-permute-done.1.refs_8_.refs_0_.refs_2_, ...), custom_call_target="tpu_custom_call" | custom-call | flops 1048576 | bytes 370000000 | tf_op jit(solution)/shard_map/project/pallas_call | solution.py:230
  112.5 1.7 add_blocks.7.refs_10_
  114.3 1.6 collective-permute-start.15
  115.9 3.7 %collective-permute-start.7 = (bf16[1024,256]{1,0:T(8,128)(2,1)}, bf16[1024,256]{1,0:T(8,128)(2,1)S(1)}, u32[]{:S(2)}, u32[]{:S(2)}) collective-permute-start(bf16[1024,256]{1,0:T(8,128)(2,1)} %collective-permute-done.6.refs_4_.refs_6_.refs_0_.refs_2_), channel_id=1, source_target_pairs={{0,8},{1,9},{2,10},{3,11},{4,12},{5,13},{6,14},{7,15},{8,0},{9,1},... | collective-permute-start | bytes 1572872 | tf_op jit(solution)/shard_map/ppermute | solution.py:429
  119.6 7.0 %collective-permute-done.10.refs_5_.refs_7_ = bf16[1024,512]{1,0:T(8,128)(2,1)} collective-permute-done((bf16[1024,512]{1,0:T(8,128)(2,1)}, bf16[1024,512]{1,0:T(8,128)(2,1)}, u32[]{:S(2)}, u32[]{:S(2)}) %collective-permute-start.10) | collective-permute-done | bytes 1048608 | tf_op jit(solution)/shard_map/ppermute | solution.py:429
  126.5 9.5 %project.9 = (f32[1024,1024]{1,0:T(8,128)}, bf16[1024,256]{1,0:T(8,128)(2,1)S(1)}, bf16[1024,256]{1,0:T(8,128)(2,1)S(1)}, bf16[1024,256]{1,0:T(8,128)(2,1)S(1)}, bf16[1024,256]{1,0:T(8,128)(2,1)S(1)}) custom-call(s32[9]{0:T(128)S(1)} %stack.58.place_ref, bf16[1024,1024]{1,0:T(8,128)(2,1)} %collective-permute-done.1.refs_8_.refs_0_.refs_2_, ...), custom_call_target="tpu_custom_call" | custom-call | flops 1048576 | bytes 370000000 | tf_op jit(solution)/shard_map/project/pallas_call | solution.py:230
  136.1 2.1 %collective-permute-start.4 = (bf16[1024,256]{1,0:T(8,128)(2,1)S(1)}, bf16[1024,256]{1,0:T(8,128)(2,1)S(1)}, u32[]{:S(2)}, u32[]{:S(2)}) collective-permute-start(bf16[1024,256]{1,0:T(8,128)(2,1)S(1)} %collective-permute-done.3.refs_4_.refs_6_.refs_0_.refs_2_), channel_id=1, source_target_pairs={{0,8},{1,9},{2,10},{3,11},{4,12},{5,13},{6,14},{7,15},{8,0},{9,1},... | collective-permute-start | bytes 1572872 | tf_op jit(solution)/shard_map/ppermute | solution.py:429
  138.2 3.8 %project.7 = (bf16[1024,128]{1,0:T(8,128)(2,1)S(1)}, bf16[1024,128]{1,0:T(8,128)(2,1)S(1)}, bf16[1024,256]{1,0:T(8,128)(2,1)S(1)}) custom-call(s32[9]{0:T(128)S(1)} %stack.58.place_ref, bf16[1024,1024]{1,0:T(8,128)(2,1)} %collective-permute-done.1.refs_8_.refs_0_.refs_2_, bf16[1024,1024]{1,0:T(8,128)(2,1)} %copy-done, ...), custom_call_target="tpu_custom_call" | custom-call | flops 1048576 | bytes 370000000 | tf_op jit(solution)/shard_map/project/pallas_call | solution.py:230
  142.0 0.2 collective-permute-start.8
  142.2 0.4 collective-permute-start.17
  142.7 1.5 collective-permute-start.18
  144.3 4.7 %project.10.refs_8_.refs_7_ = f32[1024,1024]{1,0:T(8,128)S(1)} custom-call(s32[9]{0:T(128)S(1)} %stack.58.place_ref, bf16[1024,256]{1,0:T(8,128)(2,1)} %collective-permute-done.6.refs_4_.refs_6_.refs_0_.refs_2_, bf16[1024,256]{1,0:T(8,128)(2,1)S(1)} %collective-permute-done.7.refs_5_.refs_7_.refs_1_.refs_3_, ...), custom_call_target="tpu_custom_call" | custom-call | flops 1048576 | bytes 370000 | tf_op jit(solution)/shard_map/project/pallas_call | solution.py:230
  149.0 2.0 %copy-done.1 = f32[1024,1024]{1,0:T(8,128)} copy-done((f32[1024,1024]{1,0:T(8,128)}, f32[1024,1024]{1,0:T(8,128)S(1)}, u32[]{:S(2)}) %copy-start.1) | copy-done | bytes 4194328
  151.0 3.6 %project.11 = (bf16[1024,128]{1,0:T(8,128)(2,1)S(1)}, bf16[1024,128]{1,0:T(8,128)(2,1)S(1)}, bf16[1024,256]{1,0:T(8,128)(2,1)S(1)}) custom-call(s32[9]{0:T(128)S(1)} %stack.58.place_ref, bf16[1024,1024]{1,0:T(8,128)(2,1)} %collective-permute-done.1.refs_8_.refs_0_.refs_2_, bf16[1024,1024]{1,0:T(8,128)(2,1)} %copy-done, ...), custom_call_target="tpu_custom_call" | custom-call | flops 1048576 | bytes 370000000 | tf_op jit(solution)/shard_map/project/pallas_call | solution.py:230
  154.8 2.0 %collective-permute-done.18.refs_2_.refs_6_ = bf16[1024,256]{1,0:T(8,128)(2,1)S(1)} collective-permute-done((bf16[1024,256]{1,0:T(8,128)(2,1)S(1)}, bf16[1024,256]{1,0:T(8,128)(2,1)S(1)}, u32[]{:S(2)}, u32[]{:S(2)}) %collective-permute-start.18) | collective-permute-done | bytes 524320 | tf_op jit(solution)/shard_map/ppermute | solution.py:433
  156.8 0.2 add_blocks.9.refs_4_
  157.1 1.6 collective-permute-start.21
  158.7 0.3 add_blocks.10.refs_6_
  159.0 1.6 collective-permute-start.20
  160.6 13.9 %gradients.1 = (f32[1024,1024]{1,0:T(8,128)}, f32[1024,1024]{1,0:T(8,128)}, f32[1024,1024]{1,0:T(8,128)}, bf16[128,1024]{1,0:T(8,128)(2,1)}, bf16[128,1024]{1,0:...) custom-call(s32[9]{0:T(128)S(1)} %stack.58.place_ref, ...), custom_call_target="tpu_custom_call" | custom-call | flops 1048576 | bytes 370000000 | tf_op jit(solution)/shard_map/gradients/pallas_call | solution.py:322
  174.7 0.4 add_blocks.11.refs_1_
  175.1 0.2 copy-done.31
  175.4 0.2 copy-done.20
  175.6 0.2 copy-done.18
  175.8 0.8 copy-done.22
  176.6 0.3 collective-permute-start.22
  176.9 0.5 collective-permute-start.24
  177.4 1.0 copy-done.17
  178.5 1.0 copy-done.21
  179.5 2.7 %finish.2.refs_1_.refs_10_ = f32[1024,512]{1,0:T(8,128)} custom-call(s32[1]{0:T(128)} %bitcast.13.early_ref, bf16[1024,512]{1,0:T(8,128)(2,1)S(1)} %get-tuple-element.42.refs_0_, bf16[1024,512]{1,0:T(8,128)(2,1)} %collective-permute-done.11.refs_1_, bf16[1024,512]{1,0:T(8,128)(2,1)} %collective-permute-done.13.refs_2_, bf16[1024,512]{1,0:T(8,128)(2,1)} %copy-done.5, ...), custom_call_target="tpu_custom_call" | custom-call | flops 1048576 | bytes 7400000 | tf_op jit(solution)/shard_map/finish/pallas_call | solution.py:406
  182.2 0.2 copy-done.4
  182.6 2.1 %last_rows.1 = (f32[1024,1024]{1,0:T(8,128)}, f32[1024,1024]{1,0:T(8,128)}) custom-call(s32[1]{0:T(128)} %bitcast.12.end_ref, bf16[128,1024]{1,0:T(8,128)(2,1)S(1)} %copy-done.32, bf16[128,1024]{1,0:T(8,128)(2,1)S(1)} %collective-permute-done.19.after_ref, bf16[1024,1024]{1,0:T(8,128)(2,1)S(1)} %copy-done.3, ...), custom_call_target="tpu_custom_call", output_to_operand_aliasing={{0}: (8, {}), {1}: (9, {})} | custom-call | flops 1048576 | bytes 7400000 | tf_op jit(solution)/shard_map/last_rows/pallas_call | solution.py:377
  184.7 0.9 copy-done.34
  185.6 1.6 fusion.1
  187.2 0.7 collective-permute-start.23
  187.9 2.2 %collective-permute-start.26 = (f32[128,128]{1,0:T(8,128)}, f32[128,128]{1,0:T(8,128)}, u32[]{:S(2)}, u32[]{:S(2)}) collective-permute-start(f32[128,128]{1,0:T(8,128)} %get-tuple-element.66), channel_id=1, source_target_pairs={{0,6},{1,7},{2,4},{3,5},{4,2},{5,3},{6,0},{7,1},{8,14},{9,15},{10,... | collective-permute-start | bytes 196616 | tf_op jit(solution)/shard_map/ppermute | solution.py:433
  190.2 0.5 collective-permute-start.25
  190.7 0.6 collective-permute-done.24.refs_9_
  191.3 2.7 %finish.3.refs_1_ = f32[1024,512]{1,0:T(8,128)} custom-call(s32[1]{0:T(128)} %bitcast.13.early_ref, bf16[1024,512]{1,0:T(8,128)(2,1)S(1)} %get-tuple-element.42.refs_0_, bf16[1024,512]{1,0:T(8,128)(2,1)} %collective-permute-done.11.refs_1_, bf16[1024,512]{1,0:T(8,128)(2,1)} %collective-permute-done.13.refs_2_, ...), custom_call_target="tpu_custom_call", output_to_operand_aliasing={{}: (11, {})} | custom-call | flops 1048576 | bytes 7400000 | tf_op jit(solution)/shard_map/finish/pallas_call | solution.py:406
  194.0 0.6 copy-done.39
  194.6 1.6 fusion.4
  (96 shorter events, 1.1 us)
Async XLA Ops:
  0.6 28.7 %collective-permute-start.1 = (bf16[1024,1024]{1,0:T(8,128)(2,1)}, bf16[1024,1024]{1,0:T(8,128)(2,1)}, u32[]{:S(2)}, u32[]{:S(2)}) collective-permute-start(bf16[1024,1024]{1,0:T(8,128)(2,1)} %refs_1_.1), channel_id=1, source_target_pairs={{8,16},{9,17},{10,18},{11,19},{12,20},{13,21},{14,22},{15,23},{16,... | collective-permute-start | bytes 6291464 | tf_op jit(solution)/shard_map/ppermute | solution.py:429
  2.6 50.6 %collective-permute-start = (bf16[1024,1024]{1,0:T(8,128)(2,1)}, bf16[1024,1024]{1,0:T(8,128)(2,1)}, u32[]{:S(2)}, u32[]{:S(2)}) collective-permute-start(bf16[1024,1024]{1,0:T(8,128)(2,1)} %refs_1_.1), channel_id=1, source_target_pairs={{0,8},{1,9},{2,10},{3,11},{4,12},{5,13},{6,14},{7,15},{8,0},{9,1},... | collective-permute-start | bytes 6291464 | tf_op jit(solution)/shard_map/ppermute | solution.py:429
  8.3 6.7 %collective-permute-start.2 = (bf16[128,1024]{1,0:T(8,128)(2,1)S(1)}, bf16[128,1024]{1,0:T(8,128)(2,1)S(1)}, u32[]{:S(2)}, u32[]{:S(2)}) collective-permute-start(bf16[128,1024]{1,0:T(8,128)(2,1)S(1)} %multiply_convert_fusion), channel_id=1, source_target_pairs={{0,1},{1,2},{2,3},{3,4},{4,5},{5,6},{6,7},{7,0},{8,9},{9,10},{10,1... | collective-permute-start | bytes 786440 | tf_op jit(solution)/shard_map/ppermute | solution.py:526
  15.1 1.0 copy-start.8
  16.0 0.9 copy-start.23
  16.9 0.9 copy-start.37
  26.6 1.3 copy-start.2
  27.9 1.4 copy-start.10
  29.3 74.4 %collective-permute-start.5 = (bf16[1024,1024]{1,0:T(8,128)(2,1)}, bf16[1024,1024]{1,0:T(8,128)(2,1)S(1)}, u32[]{:S(2)}, u32[]{:S(2)}) collective-permute-start(bf16[1024,1024]{1,0:T(8,128)(2,1)} %collective-permute-done.1.refs_8_.refs_0_.refs_2_), channel_id=1, source_target_pairs={{0,8},{1,9},{2,10},{3,11},{4,12},{5,13},{6,14},{7,15},{8,0},{9,1},... | collective-permute-start | bytes 6291464 | tf_op jit(solution)/shard_map/ppermute | solution.py:429
  67.3 1.0 copy-start.25
  68.3 1.0 copy-start.38
  69.3 5.9 %collective-permute-start.12 = (bf16[1024,512]{1,0:T(8,128)(2,1)}, bf16[1024,512]{1,0:T(8,128)(2,1)}, u32[]{:S(2)}, u32[]{:S(2)}) collective-permute-start(bf16[1024,512]{1,0:T(8,128)(2,1)} %get-tuple-element.45), channel_id=1, source_target_pairs={{0,1},{1,0},{2,3},{3,2},{4,5},{5,4},{6,7},{7,6},{8,9},{9,8},{10,11... | collective-permute-start | bytes 3145736 | tf_op jit(solution)/shard_map/ppermute | solution.py:433
  73.1 7.0 %collective-permute-start.9 = (bf16[1024,512]{1,0:T(8,128)(2,1)}, bf16[1024,512]{1,0:T(8,128)(2,1)}, u32[]{:S(2)}, u32[]{:S(2)}) collective-permute-start(bf16[1024,512]{1,0:T(8,128)(2,1)} %get-tuple-element.41), channel_id=1, source_target_pairs={{8,16},{9,17},{10,18},{11,19},{12,20},{13,21},{14,22},{15,23},{16,... | collective-permute-start | bytes 3145736 | tf_op jit(solution)/shard_map/ppermute | solution.py:429
  74.7 37.8 %collective-permute-start.11 = (bf16[1024,512]{1,0:T(8,128)(2,1)}, bf16[1024,512]{1,0:T(8,128)(2,1)}, u32[]{:S(2)}, u32[]{:S(2)}) collective-permute-start(bf16[1024,512]{1,0:T(8,128)(2,1)} %copy-done.38), channel_id=1, source_target_pairs={{0,1},{1,0},{2,3},{3,2},{4,5},{5,4},{6,7},{7,6},{8,9},{9,8},{10,11... | collective-permute-start | bytes 3145736 | tf_op jit(solution)/shard_map/ppermute | solution.py:433
  75.2 1.2 copy-start.26
  78.6 33.9 %collective-permute-start.13 = (bf16[1024,512]{1,0:T(8,128)(2,1)}, bf16[1024,512]{1,0:T(8,128)(2,1)}, u32[]{:S(2)}, u32[]{:S(2)}) collective-permute-start(bf16[1024,512]{1,0:T(8,128)(2,1)} %add_blocks.6.refs_6_), channel_id=1, source_target_pairs={{0,2},{1,3},{2,0},{3,1},{4,6},{5,7},{6,4},{7,5},{8,10},{9,11},{10,... | collective-permute-start | bytes 3145736 | tf_op jit(solution)/shard_map/ppermute | solution.py:433
  80.1 46.5 %collective-permute-start.10 = (bf16[1024,512]{1,0:T(8,128)(2,1)}, bf16[1024,512]{1,0:T(8,128)(2,1)}, u32[]{:S(2)}, u32[]{:S(2)}) collective-permute-start(bf16[1024,512]{1,0:T(8,128)(2,1)} %collective-permute-done.9.refs_4_.refs_6_), channel_id=1, source_target_pairs={{0,8},{1,9},{2,10},{3,11},{4,12},{5,13},{6,14},{7,15},{8,0},{9,1},... | collective-permute-start | bytes 3145736 | tf_op jit(solution)/shard_map/ppermute | solution.py:429
  102.2 13.6 %collective-permute-start.6 = (bf16[1024,256]{1,0:T(8,128)(2,1)}, bf16[1024,256]{1,0:T(8,128)(2,1)}, u32[]{:S(2)}, u32[]{:S(2)}) collective-permute-start(bf16[1024,256]{1,0:T(8,128)(2,1)} %get-tuple-element.38), channel_id=1, source_target_pairs={{8,16},{9,17},{10,18},{11,19},{12,20},{13,21},{14,22},{15,23},{16,... | collective-permute-start | bytes 1572872 | tf_op jit(solution)/shard_map/ppermute | solution.py:429
  103.8 8.8 %copy-start = (bf16[1024,1024]{1,0:T(8,128)(2,1)}, bf16[1024,1024]{1,0:T(8,128)(2,1)S(1)}, u32[]{:S(2)}) copy-start(bf16[1024,1024]{1,0:T(8,128)(2,1)S(1)} %collective-permute-done.5.refs_1_.refs_3_) | copy-start | bytes 6291460
  103.8 32.3 %collective-permute-start.3 = (bf16[1024,256]{1,0:T(8,128)(2,1)}, bf16[1024,256]{1,0:T(8,128)(2,1)S(1)}, u32[]{:S(2)}, u32[]{:S(2)}) collective-permute-start(bf16[1024,256]{1,0:T(8,128)(2,1)} %get-tuple-element.37), channel_id=1, source_target_pairs={{8,16},{9,17},{10,18},{11,19},{12,20},{13,21},{14,22},{15,23},{16,... | collective-permute-start | bytes 1572872 | tf_op jit(solution)/shard_map/ppermute | solution.py:429
  114.3 36.8 %collective-permute-start.15 = (bf16[1024,512]{1,0:T(8,128)(2,1)S(1)}, bf16[1024,512]{1,0:T(8,128)(2,1)S(1)}, u32[]{:S(2)}, u32[]{:S(2)}) collective-permute-start(bf16[1024,512]{1,0:T(8,128)(2,1)S(1)} %add_blocks.7.refs_10_), channel_id=1, source_target_pairs={{0,4},{1,5},{2,6},{3,7},{4,0},{5,1},{6,2},{7,3},{8,12},{9,13},{10,... | collective-permute-start | bytes 3145736 | tf_op jit(solution)/shard_map/ppermute | solution.py:433
  115.9 22.3 %collective-permute-start.7 = (bf16[1024,256]{1,0:T(8,128)(2,1)}, bf16[1024,256]{1,0:T(8,128)(2,1)S(1)}, u32[]{:S(2)}, u32[]{:S(2)}) collective-permute-start(bf16[1024,256]{1,0:T(8,128)(2,1)} %collective-permute-done.6.refs_4_.refs_6_.refs_0_.refs_2_), channel_id=1, source_target_pairs={{0,8},{1,9},{2,10},{3,11},{4,12},{5,13},{6,14},{7,15},{8,0},{9,1},... | collective-permute-start | bytes 1572872 | tf_op jit(solution)/shard_map/ppermute | solution.py:429
  136.0 20.8 %copy-start.12 = (bf16[1024,256]{1,0:T(8,128)(2,1)}, bf16[1024,256]{1,0:T(8,128)(2,1)S(1)}, u32[]{:S(2)}) copy-start(bf16[1024,256]{1,0:T(8,128)(2,1)S(1)} %get-tuple-element.52.refs_0_.refs_4_) | copy-start | bytes 1572868
  136.0 6.6 %collective-permute-start.14 = (bf16[1024,256]{1,0:T(8,128)(2,1)S(1)}, bf16[1024,256]{1,0:T(8,128)(2,1)S(1)}, u32[]{:S(2)}, u32[]{:S(2)}) collective-permute-start(bf16[1024,256]{1,0:T(8,128)(2,1)S(1)} %get-tuple-element.47), channel_id=1, source_target_pairs={{0,1},{1,0},{2,3},{3,2},{4,5},{5,4},{6,7},{7,6},{8,9},{9,8},{10,11... | collective-permute-start | bytes 1572872 | tf_op jit(solution)/shard_map/ppermute | solution.py:433
  136.1 14.9 %collective-permute-start.4 = (bf16[1024,256]{1,0:T(8,128)(2,1)S(1)}, bf16[1024,256]{1,0:T(8,128)(2,1)S(1)}, u32[]{:S(2)}, u32[]{:S(2)}) collective-permute-start(bf16[1024,256]{1,0:T(8,128)(2,1)S(1)} %collective-permute-done.3.refs_4_.refs_6_.refs_0_.refs_2_), channel_id=1, source_target_pairs={{0,8},{1,9},{2,10},{3,11},{4,12},{5,13},{6,14},{7,15},{8,0},{9,1},... | collective-permute-start | bytes 1572872 | tf_op jit(solution)/shard_map/ppermute | solution.py:429
  142.0 16.7 %collective-permute-start.8 = (bf16[1024,256]{1,0:T(8,128)(2,1)S(1)}, bf16[1024,256]{1,0:T(8,128)(2,1)S(1)}, u32[]{:S(2)}, u32[]{:S(2)}) collective-permute-start(bf16[1024,256]{1,0:T(8,128)(2,1)S(1)} %get-tuple-element.40), channel_id=1, source_target_pairs={{0,1},{1,0},{2,3},{3,2},{4,5},{5,4},{6,7},{7,6},{8,9},{9,8},{10,11... | collective-permute-start | bytes 1572872 | tf_op jit(solution)/shard_map/ppermute | solution.py:433
  142.2 12.5 %collective-permute-start.17 = (bf16[1024,256]{1,0:T(8,128)(2,1)S(1)}, bf16[1024,256]{1,0:T(8,128)(2,1)S(1)}, u32[]{:S(2)}, u32[]{:S(2)}) collective-permute-start(bf16[1024,256]{1,0:T(8,128)(2,1)S(1)} %get-tuple-element.53), channel_id=1, source_target_pairs={{0,1},{1,0},{2,3},{3,2},{4,5},{5,4},{6,7},{7,6},{8,9},{9,8},{10,11... | collective-permute-start | bytes 1572872 | tf_op jit(solution)/shard_map/ppermute | solution.py:433
  142.7 14.0 %collective-permute-start.18 = (bf16[1024,256]{1,0:T(8,128)(2,1)S(1)}, bf16[1024,256]{1,0:T(8,128)(2,1)S(1)}, u32[]{:S(2)}, u32[]{:S(2)}) collective-permute-start(bf16[1024,256]{1,0:T(8,128)(2,1)S(1)} %add_blocks.8.refs_6_), channel_id=1, source_target_pairs={{0,2},{1,3},{2,0},{3,1},{4,6},{5,7},{6,4},{7,5},{8,10},{9,11},{10,... | collective-permute-start | bytes 1572872 | tf_op jit(solution)/shard_map/ppermute | solution.py:433
  149.0 2.0 %copy-start.1 = (f32[1024,1024]{1,0:T(8,128)}, f32[1024,1024]{1,0:T(8,128)S(1)}, u32[]{:S(2)}) copy-start(f32[1024,1024]{1,0:T(8,128)S(1)} %project.10.refs_8_.refs_7_) | copy-start | bytes 12582916
  151.0 3.6 %copy-start.5 = (bf16[1024,512]{1,0:T(8,128)(2,1)}, bf16[1024,512]{1,0:T(8,128)(2,1)S(1)}, u32[]{:S(2)}) copy-start(bf16[1024,512]{1,0:T(8,128)(2,1)S(1)} %collective-permute-done.15.refs_9_.refs_3_) | copy-start | bytes 3145732
  154.7 20.0 %copy-start.27 = (bf16[1024,128]{1,0:T(8,128)(2,1)}, bf16[1024,128]{1,0:T(8,128)(2,1)S(1)}, u32[]{:S(2)}) copy-start(bf16[1024,128]{1,0:T(8,128)(2,1)S(1)} %get-tuple-element.64.refs_2_.refs_6_) | copy-start | bytes 786436
  154.7 4.0 %collective-permute-start.16 = (bf16[1024,256]{1,0:T(8,128)(2,1)S(1)}, bf16[1024,256]{1,0:T(8,128)(2,1)S(1)}, u32[]{:S(2)}, u32[]{:S(2)}) collective-permute-start(bf16[1024,256]{1,0:T(8,128)(2,1)S(1)} %get-tuple-element.51), channel_id=1, source_target_pairs={{0,1},{1,0},{2,3},{3,2},{4,5},{5,4},{6,7},{7,6},{8,9},{9,8},{10,11... | collective-permute-start | bytes 1572872 | tf_op jit(solution)/shard_map/ppermute | solution.py:433
  154.8 4.2 %copy-start.14 = (bf16[1024,256]{1,0:T(8,128)(2,1)}, bf16[1024,256]{1,0:T(8,128)(2,1)S(1)}, u32[]{:S(2)}) copy-start(bf16[1024,256]{1,0:T(8,128)(2,1)S(1)} %collective-permute-done.17.refs_1_.refs_5_) | copy-start | bytes 1572868
  156.8 2.2 %copy-start.16 = (bf16[1024,256]{1,0:T(8,128)(2,1)}, bf16[1024,256]{1,0:T(8,128)(2,1)S(1)}, u32[]{:S(2)}) copy-start(bf16[1024,256]{1,0:T(8,128)(2,1)S(1)} %collective-permute-done.18.refs_2_.refs_6_) | copy-start | bytes 1572868
  156.8 3.8 %copy-start.9 = (bf16[128,1024]{1,0:T(8,128)(2,1)S(1)}, bf16[128,1024]{1,0:T(8,128)(2,1)}, u32[]{:S(2)}) copy-start(bf16[128,1024]{1,0:T(8,128)(2,1)} %taps_ref.3) | copy-start | bytes 786436
  156.8 3.8 %copy-start.11 = (bf16[1024,1024]{1,0:T(8,128)(2,1)S(1)}, bf16[1024,1024]{1,0:T(8,128)(2,1)}, u32[]{:S(2)}) copy-start(bf16[1024,1024]{1,0:T(8,128)(2,1)} %copy-done.10) | copy-start | bytes 6291460
  156.8 3.8 %copy-start.24 = (bf16[256,256]{1,0:T(8,128)(2,1)S(1)}, bf16[256,256]{1,0:T(8,128)(2,1)}, u32[]{:S(2)}) copy-start(bf16[256,256]{1,0:T(8,128)(2,1)} %constant.51.clone.fwd_ref.refs_15_) | copy-start | bytes 393220
  156.8 3.8 %copy-start.29 = (bf16[256,256]{1,0:T(8,128)(2,1)S(1)}, bf16[256,256]{1,0:T(8,128)(2,1)}, u32[]{:S(2)}) copy-start(bf16[256,256]{1,0:T(8,128)(2,1)} %constant.53.clone.refs_16_.inv_ref) | copy-start | bytes 393220
  156.8 3.8 %copy-start.36 = (bf16[256,256]{1,0:T(8,128)(2,1)S(1)}, bf16[256,256]{1,0:T(8,128)(2,1)}, u32[]{:S(2)}) copy-start(bf16[256,256]{1,0:T(8,128)(2,1)} %constant.54.clone.refs_17_) | copy-start | bytes 393220
  157.1 17.5 %collective-permute-start.21 = (bf16[1024,256]{1,0:T(8,128)(2,1)S(1)}, bf16[1024,256]{1,0:T(8,128)(2,1)S(1)}, u32[]{:S(2)}, u32[]{:S(2)}) collective-permute-start(bf16[1024,256]{1,0:T(8,128)(2,1)S(1)} %add_blocks.9.refs_4_), channel_id=1, source_target_pairs={{0,4},{1,5},{2,6},{3,7},{4,0},{5,1},{6,2},{7,3},{8,12},{9,13},{10,... | collective-permute-start | bytes 1572872 | tf_op jit(solution)/shard_map/ppermute | solution.py:433
  158.7 16.0 %copy-start.6 = (bf16[1024,256]{1,0:T(8,128)(2,1)}, bf16[1024,256]{1,0:T(8,128)(2,1)S(1)}, u32[]{:S(2)}) copy-start(bf16[1024,256]{1,0:T(8,128)(2,1)S(1)} %collective-permute-done.8.refs_1_.refs_5_) | copy-start | bytes 1572868
  159.0 15.6 %collective-permute-start.20 = (bf16[1024,256]{1,0:T(8,128)(2,1)S(1)}, bf16[1024,256]{1,0:T(8,128)(2,1)S(1)}, u32[]{:S(2)}, u32[]{:S(2)}) collective-permute-start(bf16[1024,256]{1,0:T(8,128)(2,1)S(1)} %add_blocks.10.refs_6_), channel_id=1, source_target_pairs={{0,2},{1,3},{2,0},{3,1},{4,6},{5,7},{6,4},{7,5},{8,10},{9,11},{10,... | collective-permute-start | bytes 1572872 | tf_op jit(solution)/shard_map/ppermute | solution.py:433
  174.5 0.8 copy-start.33
  174.5 0.9 copy-start.35
  174.5 7.7 %collective-permute-start.19 = (bf16[128,1024]{1,0:T(8,128)(2,1)}, bf16[128,1024]{1,0:T(8,128)(2,1)S(1)}, u32[]{:S(2)}, u32[]{:S(2)}) collective-permute-start(bf16[128,1024]{1,0:T(8,128)(2,1)} %get-tuple-element.57.refs_5_), channel_id=1, source_target_pairs={{0,7},{1,0},{2,1},{3,2},{4,3},{5,4},{6,5},{7,6},{8,15},{9,8},{10,9... | collective-permute-start | bytes 786440 | tf_op jit(solution)/shard_map/ppermute | solution.py:531
  174.6 1.0 copy-start.20
  174.6 1.2 copy-start.18
  174.7 2.8 %copy-start.13 = (bf16[1024,256]{1,0:T(8,128)(2,1)S(1)}, bf16[1024,256]{1,0:T(8,128)(2,1)}, u32[]{:S(2)}) copy-start(bf16[1024,256]{1,0:T(8,128)(2,1)} %copy-done.12) | copy-start | bytes 1572868
  174.7 2.8 %copy-start.15 = (bf16[1024,256]{1,0:T(8,128)(2,1)S(1)}, bf16[1024,256]{1,0:T(8,128)(2,1)}, u32[]{:S(2)}) copy-start(bf16[1024,256]{1,0:T(8,128)(2,1)} %copy-done.14) | copy-start | bytes 1572868
  176.6 8.0 %collective-permute-start.22 = (f32[4,128,128]{2,1,0:T(8,128)}, f32[4,128,128]{2,1,0:T(8,128)}, u32[]{:S(2)}, u32[]{:S(2)}) collective-permute-start(f32[4,128,128]{2,1,0:T(8,128)} %hold.3), channel_id=1, source_target_pairs={{0,1},{1,0},{2,3},{3,2},{4,5},{5,4},{6,7},{7,6},{8,9},{9,8},{10,11... | collective-permute-start | bytes 786440 | tf_op jit(solution)/shard_map/ppermute | solution.py:433
  176.9 14.4 %collective-permute-start.24 = (bf16[1024,256]{1,0:T(8,128)(2,1)}, bf16[1024,256]{1,0:T(8,128)(2,1)}, u32[]{:S(2)}, u32[]{:S(2)}) collective-permute-start(bf16[1024,256]{1,0:T(8,128)(2,1)} %copy-done.22), channel_id=1, source_target_pairs={{0,4},{1,5},{2,6},{3,7},{4,0},{5,1},{6,2},{7,3},{8,12},{9,13},{10,... | collective-permute-start | bytes 1572872 | tf_op jit(solution)/shard_map/ppermute | solution.py:433
  177.4 1.0 copy-start.17
  178.5 1.0 copy-start.21
  179.5 2.7 %copy-start.3 = (bf16[1024,1024]{1,0:T(8,128)(2,1)S(1)}, bf16[1024,1024]{1,0:T(8,128)(2,1)}, u32[]{:S(2)}) copy-start(bf16[1024,1024]{1,0:T(8,128)(2,1)} %k_ref.3) | copy-start | bytes 6291460
  179.5 2.9 %copy-start.4 = (bf16[1024,1024]{1,0:T(8,128)(2,1)S(1)}, bf16[1024,1024]{1,0:T(8,128)(2,1)}, u32[]{:S(2)}) copy-start(bf16[1024,1024]{1,0:T(8,128)(2,1)} %v_ref.3) | copy-start | bytes 6291460
  179.5 3.0 %copy-start.30 = (bf16[256,256]{1,0:T(8,128)(2,1)S(1)}, bf16[256,256]{1,0:T(8,128)(2,1)}, u32[]{:S(2)}) copy-start(bf16[256,256]{1,0:T(8,128)(2,1)} %constant.53.clone.refs_16_.inv_ref) | copy-start | bytes 393220
  179.5 3.1 %copy-start.32 = (bf16[128,1024]{1,0:T(8,128)(2,1)S(1)}, bf16[128,1024]{1,0:T(8,128)(2,1)}, u32[]{:S(2)}) copy-start(bf16[128,1024]{1,0:T(8,128)(2,1)} %copy-done.31) | copy-start | bytes 786436
  184.7 1.0 copy-start.34
  184.7 6.6 %copy-start.7 = (bf16[1024,256]{1,0:T(8,128)(2,1)S(1)}, bf16[1024,256]{1,0:T(8,128)(2,1)}, u32[]{:S(2)}) copy-start(bf16[1024,256]{1,0:T(8,128)(2,1)} %copy-done.6) | copy-start | bytes 1572868
  184.7 6.6 %copy-start.19 = (bf16[1024,256]{1,0:T(8,128)(2,1)S(1)}, bf16[1024,256]{1,0:T(8,128)(2,1)}, u32[]{:S(2)}) copy-start(bf16[1024,256]{1,0:T(8,128)(2,1)} %copy-done.18) | copy-start | bytes 1572868
  184.7 6.6 %copy-start.28 = (bf16[1024,128]{1,0:T(8,128)(2,1)S(1)}, bf16[1024,128]{1,0:T(8,128)(2,1)}, u32[]{:S(2)}) copy-start(bf16[1024,128]{1,0:T(8,128)(2,1)} %copy-done.27) | copy-start | bytes 786436
  187.2 6.8 %collective-permute-start.23 = (f32[128,128]{1,0:T(8,128)S(1)}, f32[128,128]{1,0:T(8,128)S(1)}, u32[]{:S(2)}, u32[]{:S(2)}) collective-permute-start(f32[128,128]{1,0:T(8,128)S(1)} %get-tuple-element.67), channel_id=1, source_target_pairs={{0,2},{1,3},{2,0},{3,1},{4,6},{5,7},{6,4},{7,5},{8,10},{9,11},{10,... | collective-permute-start | bytes 196616 | tf_op jit(solution)/shard_map/ppermute | solution.py:433
  187.9 6.7 %collective-permute-start.26 = (f32[128,128]{1,0:T(8,128)}, f32[128,128]{1,0:T(8,128)}, u32[]{:S(2)}, u32[]{:S(2)}) collective-permute-start(f32[128,128]{1,0:T(8,128)} %get-tuple-element.66), channel_id=1, source_target_pairs={{0,6},{1,7},{2,4},{3,5},{4,2},{5,3},{6,0},{7,1},{8,14},{9,15},{10,... | collective-permute-start | bytes 196616 | tf_op jit(solution)/shard_map/ppermute | solution.py:433
  190.2 4.4 %collective-permute-start.25 = (f32[128,128]{1,0:T(8,128)S(1)}, f32[128,128]{1,0:T(8,128)}, u32[]{:S(2)}, u32[]{:S(2)}) collective-permute-start(f32[128,128]{1,0:T(8,128)S(1)} %get-tuple-element.65), channel_id=1, source_target_pairs={{0,4},{1,5},{2,6},{3,7},{4,0},{5,1},{6,2},{7,3},{8,12},{9,13},{10,... | collective-permute-start | bytes 196616 | tf_op jit(solution)/shard_map/ppermute | solution.py:433
  (3 other events, 2.1 us)
